TPU v7x, 128 devices: a whole 4x4x4 slice. The times are simulated.
128 devices in a mesh: rows: 16 (over x, z), slab: 8 (over y, core).
Axes of the slice: x: 4, y: 4, z: 4, core: 2. Of those that a mesh axis runs over, the one named last changes fastest.
Arguments:
- coefficients: bfloat16 [49152, 1024], P('rows', 'slab'), may hold values from -1.1953125 to 1.1953125
- occupations: bfloat16 [1, 1024], P(None, 'slab'), may hold values from 0.049804688 to 2
- energies: bfloat16 [1, 1024], P(None, 'slab'), may hold values from -2 to 1
- send_lists: int32 [16, 16, 2], P('rows'), may hold values from 0 to 23, as said below
- pair_rows: int32 [6144], P(('rows', 'slab')), may hold values from 0 to 2
- pair_sources: int32 [6144], P(('rows', 'slab')), may hold values from 0 to 55
Outputs:
- density: float32 [6144, 128, 128], P(('rows', 'slab'))
- energy_density: float32 [6144, 128, 128], P(('rows', 'slab'))
Inputs may be any that keep to these rules, and one draw needn't show every extreme that they name: Each send_lists[p, r] names 2 different local row blocks of the sender p.
All inputs are finite; a program needn't handle non-finite values.
Results may differ from a plain program's by a relative error of at most 0.0028.
Values may be sent and summed in bfloat16 or wider, within the bound.
No kernel may reach another device: no remote copies, remote signals or barrier semaphores. Data moves between devices by JAX's collectives and lax.ppermute only.
A program may use at most 128 MiB of HBM per device.

v0:
```python
import jax
import jax.numpy as jnp
from jax import lax
from jax.sharding import PartitionSpec as P

BS = 128


def body(coefficients, occupations, energies, send_lists, pair_rows, pair_sources):
    blocks = coefficients.shape[0] // BS
    full, occ_full, level_full = (
        lax.all_gather(coefficients, "slab", axis=1, tiled=True),
        lax.all_gather(occupations, "slab", axis=1, tiled=True),
        lax.all_gather(energies, "slab", axis=1, tiled=True),
    )
    width = full.shape[1]
    tiles = full.reshape(blocks, BS, width)
    outgoing = tiles[send_lists[0]]
    received = lax.all_to_all(outgoing, "rows", split_axis=0, concat_axis=0, tiled=True)
    group_size = blocks // lax.axis_size("slab")
    first = lax.axis_index("slab") * group_size
    mine = lax.dynamic_slice_in_dim(tiles, first, group_size, 0).astype(jnp.float32)
    occ = occ_full.astype(jnp.float32).reshape(1, 1, width)
    level = level_full.astype(jnp.float32).reshape(1, 1, width)
    weighted = (mine * occ).astype(jnp.bfloat16)
    energetic = (mine * occ * level).astype(jnp.bfloat16)
    sources = jnp.concatenate([tiles, received.reshape(-1, BS, width)], axis=0)
    count_sources = sources.shape[0]
    dense_d = jnp.einsum("rak,sbk->rsab", weighted, sources, preferred_element_type=jnp.float32)
    dense_e = jnp.einsum("rak,sbk->rsab", energetic, sources, preferred_element_type=jnp.float32)
    dense_d = dense_d.reshape(group_size * count_sources, BS, BS)
    dense_e = dense_e.reshape(group_size * count_sources, BS, BS)
    picks = pair_rows * count_sources + pair_sources
    return (dense_d[picks], dense_e[picks])


def solution(mesh):
    placed = (
        P("rows", "slab"),
        P(None, "slab"),
        P(None, "slab"),
        P("rows", None, None),
        P(("rows", "slab")),
        P(("rows", "slab")),
    )
    return jax.shard_map(
        body,
        mesh=mesh,
        in_specs=placed,
        out_specs=(P(("rows", "slab"), None, None), P(("rows", "slab"), None, None)),
        check_vma=False,
    )
```

profile of v0, /device:TPU:1, one launch (start us, length us, event | category | flops | bytes accessed | tf_op | source)
XLA Modules:
  0.0 288.1 jit_solution(17501657503381867024)
XLA Ops:
  7.2 0.0 all-gather.2.cloned.1.call-start
  7.2 0.7 all-gather.2.cloned.1.call-update
  7.9 0.7 compare_select_fusion
  8.6 0.1 copy.9
  8.7 0.1 reshape.56
  8.8 49.5 %all-gather.2.cloned.1.call-done = bf16[3072,1024]{1,0:T(8,128)(2,1)} async-done(((bf16[3072,128]{1,0:T(8,128)(2,1)}), bf16[3072,1024]{1,0:T(8,128)(2,1)}) %all-gather.2.cloned.1.call-update) | async-done | bytes 6291472 | tf_op jit(solution)/shard_map/all_gather | solution.py:12
  58.3 7.8 %gather_fusion = bf16[32,128,1024]{2,1,0:T(8,128)(2,1)} fusion(bf16[24,128,1024]{2,1,0:T(8,128)(2,1)} %bitcast.34, s32[1024]{0:T(1024)S(1)} %pad_clamp_fusion.1), kind=kCustom, calls=%fused_computation | custom fusion | bytes 16777344 | tf_op jit(solution)/shard_map/gather | solution.py:18
  66.1 0.0 copy-start
  66.1 0.0 copy-start.1
  66.1 0.0 copy-start.2
  66.1 0.0 copy-start.3
  66.1 0.0 slice-start
  66.1 6.8 %all-to-all-start = ((bf16[16,2,128,1024]{3,2,1,0:T(8,128)(2,1)}), bf16[16,2,128,1024]{3,2,1,0:T(8,128)(2,1)}, u32[]{:S(2)}, u32[]{:S(2)}) async-start(bf16[16,2,128,1024]{3,2,1,0:T(8,128)(2,1)} %bitcast.31), calls=%async_computation | async-start | bytes 16777216 | tf_op jit(solution)/shard_map/all_to_all | solution.py:19
  73.0 0.0 copy-done
  73.0 10.1 %all_gather.10 = bf16[1,1024]{1,0:T(2,128)(2,1)S(1)} all-gather(bf16[1,128]{1,0:T(2,128)(2,1)S(1)} %copy-done), channel_id=1, replica_groups=mesh['rows'=16,'slab'=8] {'slab'}, dimensions={1}, use_global_device_ids=true | all-gather | bytes 2304 | tf_op jit(solution)/shard_map/all_gather | solution.py:13
  83.1 0.0 copy-done.1
  83.1 8.0 %all_gather.11 = bf16[1,1024]{1,0:T(2,128)(2,1)S(1)} all-gather(bf16[1,128]{1,0:T(2,128)(2,1)S(1)} %copy-done.1), channel_id=1, replica_groups=mesh['rows'=16,'slab'=8] {'slab'}, dimensions={1}, use_global_device_ids=true | all-gather | bytes 2304 | tf_op jit(solution)/shard_map/all_gather | solution.py:14
  91.2 0.0 copy-done.2
  91.2 0.0 copy-done.3
  91.2 127.6 %all-to-all-done = bf16[16,2,128,1024]{3,2,1,0:T(8,128)(2,1)} async-done(((bf16[16,2,128,1024]{3,2,1,0:T(8,128)(2,1)}), bf16[16,2,128,1024]{3,2,1,0:T(8,128)(2,1)}, u32[]{:S(2)}, u32[]{:S(2)}) %all-to-all-start) | async-done | bytes 8388640 | tf_op jit(solution)/shard_map/all_to_all | solution.py:19
  218.9 0.0 slice-start.1
  218.9 13.9 %fusion.2 = f32[3,56,128,128]{2,3,0,1:T(8,128)} fusion(bf16[32,128,1024]{2,1,0:T(8,128)(2,1)} %bitcast.3, bf16[24,128,1024]{2,1,0:T(8,128)(2,1)} %bitcast.35, f32[1024]{0:T(1024)S(1)} %bitcast.39, s32[]{:T(128)S(6)} %select_n.18), kind=kOutput, calls=%fused_computation.6 | convolution fusion | flops 5667684352 | bytes 26480644 | tf_op jit(solution)/shard_map/rak,sbk->rsab/dot_general | solution.py:29
  232.8 0.0 slice-done
  232.8 0.0 slice-done.1
  232.8 11.1 %fusion.3 = f32[3,56,128,128]{2,3,0,1:T(8,128)} fusion(bf16[32,128,1024]{2,1,0:T(8,128)(2,1)} %bitcast.3, bf16[24,128,1024]{2,1,0:T(8,128)(2,1)S(1)} %bitcast.38, f32[1024]{0:T(1024)S(1)} %bitcast.41, f32[1024]{0:T(1024)S(1)} %bitcast.40, s32[]{:T(128)S(6)} %select_n.18), kind=kOutput, calls=%fused_computation.7 | convolution fusion | flops 5668077568 | bytes 26484740 | tf_op jit(solution)/shard_map/rak,sbk->rsab/dot_general | solution.py:30
  243.9 12.1 %copy.11 = f32[3,56,128,128]{3,2,1,0:T(8,128)} copy(f32[3,56,128,128]{2,3,0,1:T(8,128)} %fusion.3) | data formatting | bytes 22020096 | tf_op jit(solution)/shard_map/rak,sbk->rsab/transpose | solution.py:30
  256.0 12.1 %copy.10 = f32[3,56,128,128]{3,2,1,0:T(8,128)} copy(f32[3,56,128,128]{2,3,0,1:T(8,128)} %fusion.2) | data formatting | bytes 22020096 | tf_op jit(solution)/shard_map/rak,sbk->rsab/transpose | solution.py:29
  268.1 6.5 %gather_fusion.2 = f32[48,128,128]{2,1,0:T(8,128)} fusion(f32[168,128,128]{2,1,0:T(8,128)} %bitcast.33, s32[1024]{0:T(1024)S(1)} %pad_clamp_fusion), kind=kCustom, calls=%fused_computation.2 | custom fusion | bytes 6291648 | tf_op jit(solution)/shard_map/gather | solution.py:34
  274.7 6.5 %gather_fusion.1 = f32[48,128,128]{2,1,0:T(8,128)} fusion(f32[168,128,128]{2,1,0:T(8,128)} %bitcast.32, s32[1024]{0:T(1024)S(1)} %pad_clamp_fusion), kind=kCustom, calls=%fused_computation.1 | custom fusion | bytes 6291648 | tf_op jit(solution)/shard_map/gather | solution.py:34
  (6 shorter events, 0.0 us)
Async XLA Ops:
  7.2 51.2 %all-gather.2.cloned.1.call-start = ((), (), s32[]{:S(2)}) async-start(), calls=%async_computation.1 | async-start | bytes 7077888 | tf_op jit(solution)/shard_map/all_gather | solution.py:12
  66.1 6.9 %copy-start = (bf16[1,128]{1,0:T(2,128)(2,1)S(1)}, bf16[1,128]{1,0:T(2,128)(2,1)}, u32[]{:S(2)}) copy-start(bf16[1,128]{1,0:T(2,128)(2,1)} %param.7) | copy-start | bytes 772
  66.1 17.0 %copy-start.1 = (bf16[1,128]{1,0:T(2,128)(2,1)S(1)}, bf16[1,128]{1,0:T(2,128)(2,1)}, u32[]{:S(2)}) copy-start(bf16[1,128]{1,0:T(2,128)(2,1)} %param.8) | copy-start | bytes 772
  66.1 25.1 %copy-start.2 = (s32[48]{0:T(128)S(1)}, s32[48]{0:T(128)}, u32[]{:S(2)}) copy-start(s32[48]{0:T(128)} %param.11) | copy-start | bytes 580
  66.1 25.1 %copy-start.3 = (s32[48]{0:T(128)S(1)}, s32[48]{0:T(128)}, u32[]{:S(2)}) copy-start(s32[48]{0:T(128)} %param.10) | copy-start | bytes 580
  66.1 166.7 %slice-start = ((s8[6291456]{0:T(1024)(128)(4,1)}), s8[2097152]{0:T(1024)(128)(4,1)S(1)}, s32[]{:S(2)}) async-start(s8[6291456]{0:T(1024)(128)(4,1)} %bitcast.36), calls=%async_computation.2 | async-start | bytes 4194304
  66.1 152.7 %all-to-all-start = ((bf16[16,2,128,1024]{3,2,1,0:T(8,128)(2,1)}), bf16[16,2,128,1024]{3,2,1,0:T(8,128)(2,1)}, u32[]{:S(2)}, u32[]{:S(2)}) async-start(bf16[16,2,128,1024]{3,2,1,0:T(8,128)(2,1)} %bitcast.31), calls=%async_computation | async-start | bytes 16777216 | tf_op jit(solution)/shard_map/all_to_all | solution.py:19
  218.9 14.0 %slice-start.1 = ((s8[6291456]{0:T(1024)(128)(4,1)}), s8[4194304]{0:T(1024)(128)(4,1)S(1)}, s32[]{:S(2)}) async-start(s8[6291456]{0:T(1024)(128)(4,1)} %bitcast.36), calls=%async_computation.3 | async-start | bytes 8388608
Sparse Core Ops, SparseCore 0:
  9.7 48.5 all-gather.1
where the time goes:
time: 293 us; the launch traced here: 288 us
  waiting for transfers between devices  178 us (61%)
  local copies, waits for them, and re-layouts  45.3 us (15%)
  matrix products  25.1 us (9%)
  blocking collectives  18.2 us (6%)
  between operations  14.1 us (5%)
  starting transfers between devices  6.88 us (2%)
    all_to_all x1, waiting for transfers between devices, body(): lax.all_to_all(outgoing, 'rows', split_axis=0, concat_axis=0, tiled=True)  128 us
    all_gather x1, waiting for transfers between devices, body(): lax.all_gather(coefficients, 'slab', axis=1, tiled=True)  49.5 us
    dot_general x1, matrix products, body(): jnp.einsum('rak,sbk->rsab', weighted, sources, preferred_element_type=jnp...  13.9 us
    gather x2, local copies, waits for them, and re-layouts, body(): return (dense_d[picks], dense_e[picks])  13.1 us
    transpose x1, local copies, waits for them, and re-layouts, body(): jnp.einsum('rak,sbk->rsab', weighted, sources, preferred_element_type=jnp...  12.1 us
    transpose x1, local copies, waits for them, and re-layouts, body(): jnp.einsum('rak,sbk->rsab', energetic, sources, preferred_element_type=jn...  12.1 us
    dot_general x1, matrix products, body(): jnp.einsum('rak,sbk->rsab', energetic, sources, preferred_element_type=jn...  11.1 us
    all_gather x1, blocking collectives, body(): lax.all_gather(occupations, 'slab', axis=1, tiled=True)  10.1 us
  transfers between devices with their start and end apart: 2, of which 2 were waited for; matrix products, arithmetic and copies ran while one was open for 0% of the time, Pallas kernels for 0%

commit v1 on v0

v1 whole, which is shorter than its diff:
```python
import functools

import jax
import jax.numpy as jnp
from jax import lax
from jax.experimental import pallas as pl
from jax.experimental.pallas import tpu as pltpu
from jax.sharding import PartitionSpec as P

BS = 128
YS = 4
UNROLL = 4
VM = pl.BlockSpec(memory_space=pltpu.VMEM)
SM = pl.BlockSpec(memory_space=pltpu.SMEM)
ANY = pl.BlockSpec(memory_space=pl.ANY)


def load_all(held, s_ref, sem):
    copies = [pltpu.make_async_copy(ref, s_ref.at[k], sem.at[k]) for k, ref in enumerate(held)]
    for copy in copies:
        copy.start()
    return copies


def list_pairs(wanted, order, pairs):
    def add(g, count):
        order[count] = g
        return count + wanted(g).astype(jnp.int32)

    return lax.fori_loop(0, pairs, add, 0)


def run_pairs(order, count, row_ref, block_of, s_ref, w_ref, outs, stage, sem):
    def copies(j):
        return [pltpu.make_async_copy(stage.at[n, j], outs[n].at[order[j]], sem.at[n, j]) for n in range(2)]

    def compute(t, _):
        for u in range(UNROLL):
            j = t * UNROLL + u
            g = order[jnp.minimum(j, count - 1)]
            first = pl.multiple_of(block_of(g) * BS, BS)
            other = jnp.concatenate([s_ref[k, pl.ds(first, BS), :] for k in range(s_ref.shape[0])], axis=1)
            both = lax.dot_general(
                w_ref[row_ref[g]], other, (((1,), (1,)), ((), ())), preferred_element_type=jnp.float32
            )
            stage[0, j] = both[:BS]
            stage[1, j] = both[BS:]
        for u in range(UNROLL):
            j = t * UNROLL + u

            @pl.when(j < count)
            def _():
                for copy in copies(j):
                    copy.start()

        return 0

    def drain(j, _):
        for copy in copies(j):
            copy.wait()
        return 0

    lax.fori_loop(0, (count + UNROLL - 1) // UNROLL, compute, 0)
    lax.fori_loop(0, count, drain, 0)


def near_kernel(row_ref, src_ref, q_ref, level_ref, *refs, group, blocks):
    held = refs[:8]
    dens_ref, ener_ref, w_ref, token_ref, s_ref, stage, order, in_sem, sem = refs[8:]
    loads = load_all(held, s_ref, in_sem)
    count = list_pairs(lambda g: src_ref[g] < blocks, order, row_ref.shape[0])
    q = q_ref[0]
    c = q % 2
    for s in range(8):
        mine = s < 4
        core = c if mine else 1 - c
        turn = (0, 1 + core, 2 - core, 3)[s % 4]
        occ = level_ref[turn, 0 if mine else 2]
        level = level_ref[turn, 1 if mine else 3]
        loads[s].wait()
        for i in range(group):
            first = pl.multiple_of((q * group + i) * BS, BS)
            weighted = s_ref[s, pl.ds(first, BS), :].astype(jnp.float32) * occ
            w_ref[i, :BS, s * BS : (s + 1) * BS] = weighted.astype(jnp.bfloat16)
            w_ref[i, BS:, s * BS : (s + 1) * BS] = (weighted * level).astype(jnp.bfloat16)
    run_pairs(order, count, row_ref, lambda g: src_ref[g], s_ref, w_ref, [dens_ref, ener_ref], stage, sem)
    token_ref[...] = jnp.zeros_like(token_ref)


def far_kernel(row_ref, src_ref, w_ref, dens_in, ener_in, *refs, blocks):
    held = refs[:8]
    dens_ref, ener_ref, s_ref, stage, order, in_sem, sem = refs[8:]
    loads = load_all(held, s_ref, in_sem)
    count = list_pairs(lambda g: src_ref[g] >= blocks, order, row_ref.shape[0])
    for load in loads:
        load.wait()
    run_pairs(order, count, row_ref, lambda g: src_ref[g] - blocks, s_ref, w_ref, [dens_ref, ener_ref], stage, sem)


def hop(x, step):
    pairs = [(2 * y + c, 2 * ((y + YS + step * (1 - 2 * c)) % YS) + c) for y in range(YS) for c in range(2)]
    return lax.ppermute(x, "slab", pairs)


def turn(x, dy):
    pairs = [(2 * y + c, 2 * ((y + dy) % YS) + c) for y in range(YS) for c in range(2)]
    return lax.ppermute(x, "slab", pairs)


def swap(x):
    return lax.ppermute(x, "slab", [(q, q ^ 1) for q in range(2 * YS)])


def exchange(tiles, picks):
    picked = tiles.reshape(-1, BS, BS)[picks]
    return lax.all_to_all(picked, "rows", split_axis=0, concat_axis=0, tiled=True).reshape(-1, BS)


def after(x, *others):
    return lax.optimization_barrier((x, *others))[0]


def body(coefficients, occupations, energies, send_lists, pair_rows, pair_sources):
    blocks = coefficients.shape[0] // BS
    shards = lax.axis_size("slab")
    group = blocks // shards
    pairs = pair_rows.shape[0]
    own = coefficients
    front, back = hop(own, 1), hop(own, -1)
    level = jnp.concatenate([occupations, energies], axis=0)
    level = jnp.concatenate([level, swap(level)], axis=0)
    got = exchange(own, after(send_lists[0], level))
    levels = jnp.stack([level, turn(level, 1), turn(level, -1), turn(level, 2)])
    last = hop(after(front, back, levels), 1)
    levels = levels.astype(jnp.float32)[:, :, None, :]
    got_front, got_back = hop(got, 1), hop(got, -1)
    got_last = exchange(last, send_lists[0])
    held = [own, front, back, last]
    held = held + [swap(x) for x in held]
    q = lax.axis_index("slab").reshape(1).astype(jnp.int32)

    out = jax.ShapeDtypeStruct((pairs, BS, BS), jnp.float32)
    slots = pairs + UNROLL

    def scratch(rows):
        return [
            pltpu.VMEM((shards, rows, BS), jnp.bfloat16),
            pltpu.VMEM((2, slots, BS, BS), jnp.float32),
            pltpu.SMEM((slots,), jnp.int32),
            pltpu.SemaphoreType.DMA((shards,)),
            pltpu.SemaphoreType.DMA((2, slots)),
        ]

    params = pltpu.CompilerParams(vmem_limit_bytes=24 * 1024 * 1024)
    cost = pl.CostEstimate(flops=pairs * 4 * BS * BS * shards * BS, bytes_accessed=12 << 20, transcendentals=0)
    dens, ener, weights, token = pl.pallas_call(
        functools.partial(near_kernel, group=group, blocks=blocks),
        in_specs=[SM, SM, SM, VM] + [ANY] * len(held),
        out_specs=[ANY, ANY, VM, VM],
        scratch_shapes=scratch(blocks * BS),
        out_shape=[
            out,
            out,
            jax.ShapeDtypeStruct((group, 2 * BS, shards * BS), jnp.bfloat16),
            jax.ShapeDtypeStruct((8, BS), jnp.float32),
        ],
        compiler_params=params,
        cost_estimate=cost,
    )(pair_rows, pair_sources, q, levels, *held)
    received = [got, after(got_front, token), after(got_back, token), got_last]
    received = received + [swap(x) for x in received]
    return pl.pallas_call(
        functools.partial(far_kernel, blocks=blocks),
        in_specs=[SM, SM, VM, ANY, ANY] + [ANY] * len(received),
        out_specs=[ANY, ANY],
        scratch_shapes=scratch(got.shape[0]),
        out_shape=[out, out],
        input_output_aliases={3: 0, 4: 1},
        compiler_params=params,
        cost_estimate=cost,
    )(pair_rows, pair_sources, weights, dens, ener, *received)


def solution(mesh):
    placed = (
        P("rows", "slab"),
        P(None, "slab"),
        P(None, "slab"),
        P("rows", None, None),
        P(("rows", "slab")),
        P(("rows", "slab")),
    )
    return jax.shard_map(
        body,
        mesh=mesh,
        in_specs=placed,
        out_specs=(P(("rows", "slab"), None, None), P(("rows", "slab"), None, None)),
        check_vma=False,
    )
```

time: 293 us -> 84.6 us (0.29); the launches traced: 288 us -> 84.5 us
  waiting for transfers between devices: 178 us -> 9.59 us
  starting transfers between devices: 6.88 us -> 43 us
  local copies, waits for them, and re-layouts: 45.3 us -> 9.73 us
  matrix products: 25.1 us -> 0 us
  Pallas kernels: 0 us -> 19.2 us
  blocking collectives: 18.2 us -> 0 us
  between operations: 14.1 us -> 0.85 us
    all_to_all x1 -> x2, waiting for transfers between devices: 128 us -> 1.48 us  [exchange(): lax.all_to_all(picked, 'rows', split_axis=0, concat_axis=0, tiled=True)]
    all_gather x1 -> x0, waiting for transfers between devices: 49.5 us -> none  [body(): lax.all_gather(coefficients, 'slab', axis=1, tiled=True)]
    ppermute x0 -> x17, starting transfers between devices: none -> 28 us  [the longest x9 17.1 us: swap(): return lax.ppermute(x, 'slab', [(q, q ^ 1) for q in range(2 * YS)])]
    dot_general x2 -> x0, matrix products: 25.1 us -> none  [the longest x1 13.9 us: body(): jnp.einsum('rak,sbk->rsab', weighted, sources, preferred_element_type=jnp...]
    transpose x2 -> x0, local copies, waits for them, and re-layouts: 24.2 us -> none  [the longest x1 12.1 us: body(): jnp.einsum('rak,sbk->rsab', weighted, sources, preferred_element_type=jnp...]
    pallas_call x0 -> x2, Pallas kernels: none -> 19.2 us  [the longest x1 11 us: body(): pl.pallas_call(functools.partial(far_kernel, blocks=blocks), in_specs=[SM...]
    all_gather x2 -> x0, blocking collectives: 18.2 us -> none  [the longest x1 10.1 us: body(): lax.all_gather(occupations, 'slab', axis=1, tiled=True)]
    gather x3 -> x2, local copies, waits for them, and re-layouts: 20.9 us -> 5.61 us  [exchange(): picked = tiles.reshape(-1, BS, BS)[picks]]
  transfers between devices with their start and end apart: 2 -> 19, of which waited for: 2 -> 6; matrix products, arithmetic and copies ran while one was open for 0% -> 10% of each run, Pallas kernels for 0% -> 10%
where the time goes in v1:
time: 84.6 us; the launch traced here: 84.5 us
  starting transfers between devices  43 us (51%)
  Pallas kernels  19.2 us (23%)
  local copies, waits for them, and re-layouts  9.73 us (12%)
  waiting for transfers between devices  9.59 us (11%)
  other arithmetic  2.09 us (2%)
  between operations  0.85 us (1%)
    ppermute x9, starting transfers between devices, swap(): return lax.ppermute(x, 'slab', [(q, q ^ 1) for q in range(2 * YS)])  17.1 us
    all_to_all x2, starting transfers between devices, exchange(): lax.all_to_all(picked, 'rows', split_axis=0, concat_axis=0, tiled=True)  15 us
    pallas_call x1, Pallas kernels, body(): pl.pallas_call(functools.partial(far_kernel, blocks=blocks), in_specs=[SM...  11 us
    ppermute x5, starting transfers between devices, hop(): return lax.ppermute(x, 'slab', pairs)  8.36 us
    pallas_call x1, Pallas kernels, body(): pl.pallas_call(functools.partial(near_kernel, group=group, blocks=blocks)...  8.2 us
    gather x2, local copies, waits for them, and re-layouts, exchange(): picked = tiles.reshape(-1, BS, BS)[picks]  5.61 us
    unnamed x20, local copies, waits for them, and re-layouts  3.76 us
    ppermute x5, waiting for transfers between devices, hop(): return lax.ppermute(x, 'slab', pairs)  3.57 us
  transfers between devices with their start and end apart: 19, of which 6 were waited for; matrix products, arithmetic and copies ran while one was open for 10% of the time, Pallas kernels for 10%

profile of v1, /device:TPU:1, one launch (start us, length us, event | category | flops | bytes accessed | tf_op | source)
XLA Modules:
  0.0 84.5 jit_solution(10755947828435880214)
XLA Ops:
  0.6 0.0 copy-start.2
  0.6 0.0 copy-start.7
  0.7 2.2 %collective-permute-start.5 = (bf16[3072,128]{1,0:T(8,128)(2,1)}, bf16[3072,128]{1,0:T(8,128)(2,1)}, u32[]{:S(2)}, u32[]{:S(2)}) collective-permute-start(bf16[3072,128]{1,0:T(8,128)(2,1)} %refs_0_.1), channel_id=1, source_target_pairs={{0,6},{1,3},{2,0},{3,5},{4,2},{5,7},{6,4},{7,1},{8,14},{9,11},{10,... | collective-permute-start | bytes 2359304 | tf_op jit(solution)/shard_map/ppermute | solution.py:102
  2.8 1.5 %collective-permute-start.4 = (bf16[3072,128]{1,0:T(8,128)(2,1)}, bf16[3072,128]{1,0:T(8,128)(2,1)}, u32[]{:S(2)}, u32[]{:S(2)}) collective-permute-start(bf16[3072,128]{1,0:T(8,128)(2,1)} %refs_0_.1), channel_id=1, source_target_pairs={{0,2},{1,7},{2,4},{3,1},{4,6},{5,3},{6,0},{7,5},{8,10},{9,15},{10,... | collective-permute-start | bytes 2359304 | tf_op jit(solution)/shard_map/ppermute | solution.py:102
  4.4 0.7 pad_maximum_fusion.1
  5.1 0.9 %collective-permute-start = (bf16[2,128]{1,0:T(2,128)(2,1)S(1)}, bf16[2,128]{1,0:T(2,128)(2,1)S(1)}, u32[]{:S(2)}, u32[]{:S(2)}) collective-permute-start(bf16[2,128]{1,0:T(2,128)(2,1)S(1)} %pad_maximum_fusion.1), channel_id=1, source_target_pairs={{0,1},{1,0},{2,3},{3,2},{4,5},{5,4},{6,7},{7,6},{8,9},{9,8},{10,11... | collective-permute-start | bytes 1544 | tf_op jit(solution)/shard_map/ppermute | solution.py:111
  5.9 0.8 collective-permute-done
  6.7 0.7 pad_maximum_fusion
  7.4 0.7 compare_select_fusion.1
  8.1 0.1 copy.34
  8.2 0.1 reshape.113
  8.3 2.8 %gather_fusion = bf16[32,128,128]{2,1,0:T(8,128)(2,1)} fusion(bf16[24,128,128]{2,1,0:T(8,128)(2,1)} %bitcast.23, s32[1024]{0:T(1024)S(1)} %pad_clamp_fusion.1), kind=kCustom, calls=%fused_computation | custom fusion | bytes 2097280 | tf_op jit(solution)/shard_map/gather | solution.py:115
  11.1 7.7 %all-to-all-start = ((bf16[16,2,128,128]{3,2,1,0:T(8,128)(2,1)}), bf16[16,2,128,128]{3,2,1,0:T(8,128)(2,1)S(1)}, u32[]{:S(2)}, u32[]{:S(2)}) async-start(bf16[16,2,128,128]{3,2,1,0:T(8,128)(2,1)} %bitcast.7), calls=%async_computation | async-start | bytes 2097152 | tf_op jit(solution)/shard_map/all_to_all | solution.py:116
  18.8 0.0 copy-done.2
  18.9 0.7 collective-permute-start.7
  19.5 0.0 collective-permute-done.5.refs_2_
  19.5 3.0 %collective-permute-done.4.refs_1_ = bf16[3072,128]{1,0:T(8,128)(2,1)} collective-permute-done((bf16[3072,128]{1,0:T(8,128)(2,1)}, bf16[3072,128]{1,0:T(8,128)(2,1)}, u32[]{:S(2)}, u32[]{:S(2)}) %collective-permute-start.4) | collective-permute-done | bytes 786464 | tf_op jit(solution)/shard_map/ppermute | solution.py:102
  22.5 1.9 %collective-permute-start.6 = (bf16[3072,128]{1,0:T(8,128)(2,1)}, bf16[3072,128]{1,0:T(8,128)(2,1)}, u32[]{:S(2)}, u32[]{:S(2)}) collective-permute-start(bf16[3072,128]{1,0:T(8,128)(2,1)} %collective-permute-done.4.refs_1_), channel_id=1, source_target_pairs={{0,2},{1,7},{2,4},{3,1},{4,6},{5,3},{6,0},{7,5},{8,10},{9,15},{10,... | collective-permute-start | bytes 2359304 | tf_op jit(solution)/shard_map/ppermute | solution.py:102
  24.4 1.1 %collective-permute-start.3 = (bf16[4,128]{1,0:T(4,128)(2,1)S(1)}, bf16[4,128]{1,0:T(4,128)(2,1)S(1)}, u32[]{:S(2)}, u32[]{:S(2)}) collective-permute-start(bf16[4,128]{1,0:T(4,128)(2,1)S(1)} %pad_maximum_fusion), channel_id=1, source_target_pairs={{0,4},{1,5},{2,6},{3,7},{4,0},{5,1},{6,2},{7,3},{8,12},{9,13},{10,... | collective-permute-start | bytes 3080 | tf_op jit(solution)/shard_map/ppermute | solution.py:107
  25.5 0.8 collective-permute-start.2
  26.3 0.7 collective-permute-start.1
  27.0 0.0 copy-done.7
  27.0 0.1 copy.35
  27.1 0.1 reshape.121
  27.2 1.4 %collective-permute-done.3 = bf16[4,128]{1,0:T(4,128)(2,1)S(1)} collective-permute-done((bf16[4,128]{1,0:T(4,128)(2,1)S(1)}, bf16[4,128]{1,0:T(4,128)(2,1)S(1)}, u32[]{:S(2)}, u32[]{:S(2)}) %collective-permute-start.3) | collective-permute-done | bytes 1056 | tf_op jit(solution)/shard_map/ppermute | solution.py:107
  28.6 9.2 %collective-permute-start.9 = (bf16[3072,128]{1,0:T(8,128)(2,1)}, bf16[3072,128]{1,0:T(8,128)(2,1)}, u32[]{:S(2)}, u32[]{:S(2)}) collective-permute-start(bf16[3072,128]{1,0:T(8,128)(2,1)} %collective-permute-done.5.refs_2_), channel_id=1, source_target_pairs={{0,1},{1,0},{2,3},{3,2},{4,5},{5,4},{6,7},{7,6},{8,9},{9,8},{10,11... | collective-permute-start | bytes 2359304 | tf_op jit(solution)/shard_map/ppermute | solution.py:111
  37.8 0.0 collective-permute-done.2
  37.8 0.0 collective-permute-start.8
  37.8 0.0 collective-permute-done.1
  37.8 0.0 all-to-all-done
  37.8 0.1 collective-permute-start.12
  37.9 0.0 collective-permute-done.7.refs_4_
  37.9 0.0 copy-start.5
  37.9 2.6 %collective-permute-start.11 = (bf16[4096,128]{1,0:T(8,128)(2,1)S(1)}, bf16[4096,128]{1,0:T(8,128)(2,1)}, u32[]{:S(2)}, u32[]{:S(2)}) collective-permute-start(bf16[4096,128]{1,0:T(8,128)(2,1)S(1)} %bitcast.18), channel_id=1, source_target_pairs={{0,2},{1,7},{2,4},{3,1},{4,6},{5,3},{6,0},{7,5},{8,10},{9,15},{10,... | collective-permute-start | bytes 3145736 | tf_op jit(solution)/shard_map/ppermute | solution.py:102
  40.6 0.0 collective-permute-done.6.refs_3_
  40.6 0.4 collective-permute-start.10
  40.9 2.8 %gather_fusion.1 = bf16[32,128,128]{2,1,0:T(8,128)(2,1)} fusion(bf16[24,128,128]{2,1,0:T(8,128)(2,1)} %bitcast.9, s32[1024]{0:T(1024)S(1)} %pad_clamp_fusion), kind=kCustom, calls=%fused_computation.1 | custom fusion | bytes 2097280 | tf_op jit(solution)/shard_map/gather | solution.py:115
  43.8 0.0 copy-done.5
  43.8 7.2 %all-to-all-start.1 = ((bf16[16,2,128,128]{3,2,1,0:T(8,128)(2,1)}), bf16[16,2,128,128]{3,2,1,0:T(8,128)(2,1)S(1)}, u32[]{:S(2)}, u32[]{:S(2)}) async-start(bf16[16,2,128,128]{3,2,1,0:T(8,128)(2,1)} %bitcast.24), calls=%async_computation.1 | async-start | bytes 2097152 | tf_op jit(solution)/shard_map/all_to_all | solution.py:116
  51.0 0.0 copy-done.8
  51.0 0.0 copy-done.9
  51.1 0.0 collective-permute-done.9.refs_6_
  51.1 0.9 %collective-permute-start.13 = (bf16[4096,128]{1,0:T(8,128)(2,1)S(1)}, bf16[4096,128]{1,0:T(8,128)(2,1)}, u32[]{:S(2)}, u32[]{:S(2)}) collective-permute-start(bf16[4096,128]{1,0:T(8,128)(2,1)S(1)} %bitcast.19), channel_id=1, source_target_pairs={{0,1},{1,0},{2,3},{3,2},{4,5},{5,4},{6,7},{7,6},{8,9},{9,8},{10,11... | collective-permute-start | bytes 3145736 | tf_op jit(solution)/shard_map/ppermute | solution.py:111
  52.0 0.0 collective-permute-done.8.refs_5_
  52.0 0.0 collective-permute-done.10.refs_7_
  52.0 0.0 copy-done.3
  52.0 0.0 copy-done.4
  52.0 0.0 copy-start.6
  52.0 1.1 %copy-done.6 = bf16[3072,128]{1,0:T(8,128)(2,1)S(1)} copy-done((bf16[3072,128]{1,0:T(8,128)(2,1)S(1)}, bf16[3072,128]{1,0:T(8,128)(2,1)}, u32[]{:S(2)}) %copy-start.6) | copy-done | bytes 786456
  53.2 8.2 %shard_map.77 = (f32[48,128,128]{2,1,0:T(8,128)}, f32[48,128,128]{2,1,0:T(8,128)}, bf16[3,256,1024]{2,1,0:T(8,128)(2,1)S(1)}, f32[8,128]{1,0:T(8,128)}) custom-call(s32[48]{0:T(128)S(1)} %copy-done.3, s32[48]{0:T(128)S(1)} %copy-done.4, s32[1]{0:T(128)} %bitcast.q_ref, f32[4,4,1,128]{3,2,1,0:T(1,128)S(1)} %maximum_convert_fusion.level_ref, ...), custom_call_target="tpu_custom_call" | custom-call | flops 3221225472 | bytes 12582912 | tf_op jit(solution)/shard_map/pallas_call | solution.py:156
  61.4 0.0 copy-start
  61.4 1.2 %copy-done = bf16[3,256,1024]{2,1,0:T(8,128)(2,1)} copy-done((bf16[3,256,1024]{2,1,0:T(8,128)(2,1)}, bf16[3,256,1024]{2,1,0:T(8,128)(2,1)S(1)}, u32[]{:S(2)}) %copy-start) | copy-done | bytes 1572888
  62.6 0.0 collective-permute-done.12.refs_2_
  62.6 0.6 collective-permute-done.11.refs_1_
  63.2 1.6 %collective-permute-start.14 = (bf16[4096,128]{1,0:T(8,128)(2,1)}, bf16[4096,128]{1,0:T(8,128)(2,1)S(1)}, u32[]{:S(2)}, u32[]{:S(2)}) collective-permute-start(bf16[4096,128]{1,0:T(8,128)(2,1)} %collective-permute-done.11.refs_1_), channel_id=1, source_target_pairs={{0,1},{1,0},{2,3},{3,2},{4,5},{5,4},{6,7},{7,6},{8,9},{9,8},{10,11... | collective-permute-start | bytes 3145736 | tf_op jit(solution)/shard_map/ppermute | solution.py:111
  64.8 0.0 collective-permute-start.15
  64.8 1.5 %all-to-all-done.1 = bf16[16,2,128,128]{3,2,1,0:T(8,128)(2,1)S(1)} async-done(((bf16[16,2,128,128]{3,2,1,0:T(8,128)(2,1)}), bf16[16,2,128,128]{3,2,1,0:T(8,128)(2,1)S(1)}, u32[]{:S(2)}, u32[]{:S(2)}) %all-to-all-start.1) | async-done | bytes 1048608 | tf_op jit(solution)/shard_map/all_to_all | solution.py:116
  66.3 3.5 %collective-permute-start.16 = (bf16[4096,128]{1,0:T(8,128)(2,1)S(1)}, bf16[4096,128]{1,0:T(8,128)(2,1)S(1)}, u32[]{:S(2)}, u32[]{:S(2)}) collective-permute-start(bf16[4096,128]{1,0:T(8,128)(2,1)S(1)} %bitcast.21), channel_id=1, source_target_pairs={{0,1},{1,0},{2,3},{3,2},{4,5},{5,4},{6,7},{7,6},{8,9},{9,8},{10,11... | collective-permute-start | bytes 3145736 | tf_op jit(solution)/shard_map/ppermute | solution.py:111
  69.8 0.0 collective-permute-done.13.refs_4_
  69.8 0.0 collective-permute-done.14.refs_5_
  69.8 0.0 collective-permute-done.15.refs_6_
  69.8 2.3 %collective-permute-done.16.refs_7_ = bf16[4096,128]{1,0:T(8,128)(2,1)S(1)} collective-permute-done((bf16[4096,128]{1,0:T(8,128)(2,1)S(1)}, bf16[4096,128]{1,0:T(8,128)(2,1)S(1)}, u32[]{:S(2)}, u32[]{:S(2)}) %collective-permute-start.16) | collective-permute-done | bytes 1048608 | tf_op jit(solution)/shard_map/ppermute | solution.py:111
  72.1 1.4 %copy-done.1 = bf16[3,256,1024]{2,1,0:T(8,128)(2,1)S(1)} copy-done((bf16[3,256,1024]{2,1,0:T(8,128)(2,1)S(1)}, bf16[3,256,1024]{2,1,0:T(8,128)(2,1)}, u32[]{:S(2)}) %copy-start.1) | copy-done | bytes 1572888
  73.5 11.0 %shard_map.78 = (f32[48,128,128]{2,1,0:T(8,128)}, f32[48,128,128]{2,1,0:T(8,128)}) custom-call(s32[48]{0:T(128)S(1)} %copy-done.3, s32[48]{0:T(128)S(1)} %copy-done.4, bf16[3,256,1024]{2,1,0:T(8,128)(2,1)S(1)} %copy-done.1, f32[48,128,128]{2,1,0:T(8,128)} %get-tuple-element.12.dens_in, ...), custom_call_target="tpu_custom_call", output_to_operand_aliasing={{0}: (3, {}), {1}: (4, {})} | custom-call | flops 3221225472 | bytes 12582912 | tf_op jit(solution)/shard_map/pallas_call | solution.py:172
  (14 shorter events, 0.1 us)
Async XLA Ops:
  0.6 18.2 %copy-start.2 = (bf16[3072,128]{1,0:T(8,128)(2,1)S(1)}, bf16[3072,128]{1,0:T(8,128)(2,1)}, u32[]{:S(2)}) copy-start(bf16[3072,128]{1,0:T(8,128)(2,1)} %refs_0_.1) | copy-start | bytes 2359300
  0.6 26.4 %copy-start.7 = (s32[1,16,2]{1,2,0:T(2,128)S(1)}, s32[1,16,2]{1,2,0:T(2,128)}, u32[]{:S(2)}) copy-start(s32[1,16,2]{1,2,0:T(2,128)} %param.9) | copy-start | bytes 388
  0.7 18.9 %collective-permute-start.5 = (bf16[3072,128]{1,0:T(8,128)(2,1)}, bf16[3072,128]{1,0:T(8,128)(2,1)}, u32[]{:S(2)}, u32[]{:S(2)}) collective-permute-start(bf16[3072,128]{1,0:T(8,128)(2,1)} %refs_0_.1), channel_id=1, source_target_pairs={{0,6},{1,3},{2,0},{3,5},{4,2},{5,7},{6,4},{7,1},{8,14},{9,11},{10,... | collective-permute-start | bytes 2359304 | tf_op jit(solution)/shard_map/ppermute | solution.py:102
  2.8 19.6 %collective-permute-start.4 = (bf16[3072,128]{1,0:T(8,128)(2,1)}, bf16[3072,128]{1,0:T(8,128)(2,1)}, u32[]{:S(2)}, u32[]{:S(2)}) collective-permute-start(bf16[3072,128]{1,0:T(8,128)(2,1)} %refs_0_.1), channel_id=1, source_target_pairs={{0,2},{1,7},{2,4},{3,1},{4,6},{5,3},{6,0},{7,5},{8,10},{9,15},{10,... | collective-permute-start | bytes 2359304 | tf_op jit(solution)/shard_map/ppermute | solution.py:102
  5.1 1.7 %collective-permute-start = (bf16[2,128]{1,0:T(2,128)(2,1)S(1)}, bf16[2,128]{1,0:T(2,128)(2,1)S(1)}, u32[]{:S(2)}, u32[]{:S(2)}) collective-permute-start(bf16[2,128]{1,0:T(2,128)(2,1)S(1)} %pad_maximum_fusion.1), channel_id=1, source_target_pairs={{0,1},{1,0},{2,3},{3,2},{4,5},{5,4},{6,7},{7,6},{8,9},{9,8},{10,11... | collective-permute-start | bytes 1544 | tf_op jit(solution)/shard_map/ppermute | solution.py:111
  11.1 39.9 %copy-start.8 = (bf16[1,128]{1,0:T(2,128)(2,1)S(1)}, bf16[1,128]{1,0:T(2,128)(2,1)}, u32[]{:S(2)}) copy-start(bf16[1,128]{1,0:T(2,128)(2,1)} %param.8) | copy-start | bytes 772
  11.1 40.0 %copy-start.9 = (bf16[1,128]{1,0:T(2,128)(2,1)S(1)}, bf16[1,128]{1,0:T(2,128)(2,1)}, u32[]{:S(2)}) copy-start(bf16[1,128]{1,0:T(2,128)(2,1)} %param.7) | copy-start | bytes 772
  11.1 40.9 %copy-start.3 = (s32[48]{0:T(128)S(1)}, s32[48]{0:T(128)}, u32[]{:S(2)}) copy-start(s32[48]{0:T(128)} %row_ref.3) | copy-start | bytes 580
  11.1 40.9 %copy-start.4 = (s32[48]{0:T(128)S(1)}, s32[48]{0:T(128)}, u32[]{:S(2)}) copy-start(s32[48]{0:T(128)} %src_ref.3) | copy-start | bytes 580
  11.1 26.7 %all-to-all-start = ((bf16[16,2,128,128]{3,2,1,0:T(8,128)(2,1)}), bf16[16,2,128,128]{3,2,1,0:T(8,128)(2,1)S(1)}, u32[]{:S(2)}, u32[]{:S(2)}) async-start(bf16[16,2,128,128]{3,2,1,0:T(8,128)(2,1)} %bitcast.7), calls=%async_computation | async-start | bytes 2097152 | tf_op jit(solution)/shard_map/all_to_all | solution.py:116
  18.9 19.1 %collective-permute-start.7 = (bf16[3072,128]{1,0:T(8,128)(2,1)S(1)}, bf16[3072,128]{1,0:T(8,128)(2,1)S(1)}, u32[]{:S(2)}, u32[]{:S(2)}) collective-permute-start(bf16[3072,128]{1,0:T(8,128)(2,1)S(1)} %copy-done.2), channel_id=1, source_target_pairs={{0,1},{1,0},{2,3},{3,2},{4,5},{5,4},{6,7},{7,6},{8,9},{9,8},{10,11... | collective-permute-start | bytes 2359304 | tf_op jit(solution)/shard_map/ppermute | solution.py:111
  22.5 18.1 %collective-permute-start.6 = (bf16[3072,128]{1,0:T(8,128)(2,1)}, bf16[3072,128]{1,0:T(8,128)(2,1)}, u32[]{:S(2)}, u32[]{:S(2)}) collective-permute-start(bf16[3072,128]{1,0:T(8,128)(2,1)} %collective-permute-done.4.refs_1_), channel_id=1, source_target_pairs={{0,2},{1,7},{2,4},{3,1},{4,6},{5,3},{6,0},{7,5},{8,10},{9,15},{10,... | collective-permute-start | bytes 2359304 | tf_op jit(solution)/shard_map/ppermute | solution.py:102
  24.4 4.2 %collective-permute-start.3 = (bf16[4,128]{1,0:T(4,128)(2,1)S(1)}, bf16[4,128]{1,0:T(4,128)(2,1)S(1)}, u32[]{:S(2)}, u32[]{:S(2)}) collective-permute-start(bf16[4,128]{1,0:T(4,128)(2,1)S(1)} %pad_maximum_fusion), channel_id=1, source_target_pairs={{0,4},{1,5},{2,6},{3,7},{4,0},{5,1},{6,2},{7,3},{8,12},{9,13},{10,... | collective-permute-start | bytes 3080 | tf_op jit(solution)/shard_map/ppermute | solution.py:107
  25.5 12.3 %collective-permute-start.2 = (bf16[4,128]{1,0:T(4,128)(2,1)S(1)}, bf16[4,128]{1,0:T(4,128)(2,1)S(1)}, u32[]{:S(2)}, u32[]{:S(2)}) collective-permute-start(bf16[4,128]{1,0:T(4,128)(2,1)S(1)} %pad_maximum_fusion), channel_id=1, source_target_pairs={{0,6},{1,7},{2,0},{3,1},{4,2},{5,3},{6,4},{7,5},{8,14},{9,15},{10,... | collective-permute-start | bytes 3080 | tf_op jit(solution)/shard_map/ppermute | solution.py:107
  26.3 11.5 %collective-permute-start.1 = (bf16[4,128]{1,0:T(4,128)(2,1)S(1)}, bf16[4,128]{1,0:T(4,128)(2,1)S(1)}, u32[]{:S(2)}, u32[]{:S(2)}) collective-permute-start(bf16[4,128]{1,0:T(4,128)(2,1)S(1)} %pad_maximum_fusion), channel_id=1, source_target_pairs={{0,2},{1,3},{2,4},{3,5},{4,6},{5,7},{6,0},{7,1},{8,10},{9,11},{10,... | collective-permute-start | bytes 3080 | tf_op jit(solution)/shard_map/ppermute | solution.py:107
  28.6 22.5 %collective-permute-start.9 = (bf16[3072,128]{1,0:T(8,128)(2,1)}, bf16[3072,128]{1,0:T(8,128)(2,1)}, u32[]{:S(2)}, u32[]{:S(2)}) collective-permute-start(bf16[3072,128]{1,0:T(8,128)(2,1)} %collective-permute-done.5.refs_2_), channel_id=1, source_target_pairs={{0,1},{1,0},{2,3},{3,2},{4,5},{5,4},{6,7},{7,6},{8,9},{9,8},{10,11... | collective-permute-start | bytes 2359304 | tf_op jit(solution)/shard_map/ppermute | solution.py:111
  37.8 14.2 %collective-permute-start.8 = (bf16[3072,128]{1,0:T(8,128)(2,1)}, bf16[3072,128]{1,0:T(8,128)(2,1)}, u32[]{:S(2)}, u32[]{:S(2)}) collective-permute-start(bf16[3072,128]{1,0:T(8,128)(2,1)} %collective-permute-done.4.refs_1_), channel_id=1, source_target_pairs={{0,1},{1,0},{2,3},{3,2},{4,5},{5,4},{6,7},{7,6},{8,9},{9,8},{10,11... | collective-permute-start | bytes 2359304 | tf_op jit(solution)/shard_map/ppermute | solution.py:111
  37.8 24.8 %collective-permute-start.12 = (bf16[4096,128]{1,0:T(8,128)(2,1)S(1)}, bf16[4096,128]{1,0:T(8,128)(2,1)}, u32[]{:S(2)}, u32[]{:S(2)}) collective-permute-start(bf16[4096,128]{1,0:T(8,128)(2,1)S(1)} %bitcast.17), channel_id=1, source_target_pairs={{0,6},{1,3},{2,0},{3,5},{4,2},{5,7},{6,4},{7,1},{8,14},{9,11},{10,... | collective-permute-start | bytes 3145736 | tf_op jit(solution)/shard_map/ppermute | solution.py:102
  37.9 5.9 %copy-start.5 = (bf16[3072,128]{1,0:T(8,128)(2,1)}, bf16[3072,128]{1,0:T(8,128)(2,1)S(1)}, u32[]{:S(2)}) copy-start(bf16[3072,128]{1,0:T(8,128)(2,1)S(1)} %collective-permute-done.7.refs_4_) | copy-start | bytes 2359300
  37.9 25.2 %collective-permute-start.11 = (bf16[4096,128]{1,0:T(8,128)(2,1)S(1)}, bf16[4096,128]{1,0:T(8,128)(2,1)}, u32[]{:S(2)}, u32[]{:S(2)}) collective-permute-start(bf16[4096,128]{1,0:T(8,128)(2,1)S(1)} %bitcast.18), channel_id=1, source_target_pairs={{0,2},{1,7},{2,4},{3,1},{4,6},{5,3},{6,0},{7,5},{8,10},{9,15},{10,... | collective-permute-start | bytes 3145736 | tf_op jit(solution)/shard_map/ppermute | solution.py:102
  40.6 11.4 %collective-permute-start.10 = (bf16[3072,128]{1,0:T(8,128)(2,1)}, bf16[3072,128]{1,0:T(8,128)(2,1)}, u32[]{:S(2)}, u32[]{:S(2)}) collective-permute-start(bf16[3072,128]{1,0:T(8,128)(2,1)} %collective-permute-done.6.refs_3_), channel_id=1, source_target_pairs={{0,1},{1,0},{2,3},{3,2},{4,5},{5,4},{6,7},{7,6},{8,9},{9,8},{10,11... | collective-permute-start | bytes 2359304 | tf_op jit(solution)/shard_map/ppermute | solution.py:111
  43.8 22.5 %all-to-all-start.1 = ((bf16[16,2,128,128]{3,2,1,0:T(8,128)(2,1)}), bf16[16,2,128,128]{3,2,1,0:T(8,128)(2,1)S(1)}, u32[]{:S(2)}, u32[]{:S(2)}) async-start(bf16[16,2,128,128]{3,2,1,0:T(8,128)(2,1)} %bitcast.24), calls=%async_computation.1 | async-start | bytes 2097152 | tf_op jit(solution)/shard_map/all_to_all | solution.py:116
  51.1 18.6 %collective-permute-start.13 = (bf16[4096,128]{1,0:T(8,128)(2,1)S(1)}, bf16[4096,128]{1,0:T(8,128)(2,1)}, u32[]{:S(2)}, u32[]{:S(2)}) collective-permute-start(bf16[4096,128]{1,0:T(8,128)(2,1)S(1)} %bitcast.19), channel_id=1, source_target_pairs={{0,1},{1,0},{2,3},{3,2},{4,5},{5,4},{6,7},{7,6},{8,9},{9,8},{10,11... | collective-permute-start | bytes 3145736 | tf_op jit(solution)/shard_map/ppermute | solution.py:111
  52.0 1.1 %copy-start.6 = (bf16[3072,128]{1,0:T(8,128)(2,1)S(1)}, bf16[3072,128]{1,0:T(8,128)(2,1)}, u32[]{:S(2)}) copy-start(bf16[3072,128]{1,0:T(8,128)(2,1)} %copy-done.5) | copy-start | bytes 2359300
  61.4 1.2 %copy-start = (bf16[3,256,1024]{2,1,0:T(8,128)(2,1)}, bf16[3,256,1024]{2,1,0:T(8,128)(2,1)S(1)}, u32[]{:S(2)}) copy-start(bf16[3,256,1024]{2,1,0:T(8,128)(2,1)S(1)} %get-tuple-element.11.w_ref) | copy-start | bytes 4718596
  63.2 6.6 %collective-permute-start.14 = (bf16[4096,128]{1,0:T(8,128)(2,1)}, bf16[4096,128]{1,0:T(8,128)(2,1)S(1)}, u32[]{:S(2)}, u32[]{:S(2)}) collective-permute-start(bf16[4096,128]{1,0:T(8,128)(2,1)} %collective-permute-done.11.refs_1_), channel_id=1, source_target_pairs={{0,1},{1,0},{2,3},{3,2},{4,5},{5,4},{6,7},{7,6},{8,9},{9,8},{10,11... | collective-permute-start | bytes 3145736 | tf_op jit(solution)/shard_map/ppermute | solution.py:111
  64.8 5.0 %collective-permute-start.15 = (bf16[4096,128]{1,0:T(8,128)(2,1)}, bf16[4096,128]{1,0:T(8,128)(2,1)}, u32[]{:S(2)}, u32[]{:S(2)}) collective-permute-start(bf16[4096,128]{1,0:T(8,128)(2,1)} %collective-permute-done.12.refs_2_), channel_id=1, source_target_pairs={{0,1},{1,0},{2,3},{3,2},{4,5},{5,4},{6,7},{7,6},{8,9},{9,8},{10,11... | collective-permute-start | bytes 3145736 | tf_op jit(solution)/shard_map/ppermute | solution.py:111
  66.3 5.8 %collective-permute-start.16 = (bf16[4096,128]{1,0:T(8,128)(2,1)S(1)}, bf16[4096,128]{1,0:T(8,128)(2,1)S(1)}, u32[]{:S(2)}, u32[]{:S(2)}) collective-permute-start(bf16[4096,128]{1,0:T(8,128)(2,1)S(1)} %bitcast.21), channel_id=1, source_target_pairs={{0,1},{1,0},{2,3},{3,2},{4,5},{5,4},{6,7},{7,6},{8,9},{9,8},{10,11... | collective-permute-start | bytes 3145736 | tf_op jit(solution)/shard_map/ppermute | solution.py:111
  72.1 1.4 %copy-start.1 = (bf16[3,256,1024]{2,1,0:T(8,128)(2,1)S(1)}, bf16[3,256,1024]{2,1,0:T(8,128)(2,1)}, u32[]{:S(2)}) copy-start(bf16[3,256,1024]{2,1,0:T(8,128)(2,1)} %copy-done) | copy-start | bytes 4718596

commit v2 on v1

v2 whole, which is shorter than its diff:
```python
import functools

import jax
import jax.numpy as jnp
from jax import lax
from jax.experimental import pallas as pl
from jax.experimental.pallas import tpu as pltpu
from jax.sharding import PartitionSpec as P

BS = 128
YS = 4
UNROLL = 3
PART = 16
VM = pl.BlockSpec(memory_space=pltpu.VMEM)
SM = pl.BlockSpec(memory_space=pltpu.SMEM)
HB = pl.BlockSpec(memory_space=pltpu.HBM)
ANY = pl.BlockSpec(memory_space=pl.ANY)


def load_all(held, s_ref, sem):
    copies = [pltpu.make_async_copy(ref, s_ref.at[k], sem.at[k]) for k, ref in enumerate(held)]
    for copy in copies:
        copy.start()
    return copies


def list_pairs(bucket, pairs, order, counts):
    span = order.shape[0] // counts.shape[0]
    for n in range(counts.shape[0]):
        counts[n] = 0

    def add(g, _):
        n = bucket(g)
        at = counts[n]
        order[n * span + at] = g
        counts[n] = at + 1
        return 0

    lax.fori_loop(0, pairs, add, 0)


def list_batches(buckets, group, order, counts, batch, total):
    span = order.shape[0] // counts.shape[0]
    for n in buckets:

        def put(t, total, n=n):
            batch[3 * total] = n % group
            batch[3 * total + 1] = order[n * span + 2 * t]
            batch[3 * total + 2] = jnp.where(2 * t + 1 < counts[n], order[n * span + 2 * t + 1], -1)
            return total + 1

        total = lax.fori_loop(0, (counts[n] + 1) // 2, put, total)
    return total


def out_copies(b, batch, outs, stage, sem, act):
    def both(j, g):
        for n in range(2):
            act(pltpu.make_async_copy(stage.at[n, j], outs[n].at[g], sem.at[n, j]))

    both(2 * b, batch[3 * b + 1])
    second = batch[3 * b + 2]

    @pl.when(second >= 0)
    def _():
        both(2 * b + 1, second)


def run_batches(start, stop, batch, tiles, w_ref, outs, stage, sem):
    def compute(t, _):
        for u in range(UNROLL):
            b = jnp.minimum(start + t * UNROLL + u, stop - 1)
            first, second = batch[3 * b + 1], batch[3 * b + 2]
            other = jnp.concatenate([tiles(first), tiles(jnp.where(second < 0, first, second))], axis=0)
            both = lax.dot_general(
                w_ref[batch[3 * b]], other, (((1,), (1,)), ((), ())), preferred_element_type=jnp.float32
            )
            j = 2 * (start + t * UNROLL + u)
            for n in range(2):
                stage[n, j] = both[n * BS : (n + 1) * BS, :BS]
                stage[n, j + 1] = both[n * BS : (n + 1) * BS, BS:]
        for u in range(UNROLL):
            b = start + t * UNROLL + u

            @pl.when(b < stop)
            def _():
                out_copies(b, batch, outs, stage, sem, lambda copy: copy.start())

        return 0

    lax.fori_loop(0, (stop - start + UNROLL - 1) // UNROLL, compute, 0)


def drain(total, batch, outs, stage, sem):
    def one(b, _):
        out_copies(b, batch, outs, stage, sem, lambda copy: copy.wait())
        return 0

    lax.fori_loop(0, total, one, 0)


def block_tiles(s_ref, first):
    return jnp.concatenate([s_ref[k, pl.ds(first, BS), :] for k in range(s_ref.shape[0])], axis=1)


def near_kernel(row_ref, src_ref, q_ref, level_ref, *refs, group, blocks):
    held = refs[:8]
    dens_ref, ener_ref, w_ref, far_batch, far_total, s_ref, stage, order, counts, batch, in_sem, sem = refs[8:]
    loads = load_all(held, s_ref, in_sem)
    pairs, half = row_ref.shape[0], counts.shape[0] // group - 1

    def bucket(g):
        kind = jnp.where(src_ref[g] < blocks, 0, 1 + (src_ref[g] - blocks) // PART)
        return kind * group + row_ref[g]

    list_pairs(bucket, pairs, order, counts)
    zero = jnp.int32(0)
    total = list_batches(range(group), group, order, counts, batch, zero)
    done = zero
    for n in range(half):
        done = list_batches(range((n + 1) * group, (n + 2) * group), group, order, counts, far_batch, done)
        far_total[n] = done
    c = q_ref[0] % 2
    for s in range(8):
        mine = s < 4
        core = c if mine else 1 - c
        turn = (0, 1 + core, 2 - core, 3)[s % 4]
        occ = level_ref[turn, 0 if mine else 2]
        level = level_ref[turn, 1 if mine else 3]
        loads[s].wait()
        for i in range(group):
            first = pl.multiple_of((q_ref[0] * group + i) * BS, BS)
            weighted = s_ref[s, pl.ds(first, BS), :].astype(jnp.float32) * occ
            w_ref[i, :BS, s * BS : (s + 1) * BS] = weighted.astype(jnp.bfloat16)
            w_ref[i, BS:, s * BS : (s + 1) * BS] = (weighted * level).astype(jnp.bfloat16)

    def tiles(g):
        return block_tiles(s_ref, pl.multiple_of(src_ref[g] * BS, BS))

    outs = [dens_ref, ener_ref]
    run_batches(zero, total, batch, tiles, w_ref, outs, stage, sem)
    drain(total, batch, outs, stage, sem)


def far_kernel(src_ref, batch, totals, w_ref, dens_in, ener_in, *refs, blocks):
    held = refs[:8]
    dens_ref, ener_ref, s_ref, stage, in_sem, sem = refs[8:]
    parts = totals.shape[0]
    rows = s_ref.shape[1] // parts
    loads = []
    for n in range(parts):
        part = pl.ds(n * rows, rows)
        loads.append([])
        for k, ref in enumerate(held):
            copy = pltpu.make_async_copy(ref.at[part], s_ref.at[k, part], in_sem.at[n, k])
            copy.start()
            loads[n].append(copy)

    def tiles(g):
        return block_tiles(s_ref, pl.multiple_of((src_ref[g] - blocks) * BS, BS))

    outs = [dens_ref, ener_ref]
    start = jnp.int32(0)
    for n in range(parts):
        for copy in loads[n]:
            copy.wait()
        run_batches(start, totals[n], batch, tiles, w_ref, outs, stage, sem)
        start = totals[n]
    drain(start, batch, outs, stage, sem)


def hop(x, step):
    pairs = [(2 * y + c, 2 * ((y + YS + step * (1 - 2 * c)) % YS) + c) for y in range(YS) for c in range(2)]
    return lax.ppermute(x, "slab", pairs)


def turn(x, dy):
    pairs = [(2 * y + c, 2 * ((y + dy) % YS) + c) for y in range(YS) for c in range(2)]
    return lax.ppermute(x, "slab", pairs)


def swap(x):
    return lax.ppermute(x, "slab", [(q, q ^ 1) for q in range(2 * YS)])


def exchange(tiles, picks):
    tiles = tiles.reshape(-1, BS, BS).at[picks].get(mode="promise_in_bounds", wrap_negative_indices=False)
    return lax.all_to_all(tiles, "rows", split_axis=0, concat_axis=0, tiled=True).reshape(-1, BS)


def limit(mib):
    return pltpu.CompilerParams(vmem_limit_bytes=mib * 1024 * 1024)


def hbm(x):
    return pltpu.with_memory_space_constraint(x, pltpu.HBM)


def body(coefficients, occupations, energies, send_lists, pair_rows, pair_sources):
    blocks = coefficients.shape[0] // BS
    shards = lax.axis_size("slab")
    group = blocks // shards
    pairs = pair_rows.shape[0]
    own = coefficients
    front, back = hop(own, 1), hop(own, -1)
    got = exchange(own, send_lists[0])
    level = jnp.concatenate([occupations, energies], axis=0)
    level = jnp.concatenate([level, swap(level)], axis=0)
    front, back, level, own_x = lax.optimization_barrier((front, back, level, swap(own)))
    last = hop(front, 1)
    turned = [turn(level, 1), turn(level, -1), turn(level, 2)]
    got, front, back, *turned = lax.optimization_barrier((got, front, back, *turned))
    levels = jnp.stack([level, *turned]).astype(jnp.float32)[:, :, None, :]
    got_front, got_back = hop(got, 1), hop(got, -1)
    got_last = exchange(last, send_lists[0])
    held = [own, front, back, last, own_x, swap(front), swap(back), swap(last)]
    q = lax.axis_index("slab").reshape(1).astype(jnp.int32)

    out = jax.ShapeDtypeStruct((pairs, BS, BS), jnp.float32)
    parts = got.shape[0] // (PART * BS)
    slots = pairs + 2 * (group * parts + UNROLL)
    cost = pl.CostEstimate(flops=pairs * 4 * BS * BS * shards * BS, bytes_accessed=12 << 20, transcendentals=0)
    dens, ener, weights, batch, totals = pl.pallas_call(
        functools.partial(near_kernel, group=group, blocks=blocks),
        in_specs=[SM, SM, SM, VM] + [HB] * len(held),
        out_specs=[HB, HB, VM, SM, SM],
        scratch_shapes=[
            pltpu.VMEM((shards, blocks * BS, BS), jnp.bfloat16),
            pltpu.VMEM((2, slots, BS, BS), jnp.float32),
            pltpu.SMEM(((1 + parts) * group * pairs,), jnp.int32),
            pltpu.SMEM(((1 + parts) * group,), jnp.int32),
            pltpu.SMEM((3 * slots // 2,), jnp.int32),
            pltpu.SemaphoreType.DMA((shards,)),
            pltpu.SemaphoreType.DMA((2, slots)),
        ],
        out_shape=[
            out,
            out,
            jax.ShapeDtypeStruct((group, 2 * BS, shards * BS), jnp.bfloat16),
            jax.ShapeDtypeStruct((3 * slots // 2,), jnp.int32),
            jax.ShapeDtypeStruct((parts,), jnp.int32),
        ],
        compiler_params=limit(20),
        cost_estimate=cost,
    )(pair_rows, pair_sources, q, levels, *[hbm(x) for x in held])
    got_front, got_back, weights = lax.optimization_barrier((got_front, got_back, weights))
    received = [got, got_front, got_back, got_last]
    received = received + [swap(x) for x in received]
    return pl.pallas_call(
        functools.partial(far_kernel, blocks=blocks),
        in_specs=[SM, SM, SM, VM, HB, HB] + [HB] * 7 + [ANY],
        out_specs=[HB, HB],
        scratch_shapes=[
            pltpu.VMEM((shards, got.shape[0], BS), jnp.bfloat16),
            pltpu.VMEM((2, slots, BS, BS), jnp.float32),
            pltpu.SemaphoreType.DMA((parts, shards)),
            pltpu.SemaphoreType.DMA((2, slots)),
        ],
        out_shape=[out, out],
        input_output_aliases={4: 0, 5: 1},
        compiler_params=limit(20),
        cost_estimate=cost,
    )(pair_sources, batch, totals, weights, dens, ener, *[hbm(x) for x in received[:7]], received[7])


def solution(mesh):
    placed = (
        P("rows", "slab"),
        P(None, "slab"),
        P(None, "slab"),
        P("rows", None, None),
        P(("rows", "slab")),
        P(("rows", "slab")),
    )
    return jax.shard_map(
        body,
        mesh=mesh,
        in_specs=placed,
        out_specs=(P(("rows", "slab"), None, None), P(("rows", "slab"), None, None)),
        check_vma=False,
    )
```

time: 84.6 us -> 81.7 us (0.966)
  waiting for transfers between devices: 9.59 us -> 24.1 us
  starting transfers between devices: 43 us -> 34.2 us
  local copies, waits for them, and re-layouts: 9.73 us -> 5.32 us
  Pallas kernels: 19.2 us -> 16.9 us
  other arithmetic: 2.09 us -> 0.04 us
    ppermute x9, starting transfers between devices: 17.1 us -> 8.77 us  [swap(): return lax.ppermute(x, 'slab', [(q, q ^ 1) for q in range(2 * YS)])]
    ppermute x3, waiting for transfers between devices: 1.43 us -> 7.79 us  [turn(): return lax.ppermute(x, 'slab', pairs)]
    ppermute x5, waiting for transfers between devices: 3.57 us -> 9.38 us  [hop(): return lax.ppermute(x, 'slab', pairs)]
    unnamed x20 -> x15, local copies, waits for them, and re-layouts: 3.76 us -> 0.78 us
    pallas_call x1, Pallas kernels: 11 us -> 8.52 us  [body(): pl.pallas_call(functools.partial(far_kernel, blocks=blocks), in_specs=[SM...]
    all_to_all x2, waiting for transfers between devices: 1.48 us -> 3.65 us  [exchange(): lax.all_to_all(tiles, 'rows', split_axis=0, concat_axis=0, tiled=True)]
    gather x2, local copies, waits for them, and re-layouts: 5.61 us -> 4.44 us  [exchange(): tiles.reshape(-1, BS, BS).at[picks]]
    ppermute x3, starting transfers between devices: 2.61 us -> 1.49 us  [turn(): return lax.ppermute(x, 'slab', pairs)]
  transfers between devices with their start and end apart: 19 -> 19, of which waited for: 6 -> 8; matrix products, arithmetic and copies ran while one was open for 10% -> 7% of each run, Pallas kernels for 10% -> 10%
where the time goes in v2:
time: 81.7 us; the launch traced here: 81.5 us
  starting transfers between devices  34.2 us (42%)
  waiting for transfers between devices  24.1 us (29%)
  Pallas kernels  16.9 us (21%)
  local copies, waits for them, and re-layouts  5.32 us (7%)
  between operations  0.84 us (1%)
    all_to_all x2, starting transfers between devices, exchange(): lax.all_to_all(tiles, 'rows', split_axis=0, concat_axis=0, tiled=True)  15.4 us
    ppermute x5, waiting for transfers between devices, hop(): return lax.ppermute(x, 'slab', pairs)  9.38 us
    ppermute x9, starting transfers between devices, swap(): return lax.ppermute(x, 'slab', [(q, q ^ 1) for q in range(2 * YS)])  8.77 us
    ppermute x5, starting transfers between devices, hop(): return lax.ppermute(x, 'slab', pairs)  8.55 us
    pallas_call x1, Pallas kernels, body(): pl.pallas_call(functools.partial(far_kernel, blocks=blocks), in_specs=[SM...  8.52 us
    pallas_call x1, Pallas kernels, body(): pl.pallas_call(functools.partial(near_kernel, group=group, blocks=blocks)...  8.41 us
    ppermute x3, waiting for transfers between devices, turn(): return lax.ppermute(x, 'slab', pairs)  7.79 us
    gather x2, local copies, waits for them, and re-layouts, exchange(): tiles.reshape(-1, BS, BS).at[picks]  4.44 us
  transfers between devices with their start and end apart: 19, of which 8 were waited for; matrix products, arithmetic and copies ran while one was open for 7% of the time, Pallas kernels for 10%

profile of v2, /device:TPU:1, one launch (start us, length us, event | category | flops | bytes accessed | tf_op | source)
XLA Modules:
  0.0 81.5 jit_solution(15445988181615502278)
XLA Ops:
  0.6 0.0 copy-start.4
  0.6 0.0 copy-start.5
  0.7 1.5 %collective-permute-start.3 = (bf16[3072,128]{1,0:T(8,128)(2,1)}, bf16[3072,128]{1,0:T(8,128)(2,1)S(1)}, u32[]{:S(2)}, u32[]{:S(2)}) collective-permute-start(bf16[3072,128]{1,0:T(8,128)(2,1)} %refs_0_.1), channel_id=1, source_target_pairs={{0,1},{1,0},{2,3},{3,2},{4,5},{5,4},{6,7},{7,6},{8,9},{9,8},{10,11... | collective-permute-start | bytes 2359304 | tf_op jit(solution)/shard_map/ppermute | solution.py:183
  2.2 1.4 %collective-permute-start.1 = (bf16[3072,128]{1,0:T(8,128)(2,1)}, bf16[3072,128]{1,0:T(8,128)(2,1)}, u32[]{:S(2)}, u32[]{:S(2)}) collective-permute-start(bf16[3072,128]{1,0:T(8,128)(2,1)} %refs_0_.1), channel_id=1, source_target_pairs={{0,6},{1,3},{2,0},{3,5},{4,2},{5,7},{6,4},{7,1},{8,14},{9,11},{10,... | collective-permute-start | bytes 2359304 | tf_op jit(solution)/shard_map/ppermute | solution.py:174
  3.5 1.5 %collective-permute-start = (bf16[3072,128]{1,0:T(8,128)(2,1)}, bf16[3072,128]{1,0:T(8,128)(2,1)}, u32[]{:S(2)}, u32[]{:S(2)}) collective-permute-start(bf16[3072,128]{1,0:T(8,128)(2,1)} %refs_0_.1), channel_id=1, source_target_pairs={{0,2},{1,7},{2,4},{3,1},{4,6},{5,3},{6,0},{7,5},{8,10},{9,15},{10,... | collective-permute-start | bytes 2359304 | tf_op jit(solution)/shard_map/ppermute | solution.py:174
  5.0 0.8 copy.26
  5.7 0.1 reshape.85
  5.8 2.8 %gather_fusion = bf16[32,128,128]{2,1,0:T(8,128)(2,1)} fusion(bf16[24,128,128]{2,1,0:T(8,128)(2,1)} %bitcast.15, s32[1024]{0:T(1024)S(1)} %pad_clamp_fusion), kind=kCustom, calls=%fused_computation | custom fusion | bytes 2097280 | tf_op jit(solution)/shard_map/gather | solution.py:187
  8.6 0.0 copy-start
  8.6 0.0 copy-start.1
  8.6 7.7 %all-to-all-start = ((bf16[16,2,128,128]{3,2,1,0:T(8,128)(2,1)}), bf16[16,2,128,128]{3,2,1,0:T(8,128)(2,1)S(1)}, u32[]{:S(2)}, u32[]{:S(2)}) async-start(bf16[16,2,128,128]{3,2,1,0:T(8,128)(2,1)} %bitcast.3), calls=%async_computation | async-start | bytes 2097152 | tf_op jit(solution)/shard_map/all_to_all | solution.py:188
  16.4 0.0 copy-done.4
  16.4 0.0 copy-done.5
  16.4 0.7 collective-permute-start.2
  17.1 0.8 %collective-permute-done.2 = bf16[2,128]{1,0:T(2,128)(2,1)S(1)} collective-permute-done((bf16[2,128]{1,0:T(2,128)(2,1)S(1)}, bf16[2,128]{1,0:T(2,128)(2,1)S(1)}, u32[]{:S(2)}, u32[]{:S(2)}) %collective-permute-start.2) | collective-permute-done | bytes 544 | tf_op jit(solution)/shard_map/ppermute | solution.py:183
  17.9 0.0 collective-permute-done.3.refs_4_
  18.0 0.0 copy-start.6
  18.0 1.9 %collective-permute-done.1.refs_2_ = bf16[3072,128]{1,0:T(8,128)(2,1)} collective-permute-done((bf16[3072,128]{1,0:T(8,128)(2,1)}, bf16[3072,128]{1,0:T(8,128)(2,1)}, u32[]{:S(2)}, u32[]{:S(2)}) %collective-permute-start.1) | collective-permute-done | bytes 786464 | tf_op jit(solution)/shard_map/ppermute | solution.py:174
  19.8 2.8 %collective-permute-done.refs_1_ = bf16[3072,128]{1,0:T(8,128)(2,1)} collective-permute-done((bf16[3072,128]{1,0:T(8,128)(2,1)}, bf16[3072,128]{1,0:T(8,128)(2,1)}, u32[]{:S(2)}, u32[]{:S(2)}) %collective-permute-start) | collective-permute-done | bytes 786464 | tf_op jit(solution)/shard_map/ppermute | solution.py:174
  22.6 3.0 %collective-permute-start.7 = (bf16[3072,128]{1,0:T(8,128)(2,1)}, bf16[3072,128]{1,0:T(8,128)(2,1)S(1)}, u32[]{:S(2)}, u32[]{:S(2)}) collective-permute-start(bf16[3072,128]{1,0:T(8,128)(2,1)} %collective-permute-done.refs_1_), channel_id=1, source_target_pairs={{0,2},{1,7},{2,4},{3,1},{4,6},{5,3},{6,0},{7,5},{8,10},{9,15},{10,... | collective-permute-start | bytes 2359304 | tf_op jit(solution)/shard_map/ppermute | solution.py:174
  25.6 0.0 collective-permute-start.6
  25.6 0.8 collective-permute-start.5
  26.4 0.7 collective-permute-start.4
  27.1 2.6 %collective-permute-done.6 = bf16[4,128]{1,0:T(4,128)(2,1)S(1)} collective-permute-done((bf16[4,128]{1,0:T(4,128)(2,1)S(1)}, bf16[4,128]{1,0:T(4,128)(2,1)S(1)}, u32[]{:S(2)}, u32[]{:S(2)}) %collective-permute-start.6) | collective-permute-done | bytes 1056 | tf_op jit(solution)/shard_map/ppermute | solution.py:179
  29.7 5.2 %collective-permute-done.5 = bf16[4,128]{1,0:T(4,128)(2,1)S(1)} collective-permute-done((bf16[4,128]{1,0:T(4,128)(2,1)S(1)}, bf16[4,128]{1,0:T(4,128)(2,1)S(1)}, u32[]{:S(2)}, u32[]{:S(2)}) %collective-permute-start.5) | collective-permute-done | bytes 1056 | tf_op jit(solution)/shard_map/ppermute | solution.py:179
  34.9 0.0 collective-permute-done.4
  34.9 0.0 all-to-all-done
  34.9 0.0 copy-start.2
  34.9 3.6 %collective-permute-start.8 = (bf16[3072,128]{1,0:T(8,128)(2,1)}, bf16[3072,128]{1,0:T(8,128)(2,1)}, u32[]{:S(2)}, u32[]{:S(2)}) collective-permute-start(bf16[3072,128]{1,0:T(8,128)(2,1)} %collective-permute-done.refs_1_), channel_id=1, source_target_pairs={{0,1},{1,0},{2,3},{3,2},{4,5},{5,4},{6,7},{7,6},{8,9},{9,8},{10,11... | collective-permute-start | bytes 2359304 | tf_op jit(solution)/shard_map/ppermute | solution.py:183
  38.5 0.1 collective-permute-start.9
  38.6 0.0 collective-permute-done.7.refs_3_
  38.6 0.0 copy-start.3
  38.6 0.4 collective-permute-start.10
  39.0 0.0 collective-permute-start.12
  39.0 2.7 %collective-permute-start.11 = (bf16[4096,128]{1,0:T(8,128)(2,1)S(1)}, bf16[4096,128]{1,0:T(8,128)(2,1)}, u32[]{:S(2)}, u32[]{:S(2)}) collective-permute-start(bf16[4096,128]{1,0:T(8,128)(2,1)S(1)} %bitcast.12), channel_id=1, source_target_pairs={{0,2},{1,7},{2,4},{3,1},{4,6},{5,3},{6,0},{7,5},{8,10},{9,15},{10,... | collective-permute-start | bytes 3145736 | tf_op jit(solution)/shard_map/ppermute | solution.py:174
  41.7 1.7 %gather_fusion.1 = bf16[32,128,128]{2,1,0:T(8,128)(2,1)} fusion(bf16[24,128,128]{2,1,0:T(8,128)(2,1)S(1)} %bitcast.16, s32[1024]{0:T(1024)S(1)} %pad_clamp_fusion), kind=kCustom, calls=%fused_computation.1 | custom fusion | bytes 2097280 | tf_op jit(solution)/shard_map/gather | solution.py:187
  43.4 7.6 %all-to-all-start.1 = ((bf16[16,2,128,128]{3,2,1,0:T(8,128)(2,1)}), bf16[16,2,128,128]{3,2,1,0:T(8,128)(2,1)}, u32[]{:S(2)}, u32[]{:S(2)}) async-start(bf16[16,2,128,128]{3,2,1,0:T(8,128)(2,1)} %bitcast.9), calls=%async_computation.1 | async-start | bytes 2097152 | tf_op jit(solution)/shard_map/all_to_all | solution.py:188
  51.1 0.0 collective-permute-done.8.refs_5_
  51.1 0.1 collective-permute-start.13
  51.2 0.0 collective-permute-done.9.refs_6_
  51.2 0.0 collective-permute-done.10.refs_7_
  51.2 0.0 copy-done.6
  51.2 0.0 copy-done.3
  51.2 0.0 copy-done
  51.3 0.0 copy-done.1
  51.3 8.4 %shard_map.77 = (f32[48,128,128]{2,1,0:T(8,128)}, f32[48,128,128]{2,1,0:T(8,128)}, bf16[3,256,1024]{2,1,0:T(8,128)(2,1)S(1)}, s32[99]{0:T(128)S(1)}, s32[2]{0:T(128)S(1)}) custom-call(s32[48]{0:T(128)S(1)} %copy-done.1, s32[48]{0:T(128)S(1)} %copy-done, s32[1]{0:T(128)} %bitcast.q_ref, f32[4,4,1,128]{3,2,1,0:T(1,128)S(1)} %maximum_convert_fusion.level_ref, ...), custom_call_target="tpu_custom_call" | custom-call | flops 3221225472 | bytes 12582912 | tf_op jit(solution)/shard_map/pallas_call | solution.py:223
  59.7 0.0 copy-done.2
  59.7 4.8 %collective-permute-done.12.refs_2_ = bf16[4096,128]{1,0:T(8,128)(2,1)} collective-permute-done((bf16[4096,128]{1,0:T(8,128)(2,1)S(1)}, bf16[4096,128]{1,0:T(8,128)(2,1)}, u32[]{:S(2)}, u32[]{:S(2)}) %collective-permute-start.12) | collective-permute-done | bytes 1048608 | tf_op jit(solution)/shard_map/ppermute | solution.py:174
  64.5 0.0 collective-permute-done.11.refs_1_
  64.5 1.5 %collective-permute-start.14 = (bf16[4096,128]{1,0:T(8,128)(2,1)}, bf16[4096,128]{1,0:T(8,128)(2,1)}, u32[]{:S(2)}, u32[]{:S(2)}) collective-permute-start(bf16[4096,128]{1,0:T(8,128)(2,1)} %collective-permute-done.11.refs_1_), channel_id=1, source_target_pairs={{0,1},{1,0},{2,3},{3,2},{4,5},{5,4},{6,7},{7,6},{8,9},{9,8},{10,11... | collective-permute-start | bytes 3145736 | tf_op jit(solution)/shard_map/ppermute | solution.py:183
  65.9 0.0 collective-permute-start.15
  65.9 3.6 %all-to-all-done.1 = bf16[16,2,128,128]{3,2,1,0:T(8,128)(2,1)} async-done(((bf16[16,2,128,128]{3,2,1,0:T(8,128)(2,1)}), bf16[16,2,128,128]{3,2,1,0:T(8,128)(2,1)}, u32[]{:S(2)}, u32[]{:S(2)}) %all-to-all-start.1) | async-done | bytes 1048608 | tf_op jit(solution)/shard_map/all_to_all | solution.py:188
  69.6 0.9 %collective-permute-start.16 = (bf16[4096,128]{1,0:T(8,128)(2,1)}, bf16[4096,128]{1,0:T(8,128)(2,1)S(1)}, u32[]{:S(2)}, u32[]{:S(2)}) collective-permute-start(bf16[4096,128]{1,0:T(8,128)(2,1)} %bitcast.10.refs_3_), channel_id=1, source_target_pairs={{0,1},{1,0},{2,3},{3,2},{4,5},{5,4},{6,7},{7,6},{8,9},{9,8},{10,11... | collective-permute-start | bytes 3145736 | tf_op jit(solution)/shard_map/ppermute | solution.py:183
  70.5 0.0 collective-permute-done.13.refs_4_
  70.5 0.0 collective-permute-done.14.refs_5_
  70.5 0.0 collective-permute-done.15.refs_6_
  70.5 2.5 %collective-permute-done.16.refs_7_ = bf16[4096,128]{1,0:T(8,128)(2,1)S(1)} collective-permute-done((bf16[4096,128]{1,0:T(8,128)(2,1)}, bf16[4096,128]{1,0:T(8,128)(2,1)S(1)}, u32[]{:S(2)}, u32[]{:S(2)}) %collective-permute-start.16) | collective-permute-done | bytes 1048608 | tf_op jit(solution)/shard_map/ppermute | solution.py:183
  73.0 8.5 %shard_map.78 = (f32[48,128,128]{2,1,0:T(8,128)}, f32[48,128,128]{2,1,0:T(8,128)}) custom-call(s32[48]{0:T(128)S(1)} %copy-done, s32[99]{0:T(128)S(1)} %get-tuple-element.29.batch, s32[2]{0:T(128)S(1)} %get-tuple-element.30.totals, bf16[3,256,1024]{2,1,0:T(8,128)(2,1)S(1)} %get-tuple-element.33.w_ref, ...), custom_call_target="tpu_custom_call", output_to_operand_aliasing={{0}: (4, {}), {1}: (5, {})} | custom-call | flops 3221225472 | bytes 12582912 | tf_op jit(solution)/shard_map/pallas_call | solution.py:249
  (8 shorter events, 0.1 us)
Async XLA Ops:
  0.6 15.7 %copy-start.4 = (bf16[1,128]{1,0:T(2,128)(2,1)S(1)}, bf16[1,128]{1,0:T(2,128)(2,1)}, u32[]{:S(2)}) copy-start(bf16[1,128]{1,0:T(2,128)(2,1)} %param.8) | copy-start | bytes 772
  0.6 15.7 %copy-start.5 = (bf16[1,128]{1,0:T(2,128)(2,1)S(1)}, bf16[1,128]{1,0:T(2,128)(2,1)}, u32[]{:S(2)}) copy-start(bf16[1,128]{1,0:T(2,128)(2,1)} %param.7) | copy-start | bytes 772
  0.7 17.3 %collective-permute-start.3 = (bf16[3072,128]{1,0:T(8,128)(2,1)}, bf16[3072,128]{1,0:T(8,128)(2,1)S(1)}, u32[]{:S(2)}, u32[]{:S(2)}) collective-permute-start(bf16[3072,128]{1,0:T(8,128)(2,1)} %refs_0_.1), channel_id=1, source_target_pairs={{0,1},{1,0},{2,3},{3,2},{4,5},{5,4},{6,7},{7,6},{8,9},{9,8},{10,11... | collective-permute-start | bytes 2359304 | tf_op jit(solution)/shard_map/ppermute | solution.py:183
  2.2 17.7 %collective-permute-start.1 = (bf16[3072,128]{1,0:T(8,128)(2,1)}, bf16[3072,128]{1,0:T(8,128)(2,1)}, u32[]{:S(2)}, u32[]{:S(2)}) collective-permute-start(bf16[3072,128]{1,0:T(8,128)(2,1)} %refs_0_.1), channel_id=1, source_target_pairs={{0,6},{1,3},{2,0},{3,5},{4,2},{5,7},{6,4},{7,1},{8,14},{9,11},{10,... | collective-permute-start | bytes 2359304 | tf_op jit(solution)/shard_map/ppermute | solution.py:174
  3.5 19.0 %collective-permute-start = (bf16[3072,128]{1,0:T(8,128)(2,1)}, bf16[3072,128]{1,0:T(8,128)(2,1)}, u32[]{:S(2)}, u32[]{:S(2)}) collective-permute-start(bf16[3072,128]{1,0:T(8,128)(2,1)} %refs_0_.1), channel_id=1, source_target_pairs={{0,2},{1,7},{2,4},{3,1},{4,6},{5,3},{6,0},{7,5},{8,10},{9,15},{10,... | collective-permute-start | bytes 2359304 | tf_op jit(solution)/shard_map/ppermute | solution.py:174
  8.6 42.6 %copy-start = (s32[48]{0:T(128)S(1)}, s32[48]{0:T(128)}, u32[]{:S(2)}) copy-start(s32[48]{0:T(128)} %src_ref.3) | copy-start | bytes 580
  8.6 42.6 %copy-start.1 = (s32[48]{0:T(128)S(1)}, s32[48]{0:T(128)}, u32[]{:S(2)}) copy-start(s32[48]{0:T(128)} %row_ref.1) | copy-start | bytes 580
  8.6 26.3 %all-to-all-start = ((bf16[16,2,128,128]{3,2,1,0:T(8,128)(2,1)}), bf16[16,2,128,128]{3,2,1,0:T(8,128)(2,1)S(1)}, u32[]{:S(2)}, u32[]{:S(2)}) async-start(bf16[16,2,128,128]{3,2,1,0:T(8,128)(2,1)} %bitcast.3), calls=%async_computation | async-start | bytes 2097152 | tf_op jit(solution)/shard_map/all_to_all | solution.py:188
  16.4 1.5 %collective-permute-start.2 = (bf16[2,128]{1,0:T(2,128)(2,1)S(1)}, bf16[2,128]{1,0:T(2,128)(2,1)S(1)}, u32[]{:S(2)}, u32[]{:S(2)}) collective-permute-start(bf16[2,128]{1,0:T(2,128)(2,1)S(1)} %pad_maximum_fusion.1), channel_id=1, source_target_pairs={{0,1},{1,0},{2,3},{3,2},{4,5},{5,4},{6,7},{7,6},{8,9},{9,8},{10,11... | collective-permute-start | bytes 1544 | tf_op jit(solution)/shard_map/ppermute | solution.py:183
  18.0 33.3 %copy-start.6 = (bf16[3072,128]{1,0:T(8,128)(2,1)}, bf16[3072,128]{1,0:T(8,128)(2,1)S(1)}, u32[]{:S(2)}) copy-start(bf16[3072,128]{1,0:T(8,128)(2,1)S(1)} %collective-permute-done.3.refs_4_) | copy-start | bytes 2359300
  22.6 16.0 %collective-permute-start.7 = (bf16[3072,128]{1,0:T(8,128)(2,1)}, bf16[3072,128]{1,0:T(8,128)(2,1)S(1)}, u32[]{:S(2)}, u32[]{:S(2)}) collective-permute-start(bf16[3072,128]{1,0:T(8,128)(2,1)} %collective-permute-done.refs_1_), channel_id=1, source_target_pairs={{0,2},{1,7},{2,4},{3,1},{4,6},{5,3},{6,0},{7,5},{8,10},{9,15},{10,... | collective-permute-start | bytes 2359304 | tf_op jit(solution)/shard_map/ppermute | solution.py:174
  25.6 4.1 %collective-permute-start.6 = (bf16[4,128]{1,0:T(4,128)(2,1)S(1)}, bf16[4,128]{1,0:T(4,128)(2,1)S(1)}, u32[]{:S(2)}, u32[]{:S(2)}) collective-permute-start(bf16[4,128]{1,0:T(4,128)(2,1)S(1)} %pad_maximum_fusion), channel_id=1, source_target_pairs={{0,4},{1,5},{2,6},{3,7},{4,0},{5,1},{6,2},{7,3},{8,12},{9,13},{10,... | collective-permute-start | bytes 3080 | tf_op jit(solution)/shard_map/ppermute | solution.py:179
  25.6 9.3 %collective-permute-start.5 = (bf16[4,128]{1,0:T(4,128)(2,1)S(1)}, bf16[4,128]{1,0:T(4,128)(2,1)S(1)}, u32[]{:S(2)}, u32[]{:S(2)}) collective-permute-start(bf16[4,128]{1,0:T(4,128)(2,1)S(1)} %pad_maximum_fusion), channel_id=1, source_target_pairs={{0,6},{1,7},{2,0},{3,1},{4,2},{5,3},{6,4},{7,5},{8,14},{9,15},{10,... | collective-permute-start | bytes 3080 | tf_op jit(solution)/shard_map/ppermute | solution.py:179
  26.4 8.5 %collective-permute-start.4 = (bf16[4,128]{1,0:T(4,128)(2,1)S(1)}, bf16[4,128]{1,0:T(4,128)(2,1)S(1)}, u32[]{:S(2)}, u32[]{:S(2)}) collective-permute-start(bf16[4,128]{1,0:T(4,128)(2,1)S(1)} %pad_maximum_fusion), channel_id=1, source_target_pairs={{0,2},{1,3},{2,4},{3,5},{4,6},{5,7},{6,0},{7,1},{8,10},{9,11},{10,... | collective-permute-start | bytes 3080 | tf_op jit(solution)/shard_map/ppermute | solution.py:179
  34.9 24.8 %copy-start.2 = (bf16[16,2,128,128]{3,2,1,0:T(8,128)(2,1)}, bf16[16,2,128,128]{3,2,1,0:T(8,128)(2,1)S(1)}, u32[]{:S(2)}) copy-start(bf16[16,2,128,128]{3,2,1,0:T(8,128)(2,1)S(1)} %all-to-all-done) | copy-start | bytes 3145732
  34.9 16.2 %collective-permute-start.8 = (bf16[3072,128]{1,0:T(8,128)(2,1)}, bf16[3072,128]{1,0:T(8,128)(2,1)}, u32[]{:S(2)}, u32[]{:S(2)}) collective-permute-start(bf16[3072,128]{1,0:T(8,128)(2,1)} %collective-permute-done.refs_1_), channel_id=1, source_target_pairs={{0,1},{1,0},{2,3},{3,2},{4,5},{5,4},{6,7},{7,6},{8,9},{9,8},{10,11... | collective-permute-start | bytes 2359304 | tf_op jit(solution)/shard_map/ppermute | solution.py:183
  38.5 12.7 %collective-permute-start.9 = (bf16[3072,128]{1,0:T(8,128)(2,1)}, bf16[3072,128]{1,0:T(8,128)(2,1)}, u32[]{:S(2)}, u32[]{:S(2)}) collective-permute-start(bf16[3072,128]{1,0:T(8,128)(2,1)} %collective-permute-done.1.refs_2_), channel_id=1, source_target_pairs={{0,1},{1,0},{2,3},{3,2},{4,5},{5,4},{6,7},{7,6},{8,9},{9,8},{10,11... | collective-permute-start | bytes 2359304 | tf_op jit(solution)/shard_map/ppermute | solution.py:183
  38.6 12.6 %copy-start.3 = (bf16[3072,128]{1,0:T(8,128)(2,1)}, bf16[3072,128]{1,0:T(8,128)(2,1)S(1)}, u32[]{:S(2)}) copy-start(bf16[3072,128]{1,0:T(8,128)(2,1)S(1)} %collective-permute-done.7.refs_3_) | copy-start | bytes 2359300
  38.6 12.6 %collective-permute-start.10 = (bf16[3072,128]{1,0:T(8,128)(2,1)S(1)}, bf16[3072,128]{1,0:T(8,128)(2,1)}, u32[]{:S(2)}, u32[]{:S(2)}) collective-permute-start(bf16[3072,128]{1,0:T(8,128)(2,1)S(1)} %collective-permute-done.7.refs_3_), channel_id=1, source_target_pairs={{0,1},{1,0},{2,3},{3,2},{4,5},{5,4},{6,7},{7,6},{8,9},{9,8},{10,11... | collective-permute-start | bytes 2359304 | tf_op jit(solution)/shard_map/ppermute | solution.py:183
  39.0 25.4 %collective-permute-start.12 = (bf16[4096,128]{1,0:T(8,128)(2,1)S(1)}, bf16[4096,128]{1,0:T(8,128)(2,1)}, u32[]{:S(2)}, u32[]{:S(2)}) collective-permute-start(bf16[4096,128]{1,0:T(8,128)(2,1)S(1)} %bitcast.11), channel_id=1, source_target_pairs={{0,6},{1,3},{2,0},{3,5},{4,2},{5,7},{6,4},{7,1},{8,14},{9,11},{10,... | collective-permute-start | bytes 3145736 | tf_op jit(solution)/shard_map/ppermute | solution.py:174
  39.0 25.4 %collective-permute-start.11 = (bf16[4096,128]{1,0:T(8,128)(2,1)S(1)}, bf16[4096,128]{1,0:T(8,128)(2,1)}, u32[]{:S(2)}, u32[]{:S(2)}) collective-permute-start(bf16[4096,128]{1,0:T(8,128)(2,1)S(1)} %bitcast.12), channel_id=1, source_target_pairs={{0,2},{1,7},{2,4},{3,1},{4,6},{5,3},{6,0},{7,5},{8,10},{9,15},{10,... | collective-permute-start | bytes 3145736 | tf_op jit(solution)/shard_map/ppermute | solution.py:174
  43.4 26.2 %all-to-all-start.1 = ((bf16[16,2,128,128]{3,2,1,0:T(8,128)(2,1)}), bf16[16,2,128,128]{3,2,1,0:T(8,128)(2,1)}, u32[]{:S(2)}, u32[]{:S(2)}) async-start(bf16[16,2,128,128]{3,2,1,0:T(8,128)(2,1)} %bitcast.9), calls=%async_computation.1 | async-start | bytes 2097152 | tf_op jit(solution)/shard_map/all_to_all | solution.py:188
  51.1 19.3 %collective-permute-start.13 = (bf16[4096,128]{1,0:T(8,128)(2,1)S(1)}, bf16[4096,128]{1,0:T(8,128)(2,1)}, u32[]{:S(2)}, u32[]{:S(2)}) collective-permute-start(bf16[4096,128]{1,0:T(8,128)(2,1)S(1)} %bitcast.13), channel_id=1, source_target_pairs={{0,1},{1,0},{2,3},{3,2},{4,5},{5,4},{6,7},{7,6},{8,9},{9,8},{10,11... | collective-permute-start | bytes 3145736 | tf_op jit(solution)/shard_map/ppermute | solution.py:183
  64.5 6.0 %collective-permute-start.14 = (bf16[4096,128]{1,0:T(8,128)(2,1)}, bf16[4096,128]{1,0:T(8,128)(2,1)}, u32[]{:S(2)}, u32[]{:S(2)}) collective-permute-start(bf16[4096,128]{1,0:T(8,128)(2,1)} %collective-permute-done.11.refs_1_), channel_id=1, source_target_pairs={{0,1},{1,0},{2,3},{3,2},{4,5},{5,4},{6,7},{7,6},{8,9},{9,8},{10,11... | collective-permute-start | bytes 3145736 | tf_op jit(solution)/shard_map/ppermute | solution.py:183
  65.9 4.5 %collective-permute-start.15 = (bf16[4096,128]{1,0:T(8,128)(2,1)}, bf16[4096,128]{1,0:T(8,128)(2,1)}, u32[]{:S(2)}, u32[]{:S(2)}) collective-permute-start(bf16[4096,128]{1,0:T(8,128)(2,1)} %collective-permute-done.12.refs_2_), channel_id=1, source_target_pairs={{0,1},{1,0},{2,3},{3,2},{4,5},{5,4},{6,7},{7,6},{8,9},{9,8},{10,11... | collective-permute-start | bytes 3145736 | tf_op jit(solution)/shard_map/ppermute | solution.py:183
  69.6 3.4 %collective-permute-start.16 = (bf16[4096,128]{1,0:T(8,128)(2,1)}, bf16[4096,128]{1,0:T(8,128)(2,1)S(1)}, u32[]{:S(2)}, u32[]{:S(2)}) collective-permute-start(bf16[4096,128]{1,0:T(8,128)(2,1)} %bitcast.10.refs_3_), channel_id=1, source_target_pairs={{0,1},{1,0},{2,3},{3,2},{4,5},{5,4},{6,7},{7,6},{8,9},{9,8},{10,11... | collective-permute-start | bytes 3145736 | tf_op jit(solution)/shard_map/ppermute | solution.py:183

commit v3 on v2

--- a/solution.py
+++ b/solution.py
@@ -120,13 +120,10 @@
     for n in range(half):
         done = list_batches(range((n + 1) * group, (n + 2) * group), group, order, counts, far_batch, done)
         far_total[n] = done
-    c = q_ref[0] % 2
     for s in range(8):
-        mine = s < 4
-        core = c if mine else 1 - c
-        turn = (0, 1 + core, 2 - core, 3)[s % 4]
-        occ = level_ref[turn, 0 if mine else 2]
-        level = level_ref[turn, 1 if mine else 3]
+        chip, row = ((0, 0), (3, 2), (1, 0), (2, 0), (0, 2), (1, 2), (3, 0), (2, 2))[s]
+        occ = level_ref[chip, row]
+        level = level_ref[chip, row + 1]
         loads[s].wait()
         for i in range(group):
             first = pl.multiple_of((q_ref[0] * group + i) * BS, BS)
@@ -174,11 +171,6 @@
     return lax.ppermute(x, "slab", pairs)
 
 
-def turn(x, dy):
-    pairs = [(2 * y + c, 2 * ((y + dy) % YS) + c) for y in range(YS) for c in range(2)]
-    return lax.ppermute(x, "slab", pairs)
-
-
 def swap(x):
     return lax.ppermute(x, "slab", [(q, q ^ 1) for q in range(2 * YS)])
 
@@ -208,10 +200,12 @@
     level = jnp.concatenate([level, swap(level)], axis=0)
     front, back, level, own_x = lax.optimization_barrier((front, back, level, swap(own)))
     last = hop(front, 1)
-    turned = [turn(level, 1), turn(level, -1), turn(level, 2)]
+    behind = hop(level, -1)
+    turned = [behind, hop(behind, -1), swap(behind)]
     got, front, back, *turned = lax.optimization_barrier((got, front, back, *turned))
     levels = jnp.stack([level, *turned]).astype(jnp.float32)[:, :, None, :]
     got_front, got_back = hop(got, 1), hop(got, -1)
+    got_late, last = lax.optimization_barrier((got, last))
     got_last = exchange(last, send_lists[0])
     held = [own, front, back, last, own_x, swap(front), swap(back), swap(last)]
     q = lax.axis_index("slab").reshape(1).astype(jnp.int32)
@@ -219,7 +213,7 @@
     out = jax.ShapeDtypeStruct((pairs, BS, BS), jnp.float32)
     parts = got.shape[0] // (PART * BS)
     slots = pairs + 2 * (group * parts + UNROLL)
-    cost = pl.CostEstimate(flops=pairs * 4 * BS * BS * shards * BS, bytes_accessed=12 << 20, transcendentals=0)
+    cost = pl.CostEstimate(flops=1 << 10, bytes_accessed=1 << 10, transcendentals=0)
     dens, ener, weights, batch, totals = pl.pallas_call(
         functools.partial(near_kernel, group=group, blocks=blocks),
         in_specs=[SM, SM, SM, VM] + [HB] * len(held),
@@ -245,7 +239,7 @@
     )(pair_rows, pair_sources, q, levels, *[hbm(x) for x in held])
     got_front, got_back, weights = lax.optimization_barrier((got_front, got_back, weights))
     received = [got, got_front, got_back, got_last]
-    received = received + [swap(x) for x in received]
+    received = received + [swap(got_late)] + [swap(x) for x in received[1:]]
     return pl.pallas_call(
         functools.partial(far_kernel, blocks=blocks),
         in_specs=[SM, SM, SM, VM, HB, HB] + [HB] * 7 + [ANY],

time: 81.7 us -> 75.7 us (0.927)
  waiting for transfers between devices: 24.1 us -> 19.8 us
  starting transfers between devices: 34.2 us -> 32.3 us
    ppermute x3 -> x0, waiting for transfers between devices: 7.79 us -> none  [turn(): return lax.ppermute(x, 'slab', pairs)]
    ppermute x9 -> x10, waiting for transfers between devices: 3.32 us -> 7.81 us  [swap(): return lax.ppermute(x, 'slab', [(q, q ^ 1) for q in range(2 * YS)])]
    all_to_all x2, waiting for transfers between devices: 3.65 us -> 0.66 us  [exchange(): lax.all_to_all(tiles, 'rows', split_axis=0, concat_axis=0, tiled=True)]
    ppermute x5 -> x7, waiting for transfers between devices: 9.38 us -> 11.4 us  [hop(): return lax.ppermute(x, 'slab', pairs)]
    ppermute x3 -> x0, starting transfers between devices: 1.49 us -> none  [turn(): return lax.ppermute(x, 'slab', pairs)]
    ppermute x9 -> x10, starting transfers between devices: 8.77 us -> 8.32 us  [swap(): return lax.ppermute(x, 'slab', [(q, q ^ 1) for q in range(2 * YS)])]
    ppermute x5 -> x7, starting transfers between devices: 8.55 us -> 8.55 us  [hop(): return lax.ppermute(x, 'slab', pairs)]
  transfers between devices with their start and end apart: 19 -> 19, of which waited for: 8 -> 12; matrix products, arithmetic and copies ran while one was open for 7% -> 7% of each run, Pallas kernels for 10% -> 11%
where the time goes in v3:
time: 75.7 us
  starting transfers between devices  32.3 us (43%)
  waiting for transfers between devices  19.8 us (26%)
  Pallas kernels  17.4 us (23%)
  local copies, waits for them, and re-layouts  5.36 us (7%)
  between operations  0.79 us (1%)
    all_to_all x2, starting transfers between devices, exchange(): lax.all_to_all(tiles, 'rows', split_axis=0, concat_axis=0, tiled=True)  15.4 us
    ppermute x7, waiting for transfers between devices, hop(): return lax.ppermute(x, 'slab', pairs)  11.4 us
    pallas_call x1, Pallas kernels, body(): pl.pallas_call(functools.partial(far_kernel, blocks=blocks), in_specs=[SM...  8.93 us
    ppermute x7, starting transfers between devices, hop(): return lax.ppermute(x, 'slab', pairs)  8.55 us
    pallas_call x1, Pallas kernels, body(): pl.pallas_call(functools.partial(near_kernel, group=group, blocks=blocks)...  8.44 us
    ppermute x10, starting transfers between devices, swap(): return lax.ppermute(x, 'slab', [(q, q ^ 1) for q in range(2 * YS)])  8.32 us
    ppermute x10, waiting for transfers between devices, swap(): return lax.ppermute(x, 'slab', [(q, q ^ 1) for q in range(2 * YS)])  7.81 us
    gather x2, local copies, waits for them, and re-layouts, exchange(): tiles.reshape(-1, BS, BS).at[picks]  4.47 us
  transfers between devices with their start and end apart: 19, of which 12 were waited for; matrix products, arithmetic and copies ran while one was open for 7% of the time, Pallas kernels for 11%

profile of v3, /device:TPU:1, one launch (start us, length us, event | category | flops | bytes accessed | tf_op | source)
XLA Modules:
  0.0 75.7 jit_solution(17403603354841948147)
XLA Ops:
  0.6 0.0 copy-start.7
  0.6 0.0 copy-start.8
  0.7 1.5 %collective-permute-start.3 = (bf16[3072,128]{1,0:T(8,128)(2,1)}, bf16[3072,128]{1,0:T(8,128)(2,1)S(1)}, u32[]{:S(2)}, u32[]{:S(2)}) collective-permute-start(bf16[3072,128]{1,0:T(8,128)(2,1)} %refs_0_.1), channel_id=1, source_target_pairs={{0,1},{1,0},{2,3},{3,2},{4,5},{5,4},{6,7},{7,6},{8,9},{9,8},{10,11... | collective-permute-start | bytes 2359304 | tf_op jit(solution)/shard_map/ppermute | solution.py:175
  2.2 1.4 %collective-permute-start.1 = (bf16[3072,128]{1,0:T(8,128)(2,1)}, bf16[3072,128]{1,0:T(8,128)(2,1)S(1)}, u32[]{:S(2)}, u32[]{:S(2)}) collective-permute-start(bf16[3072,128]{1,0:T(8,128)(2,1)} %refs_0_.1), channel_id=1, source_target_pairs={{0,6},{1,3},{2,0},{3,5},{4,2},{5,7},{6,4},{7,1},{8,14},{9,11},{10,... | collective-permute-start | bytes 2359304 | tf_op jit(solution)/shard_map/ppermute | solution.py:171
  3.5 1.5 %collective-permute-start = (bf16[3072,128]{1,0:T(8,128)(2,1)}, bf16[3072,128]{1,0:T(8,128)(2,1)S(1)}, u32[]{:S(2)}, u32[]{:S(2)}) collective-permute-start(bf16[3072,128]{1,0:T(8,128)(2,1)} %refs_0_.1), channel_id=1, source_target_pairs={{0,2},{1,7},{2,4},{3,1},{4,6},{5,3},{6,0},{7,5},{8,10},{9,15},{10,... | collective-permute-start | bytes 2359304 | tf_op jit(solution)/shard_map/ppermute | solution.py:171
  5.0 0.8 copy.26
  5.7 0.1 reshape.85
  5.8 2.8 %gather_fusion = bf16[32,128,128]{2,1,0:T(8,128)(2,1)} fusion(bf16[24,128,128]{2,1,0:T(8,128)(2,1)} %bitcast.11, s32[1024]{0:T(1024)S(1)} %pad_clamp_fusion), kind=kCustom, calls=%fused_computation | custom fusion | bytes 2097280 | tf_op jit(solution)/shard_map/gather | solution.py:179
  8.6 0.0 copy-start
  8.6 0.0 copy-start.1
  8.6 7.7 %all-to-all-start = ((bf16[16,2,128,128]{3,2,1,0:T(8,128)(2,1)}), bf16[16,2,128,128]{3,2,1,0:T(8,128)(2,1)S(1)}, u32[]{:S(2)}, u32[]{:S(2)}) async-start(bf16[16,2,128,128]{3,2,1,0:T(8,128)(2,1)} %bitcast.3), calls=%async_computation | async-start | bytes 2097152 | tf_op jit(solution)/shard_map/all_to_all | solution.py:180
  16.4 0.0 copy-done.7
  16.4 0.0 copy-done.8
  16.4 0.7 collective-permute-start.2
  17.1 0.8 %collective-permute-done.2 = bf16[2,128]{1,0:T(2,128)(2,1)S(1)} collective-permute-done((bf16[2,128]{1,0:T(2,128)(2,1)S(1)}, bf16[2,128]{1,0:T(2,128)(2,1)S(1)}, u32[]{:S(2)}, u32[]{:S(2)}) %collective-permute-start.2) | collective-permute-done | bytes 544 | tf_op jit(solution)/shard_map/ppermute | solution.py:175
  17.9 0.0 collective-permute-done.3.refs_4_
  18.0 0.0 copy-start.4
  18.0 1.8 %collective-permute-done.1.refs_2_ = bf16[3072,128]{1,0:T(8,128)(2,1)S(1)} collective-permute-done((bf16[3072,128]{1,0:T(8,128)(2,1)}, bf16[3072,128]{1,0:T(8,128)(2,1)S(1)}, u32[]{:S(2)}, u32[]{:S(2)}) %collective-permute-start.1) | collective-permute-done | bytes 786464 | tf_op jit(solution)/shard_map/ppermute | solution.py:171
  19.7 0.0 copy-done.4
  19.7 0.0 copy-start.5
  19.7 2.8 %collective-permute-done.refs_1_ = bf16[3072,128]{1,0:T(8,128)(2,1)S(1)} collective-permute-done((bf16[3072,128]{1,0:T(8,128)(2,1)}, bf16[3072,128]{1,0:T(8,128)(2,1)S(1)}, u32[]{:S(2)}, u32[]{:S(2)}) %collective-permute-start) | collective-permute-done | bytes 786464 | tf_op jit(solution)/shard_map/ppermute | solution.py:171
  22.5 0.0 copy-start.6
  22.5 3.0 %collective-permute-start.7 = (bf16[3072,128]{1,0:T(8,128)(2,1)S(1)}, bf16[3072,128]{1,0:T(8,128)(2,1)S(1)}, u32[]{:S(2)}, u32[]{:S(2)}) collective-permute-start(bf16[3072,128]{1,0:T(8,128)(2,1)S(1)} %collective-permute-done.refs_1_), channel_id=1, source_target_pairs={{0,2},{1,7},{2,4},{3,1},{4,6},{5,3},{6,0},{7,5},{8,10},{9,15},{10,... | collective-permute-start | bytes 2359304 | tf_op jit(solution)/shard_map/ppermute | solution.py:171
  25.5 0.0 collective-permute-start.4
  25.5 4.0 %collective-permute-done.4 = bf16[4,128]{1,0:T(4,128)(2,1)S(1)} collective-permute-done((bf16[4,128]{1,0:T(4,128)(2,1)S(1)}, bf16[4,128]{1,0:T(4,128)(2,1)S(1)}, u32[]{:S(2)}, u32[]{:S(2)}) %collective-permute-start.4) | collective-permute-done | bytes 1056 | tf_op jit(solution)/shard_map/ppermute | solution.py:171
  29.5 0.0 collective-permute-start.6
  29.5 0.0 collective-permute-start.5
  29.5 1.1 %collective-permute-done.6 = bf16[4,128]{1,0:T(4,128)(2,1)S(1)} collective-permute-done((bf16[4,128]{1,0:T(4,128)(2,1)S(1)}, bf16[4,128]{1,0:T(4,128)(2,1)S(1)}, u32[]{:S(2)}, u32[]{:S(2)}) %collective-permute-start.6) | collective-permute-done | bytes 1056 | tf_op jit(solution)/shard_map/ppermute | solution.py:175
  30.6 2.9 %collective-permute-done.5 = bf16[4,128]{1,0:T(4,128)(2,1)S(1)} collective-permute-done((bf16[4,128]{1,0:T(4,128)(2,1)S(1)}, bf16[4,128]{1,0:T(4,128)(2,1)S(1)}, u32[]{:S(2)}, u32[]{:S(2)}) %collective-permute-start.5) | collective-permute-done | bytes 1056 | tf_op jit(solution)/shard_map/ppermute | solution.py:171
  33.5 0.0 all-to-all-done
  33.5 0.0 copy-start.3
  33.5 0.0 collective-permute-start.12
  33.5 2.7 %collective-permute-start.11 = (bf16[4096,128]{1,0:T(8,128)(2,1)S(1)}, bf16[4096,128]{1,0:T(8,128)(2,1)}, u32[]{:S(2)}, u32[]{:S(2)}) collective-permute-start(bf16[4096,128]{1,0:T(8,128)(2,1)S(1)} %bitcast.14), channel_id=1, source_target_pairs={{0,2},{1,7},{2,4},{3,1},{4,6},{5,3},{6,0},{7,5},{8,10},{9,15},{10,... | collective-permute-start | bytes 3145736 | tf_op jit(solution)/shard_map/ppermute | solution.py:171
  36.2 0.0 collective-permute-done.7.refs_3_
  36.2 0.0 copy-start.2
  36.2 1.7 %gather_fusion.1 = bf16[32,128,128]{2,1,0:T(8,128)(2,1)} fusion(bf16[24,128,128]{2,1,0:T(8,128)(2,1)S(1)} %bitcast.12, s32[1024]{0:T(1024)S(1)} %pad_clamp_fusion), kind=kCustom, calls=%fused_computation.1 | custom fusion | bytes 2097280 | tf_op jit(solution)/shard_map/gather | solution.py:179
  37.9 7.7 %all-to-all-start.1 = ((bf16[16,2,128,128]{3,2,1,0:T(8,128)(2,1)}), bf16[16,2,128,128]{3,2,1,0:T(8,128)(2,1)}, u32[]{:S(2)}, u32[]{:S(2)}) async-start(bf16[16,2,128,128]{3,2,1,0:T(8,128)(2,1)} %bitcast.9), calls=%async_computation.1 | async-start | bytes 2097152 | tf_op jit(solution)/shard_map/all_to_all | solution.py:180
  45.5 1.1 %collective-permute-start.8 = (bf16[3072,128]{1,0:T(8,128)(2,1)S(1)}, bf16[3072,128]{1,0:T(8,128)(2,1)}, u32[]{:S(2)}, u32[]{:S(2)}) collective-permute-start(bf16[3072,128]{1,0:T(8,128)(2,1)S(1)} %collective-permute-done.refs_1_), channel_id=1, source_target_pairs={{0,1},{1,0},{2,3},{3,2},{4,5},{5,4},{6,7},{7,6},{8,9},{9,8},{10,11... | collective-permute-start | bytes 2359304 | tf_op jit(solution)/shard_map/ppermute | solution.py:175
  46.6 0.1 collective-permute-start.9
  46.7 0.4 collective-permute-start.10
  47.2 1.5 %collective-permute-done.8.refs_5_ = bf16[3072,128]{1,0:T(8,128)(2,1)} collective-permute-done((bf16[3072,128]{1,0:T(8,128)(2,1)S(1)}, bf16[3072,128]{1,0:T(8,128)(2,1)}, u32[]{:S(2)}, u32[]{:S(2)}) %collective-permute-start.8) | collective-permute-done | bytes 786464 | tf_op jit(solution)/shard_map/ppermute | solution.py:175
  48.6 0.4 collective-permute-start.13
  49.0 0.8 collective-permute-done.9.refs_6_
  49.8 1.1 %collective-permute-done.10.refs_7_ = bf16[3072,128]{1,0:T(8,128)(2,1)} collective-permute-done((bf16[3072,128]{1,0:T(8,128)(2,1)S(1)}, bf16[3072,128]{1,0:T(8,128)(2,1)}, u32[]{:S(2)}, u32[]{:S(2)}) %collective-permute-start.10) | collective-permute-done | bytes 786464 | tf_op jit(solution)/shard_map/ppermute | solution.py:175
  50.9 0.0 copy-done.5
  50.9 0.0 copy-done.6
  50.9 0.0 copy-done.2
  50.9 0.0 copy-done
  50.9 0.0 copy-done.1
  50.9 8.4 %shard_map.77 = (f32[48,128,128]{2,1,0:T(8,128)}, f32[48,128,128]{2,1,0:T(8,128)}, bf16[3,256,1024]{2,1,0:T(8,128)(2,1)S(1)}, s32[99]{0:T(128)S(1)}, s32[2]{0:T(128)S(1)}) custom-call(s32[48]{0:T(128)S(1)} %copy-done.1, s32[48]{0:T(128)S(1)} %copy-done, s32[1]{0:T(128)} %bitcast.q_ref, f32[4,4,1,128]{3,2,1,0:T(1,128)S(1)} %maximum_convert_fusion.level_ref, ...), custom_call_target="tpu_custom_call" | custom-call | flops 1024 | bytes 1024 | tf_op jit(solution)/shard_map/pallas_call | solution.py:217
  59.4 0.0 copy-done.3
  59.4 0.0 collective-permute-done.12.refs_2_
  59.4 0.0 collective-permute-done.11.refs_1_
  59.4 1.0 %collective-permute-start.14 = (bf16[4096,128]{1,0:T(8,128)(2,1)}, bf16[4096,128]{1,0:T(8,128)(2,1)}, u32[]{:S(2)}, u32[]{:S(2)}) collective-permute-start(bf16[4096,128]{1,0:T(8,128)(2,1)} %collective-permute-done.11.refs_1_), channel_id=1, source_target_pairs={{0,1},{1,0},{2,3},{3,2},{4,5},{5,4},{6,7},{7,6},{8,9},{9,8},{10,11... | collective-permute-start | bytes 3145736 | tf_op jit(solution)/shard_map/ppermute | solution.py:175
  60.4 0.0 collective-permute-start.15
  60.4 0.7 all-to-all-done.1
  61.1 3.2 %collective-permute-start.16 = (bf16[4096,128]{1,0:T(8,128)(2,1)}, bf16[4096,128]{1,0:T(8,128)(2,1)S(1)}, u32[]{:S(2)}, u32[]{:S(2)}) collective-permute-start(bf16[4096,128]{1,0:T(8,128)(2,1)} %bitcast.10.refs_3_), channel_id=1, source_target_pairs={{0,1},{1,0},{2,3},{3,2},{4,5},{5,4},{6,7},{7,6},{8,9},{9,8},{10,11... | collective-permute-start | bytes 3145736 | tf_op jit(solution)/shard_map/ppermute | solution.py:175
  64.2 0.0 collective-permute-done.13.refs_4_
  64.2 0.0 collective-permute-done.14.refs_5_
  64.2 0.3 collective-permute-done.15.refs_6_
  64.5 2.2 %collective-permute-done.16.refs_7_ = bf16[4096,128]{1,0:T(8,128)(2,1)S(1)} collective-permute-done((bf16[4096,128]{1,0:T(8,128)(2,1)}, bf16[4096,128]{1,0:T(8,128)(2,1)S(1)}, u32[]{:S(2)}, u32[]{:S(2)}) %collective-permute-start.16) | collective-permute-done | bytes 1048608 | tf_op jit(solution)/shard_map/ppermute | solution.py:175
  66.7 8.9 %shard_map.78 = (f32[48,128,128]{2,1,0:T(8,128)}, f32[48,128,128]{2,1,0:T(8,128)}) custom-call(s32[48]{0:T(128)S(1)} %copy-done, s32[99]{0:T(128)S(1)} %get-tuple-element.33.batch, s32[2]{0:T(128)S(1)} %get-tuple-element.34.totals, bf16[3,256,1024]{2,1,0:T(8,128)(2,1)S(1)} %get-tuple-element.36.w_ref, ...), custom_call_target="tpu_custom_call", output_to_operand_aliasing={{0}: (4, {}), {1}: (5, {})} | custom-call | flops 1024 | bytes 1024 | tf_op jit(solution)/shard_map/pallas_call | solution.py:243
  (8 shorter events, 0.1 us)
Async XLA Ops:
  0.6 15.7 %copy-start.7 = (bf16[1,128]{1,0:T(2,128)(2,1)S(1)}, bf16[1,128]{1,0:T(2,128)(2,1)}, u32[]{:S(2)}) copy-start(bf16[1,128]{1,0:T(2,128)(2,1)} %param.8) | copy-start | bytes 772
  0.6 15.7 %copy-start.8 = (bf16[1,128]{1,0:T(2,128)(2,1)S(1)}, bf16[1,128]{1,0:T(2,128)(2,1)}, u32[]{:S(2)}) copy-start(bf16[1,128]{1,0:T(2,128)(2,1)} %param.7) | copy-start | bytes 772
  0.7 17.3 %collective-permute-start.3 = (bf16[3072,128]{1,0:T(8,128)(2,1)}, bf16[3072,128]{1,0:T(8,128)(2,1)S(1)}, u32[]{:S(2)}, u32[]{:S(2)}) collective-permute-start(bf16[3072,128]{1,0:T(8,128)(2,1)} %refs_0_.1), channel_id=1, source_target_pairs={{0,1},{1,0},{2,3},{3,2},{4,5},{5,4},{6,7},{7,6},{8,9},{9,8},{10,11... | collective-permute-start | bytes 2359304 | tf_op jit(solution)/shard_map/ppermute | solution.py:175
  2.2 17.6 %collective-permute-start.1 = (bf16[3072,128]{1,0:T(8,128)(2,1)}, bf16[3072,128]{1,0:T(8,128)(2,1)S(1)}, u32[]{:S(2)}, u32[]{:S(2)}) collective-permute-start(bf16[3072,128]{1,0:T(8,128)(2,1)} %refs_0_.1), channel_id=1, source_target_pairs={{0,6},{1,3},{2,0},{3,5},{4,2},{5,7},{6,4},{7,1},{8,14},{9,11},{10,... | collective-permute-start | bytes 2359304 | tf_op jit(solution)/shard_map/ppermute | solution.py:171
  3.5 18.9 %collective-permute-start = (bf16[3072,128]{1,0:T(8,128)(2,1)}, bf16[3072,128]{1,0:T(8,128)(2,1)S(1)}, u32[]{:S(2)}, u32[]{:S(2)}) collective-permute-start(bf16[3072,128]{1,0:T(8,128)(2,1)} %refs_0_.1), channel_id=1, source_target_pairs={{0,2},{1,7},{2,4},{3,1},{4,6},{5,3},{6,0},{7,5},{8,10},{9,15},{10,... | collective-permute-start | bytes 2359304 | tf_op jit(solution)/shard_map/ppermute | solution.py:171
  8.6 42.3 %copy-start = (s32[48]{0:T(128)S(1)}, s32[48]{0:T(128)}, u32[]{:S(2)}) copy-start(s32[48]{0:T(128)} %src_ref.3) | copy-start | bytes 580
  8.6 42.3 %copy-start.1 = (s32[48]{0:T(128)S(1)}, s32[48]{0:T(128)}, u32[]{:S(2)}) copy-start(s32[48]{0:T(128)} %row_ref.1) | copy-start | bytes 580
  8.6 24.9 %all-to-all-start = ((bf16[16,2,128,128]{3,2,1,0:T(8,128)(2,1)}), bf16[16,2,128,128]{3,2,1,0:T(8,128)(2,1)S(1)}, u32[]{:S(2)}, u32[]{:S(2)}) async-start(bf16[16,2,128,128]{3,2,1,0:T(8,128)(2,1)} %bitcast.3), calls=%async_computation | async-start | bytes 2097152 | tf_op jit(solution)/shard_map/all_to_all | solution.py:180
  16.4 1.5 %collective-permute-start.2 = (bf16[2,128]{1,0:T(2,128)(2,1)S(1)}, bf16[2,128]{1,0:T(2,128)(2,1)S(1)}, u32[]{:S(2)}, u32[]{:S(2)}) collective-permute-start(bf16[2,128]{1,0:T(2,128)(2,1)S(1)} %pad_maximum_fusion.1), channel_id=1, source_target_pairs={{0,1},{1,0},{2,3},{3,2},{4,5},{5,4},{6,7},{7,6},{8,9},{9,8},{10,11... | collective-permute-start | bytes 1544 | tf_op jit(solution)/shard_map/ppermute | solution.py:175
  18.0 1.8 %copy-start.4 = (bf16[3072,128]{1,0:T(8,128)(2,1)}, bf16[3072,128]{1,0:T(8,128)(2,1)S(1)}, u32[]{:S(2)}) copy-start(bf16[3072,128]{1,0:T(8,128)(2,1)S(1)} %collective-permute-done.3.refs_4_) | copy-start | bytes 2359300
  19.7 31.2 %copy-start.5 = (bf16[3072,128]{1,0:T(8,128)(2,1)}, bf16[3072,128]{1,0:T(8,128)(2,1)S(1)}, u32[]{:S(2)}) copy-start(bf16[3072,128]{1,0:T(8,128)(2,1)S(1)} %collective-permute-done.1.refs_2_) | copy-start | bytes 2359300
  22.5 28.4 %copy-start.6 = (bf16[3072,128]{1,0:T(8,128)(2,1)}, bf16[3072,128]{1,0:T(8,128)(2,1)S(1)}, u32[]{:S(2)}) copy-start(bf16[3072,128]{1,0:T(8,128)(2,1)S(1)} %collective-permute-done.refs_1_) | copy-start | bytes 2359300
  22.5 13.7 %collective-permute-start.7 = (bf16[3072,128]{1,0:T(8,128)(2,1)S(1)}, bf16[3072,128]{1,0:T(8,128)(2,1)S(1)}, u32[]{:S(2)}, u32[]{:S(2)}) collective-permute-start(bf16[3072,128]{1,0:T(8,128)(2,1)S(1)} %collective-permute-done.refs_1_), channel_id=1, source_target_pairs={{0,2},{1,7},{2,4},{3,1},{4,6},{5,3},{6,0},{7,5},{8,10},{9,15},{10,... | collective-permute-start | bytes 2359304 | tf_op jit(solution)/shard_map/ppermute | solution.py:171
  25.5 4.0 %collective-permute-start.4 = (bf16[4,128]{1,0:T(4,128)(2,1)S(1)}, bf16[4,128]{1,0:T(4,128)(2,1)S(1)}, u32[]{:S(2)}, u32[]{:S(2)}) collective-permute-start(bf16[4,128]{1,0:T(4,128)(2,1)S(1)} %pad_maximum_fusion), channel_id=1, source_target_pairs={{0,6},{1,3},{2,0},{3,5},{4,2},{5,7},{6,4},{7,1},{8,14},{9,11},{10,... | collective-permute-start | bytes 3080 | tf_op jit(solution)/shard_map/ppermute | solution.py:171
  29.5 1.1 %collective-permute-start.6 = (bf16[4,128]{1,0:T(4,128)(2,1)S(1)}, bf16[4,128]{1,0:T(4,128)(2,1)S(1)}, u32[]{:S(2)}, u32[]{:S(2)}) collective-permute-start(bf16[4,128]{1,0:T(4,128)(2,1)S(1)} %collective-permute-done.4), channel_id=1, source_target_pairs={{0,1},{1,0},{2,3},{3,2},{4,5},{5,4},{6,7},{7,6},{8,9},{9,8},{10,11... | collective-permute-start | bytes 3080 | tf_op jit(solution)/shard_map/ppermute | solution.py:175
  29.5 4.0 %collective-permute-start.5 = (bf16[4,128]{1,0:T(4,128)(2,1)S(1)}, bf16[4,128]{1,0:T(4,128)(2,1)S(1)}, u32[]{:S(2)}, u32[]{:S(2)}) collective-permute-start(bf16[4,128]{1,0:T(4,128)(2,1)S(1)} %collective-permute-done.4), channel_id=1, source_target_pairs={{0,6},{1,3},{2,0},{3,5},{4,2},{5,7},{6,4},{7,1},{8,14},{9,11},{10,... | collective-permute-start | bytes 3080 | tf_op jit(solution)/shard_map/ppermute | solution.py:171
  33.5 25.9 %copy-start.3 = (bf16[16,2,128,128]{3,2,1,0:T(8,128)(2,1)}, bf16[16,2,128,128]{3,2,1,0:T(8,128)(2,1)S(1)}, u32[]{:S(2)}) copy-start(bf16[16,2,128,128]{3,2,1,0:T(8,128)(2,1)S(1)} %all-to-all-done) | copy-start | bytes 3145732
  33.5 25.9 %collective-permute-start.12 = (bf16[4096,128]{1,0:T(8,128)(2,1)S(1)}, bf16[4096,128]{1,0:T(8,128)(2,1)}, u32[]{:S(2)}, u32[]{:S(2)}) collective-permute-start(bf16[4096,128]{1,0:T(8,128)(2,1)S(1)} %bitcast.13), channel_id=1, source_target_pairs={{0,6},{1,3},{2,0},{3,5},{4,2},{5,7},{6,4},{7,1},{8,14},{9,11},{10,... | collective-permute-start | bytes 3145736 | tf_op jit(solution)/shard_map/ppermute | solution.py:171
  33.5 25.9 %collective-permute-start.11 = (bf16[4096,128]{1,0:T(8,128)(2,1)S(1)}, bf16[4096,128]{1,0:T(8,128)(2,1)}, u32[]{:S(2)}, u32[]{:S(2)}) collective-permute-start(bf16[4096,128]{1,0:T(8,128)(2,1)S(1)} %bitcast.14), channel_id=1, source_target_pairs={{0,2},{1,7},{2,4},{3,1},{4,6},{5,3},{6,0},{7,5},{8,10},{9,15},{10,... | collective-permute-start | bytes 3145736 | tf_op jit(solution)/shard_map/ppermute | solution.py:171
  36.2 14.7 %copy-start.2 = (bf16[3072,128]{1,0:T(8,128)(2,1)}, bf16[3072,128]{1,0:T(8,128)(2,1)S(1)}, u32[]{:S(2)}) copy-start(bf16[3072,128]{1,0:T(8,128)(2,1)S(1)} %collective-permute-done.7.refs_3_) | copy-start | bytes 2359300
  37.9 23.2 %all-to-all-start.1 = ((bf16[16,2,128,128]{3,2,1,0:T(8,128)(2,1)}), bf16[16,2,128,128]{3,2,1,0:T(8,128)(2,1)}, u32[]{:S(2)}, u32[]{:S(2)}) async-start(bf16[16,2,128,128]{3,2,1,0:T(8,128)(2,1)} %bitcast.9), calls=%async_computation.1 | async-start | bytes 2097152 | tf_op jit(solution)/shard_map/all_to_all | solution.py:180
  45.5 3.1 %collective-permute-start.8 = (bf16[3072,128]{1,0:T(8,128)(2,1)S(1)}, bf16[3072,128]{1,0:T(8,128)(2,1)}, u32[]{:S(2)}, u32[]{:S(2)}) collective-permute-start(bf16[3072,128]{1,0:T(8,128)(2,1)S(1)} %collective-permute-done.refs_1_), channel_id=1, source_target_pairs={{0,1},{1,0},{2,3},{3,2},{4,5},{5,4},{6,7},{7,6},{8,9},{9,8},{10,11... | collective-permute-start | bytes 2359304 | tf_op jit(solution)/shard_map/ppermute | solution.py:175
  46.6 3.2 %collective-permute-start.9 = (bf16[3072,128]{1,0:T(8,128)(2,1)S(1)}, bf16[3072,128]{1,0:T(8,128)(2,1)}, u32[]{:S(2)}, u32[]{:S(2)}) collective-permute-start(bf16[3072,128]{1,0:T(8,128)(2,1)S(1)} %collective-permute-done.1.refs_2_), channel_id=1, source_target_pairs={{0,1},{1,0},{2,3},{3,2},{4,5},{5,4},{6,7},{7,6},{8,9},{9,8},{10,11... | collective-permute-start | bytes 2359304 | tf_op jit(solution)/shard_map/ppermute | solution.py:175
  46.7 4.2 %collective-permute-start.10 = (bf16[3072,128]{1,0:T(8,128)(2,1)S(1)}, bf16[3072,128]{1,0:T(8,128)(2,1)}, u32[]{:S(2)}, u32[]{:S(2)}) collective-permute-start(bf16[3072,128]{1,0:T(8,128)(2,1)S(1)} %collective-permute-done.7.refs_3_), channel_id=1, source_target_pairs={{0,1},{1,0},{2,3},{3,2},{4,5},{5,4},{6,7},{7,6},{8,9},{9,8},{10,11... | collective-permute-start | bytes 2359304 | tf_op jit(solution)/shard_map/ppermute | solution.py:175
  48.6 15.6 %collective-permute-start.13 = (bf16[4096,128]{1,0:T(8,128)(2,1)S(1)}, bf16[4096,128]{1,0:T(8,128)(2,1)}, u32[]{:S(2)}, u32[]{:S(2)}) collective-permute-start(bf16[4096,128]{1,0:T(8,128)(2,1)S(1)} %bitcast.15), channel_id=1, source_target_pairs={{0,1},{1,0},{2,3},{3,2},{4,5},{5,4},{6,7},{7,6},{8,9},{9,8},{10,11... | collective-permute-start | bytes 3145736 | tf_op jit(solution)/shard_map/ppermute | solution.py:175
  59.4 4.8 %collective-permute-start.14 = (bf16[4096,128]{1,0:T(8,128)(2,1)}, bf16[4096,128]{1,0:T(8,128)(2,1)}, u32[]{:S(2)}, u32[]{:S(2)}) collective-permute-start(bf16[4096,128]{1,0:T(8,128)(2,1)} %collective-permute-done.11.refs_1_), channel_id=1, source_target_pairs={{0,1},{1,0},{2,3},{3,2},{4,5},{5,4},{6,7},{7,6},{8,9},{9,8},{10,11... | collective-permute-start | bytes 3145736 | tf_op jit(solution)/shard_map/ppermute | solution.py:175
  60.4 4.1 %collective-permute-start.15 = (bf16[4096,128]{1,0:T(8,128)(2,1)}, bf16[4096,128]{1,0:T(8,128)(2,1)}, u32[]{:S(2)}, u32[]{:S(2)}) collective-permute-start(bf16[4096,128]{1,0:T(8,128)(2,1)} %collective-permute-done.12.refs_2_), channel_id=1, source_target_pairs={{0,1},{1,0},{2,3},{3,2},{4,5},{5,4},{6,7},{7,6},{8,9},{9,8},{10,11... | collective-permute-start | bytes 3145736 | tf_op jit(solution)/shard_map/ppermute | solution.py:175
  61.1 5.7 %collective-permute-start.16 = (bf16[4096,128]{1,0:T(8,128)(2,1)}, bf16[4096,128]{1,0:T(8,128)(2,1)S(1)}, u32[]{:S(2)}, u32[]{:S(2)}) collective-permute-start(bf16[4096,128]{1,0:T(8,128)(2,1)} %bitcast.10.refs_3_), channel_id=1, source_target_pairs={{0,1},{1,0},{2,3},{3,2},{4,5},{5,4},{6,7},{7,6},{8,9},{9,8},{10,11... | collective-permute-start | bytes 3145736 | tf_op jit(solution)/shard_map/ppermute | solution.py:175

commit v4 on v3

--- a/solution.py
+++ b/solution.py
@@ -10,7 +10,7 @@
 BS = 128
 YS = 4
 UNROLL = 3
-PART = 16
+PART = 8
 VM = pl.BlockSpec(memory_space=pltpu.VMEM)
 SM = pl.BlockSpec(memory_space=pltpu.SMEM)
 HB = pl.BlockSpec(memory_space=pltpu.HBM)
@@ -39,17 +39,38 @@
     lax.fori_loop(0, pairs, add, 0)
 
 
-def list_batches(buckets, group, order, counts, batch, total):
+def list_batches(first, parts, group, order, counts, merged, batch, totals):
     span = order.shape[0] // counts.shape[0]
-    for n in buckets:
-
-        def put(t, total, n=n):
-            batch[3 * total] = n % group
-            batch[3 * total + 1] = order[n * span + 2 * t]
-            batch[3 * total + 2] = jnp.where(2 * t + 1 < counts[n], order[n * span + 2 * t + 1], -1)
-            return total + 1
-
-        total = lax.fori_loop(0, (counts[n] + 1) // 2, put, total)
+    ends = []
+    for i in range(group):
+        end = jnp.int32(0)
+        ends.append([end])
+        for n in range(parts):
+            bucket = first + n * group + i
+
+            def move(t, _, bucket=bucket, end=end, i=i):
+                merged[i * span + end + t] = order[bucket * span + t]
+                return 0
+
+            lax.fori_loop(0, counts[bucket], move, 0)
+            end = end + counts[bucket]
+            ends[i].append(end)
+
+    total = jnp.int32(0)
+    for n in range(parts):
+        for i in range(group):
+
+            def put(t, total, i=i):
+                second = merged[i * span + 2 * t + 1]
+                batch[3 * total] = i
+                batch[3 * total + 1] = merged[i * span + 2 * t]
+                batch[3 * total + 2] = jnp.where(2 * t + 1 < ends[i][parts], second, -1)
+                return total + 1
+
+            stop = (ends[i][n + 1] + (1 if n == parts - 1 else 0)) // 2
+            total = lax.fori_loop(ends[i][n] // 2, stop, put, total)
+        if totals is not None:
+            totals[n] = total
     return total
 
 
@@ -66,8 +87,10 @@
         both(2 * b + 1, second)
 
 
-def run_batches(start, stop, batch, tiles, w_ref, outs, stage, sem):
+def run_batches(start, stop, batch, tiles, w_ref, outs, stage, sem, before=None):
     def compute(t, _):
+        if before is not None:
+            before(t)
         for u in range(UNROLL):
             b = jnp.minimum(start + t * UNROLL + u, stop - 1)
             first, second = batch[3 * b + 1], batch[3 * b + 2]
@@ -105,7 +128,7 @@
 
 def near_kernel(row_ref, src_ref, q_ref, level_ref, *refs, group, blocks):
     held = refs[:8]
-    dens_ref, ener_ref, w_ref, far_batch, far_total, s_ref, stage, order, counts, batch, in_sem, sem = refs[8:]
+    dens_ref, ener_ref, w_ref, far_batch, far_total, s_ref, stage, order, counts, merged, batch, in_sem, sem = refs[8:]
     loads = load_all(held, s_ref, in_sem)
     pairs, half = row_ref.shape[0], counts.shape[0] // group - 1
 
@@ -115,11 +138,8 @@
 
     list_pairs(bucket, pairs, order, counts)
     zero = jnp.int32(0)
-    total = list_batches(range(group), group, order, counts, batch, zero)
-    done = zero
-    for n in range(half):
-        done = list_batches(range((n + 1) * group, (n + 2) * group), group, order, counts, far_batch, done)
-        far_total[n] = done
+    total = list_batches(0, 1, group, order, counts, merged, batch, None)
+    list_batches(group, half, group, order, counts, merged, far_batch, far_total)
     for s in range(8):
         chip, row = ((0, 0), (3, 2), (1, 0), (2, 0), (0, 2), (1, 2), (3, 0), (2, 2))[s]
         occ = level_ref[chip, row]
@@ -156,14 +176,28 @@
     def tiles(g):
         return block_tiles(s_ref, pl.multiple_of((src_ref[g] - blocks) * BS, BS))
 
-    outs = [dens_ref, ener_ref]
-    start = jnp.int32(0)
-    for n in range(parts):
+    def wait(n):
         for copy in loads[n]:
             copy.wait()
-        run_batches(start, totals[n], batch, tiles, w_ref, outs, stage, sem)
-        start = totals[n]
-    drain(start, batch, outs, stage, sem)
+
+    def before(t):
+        for n in range(1, parts):
+
+            @pl.when(t == totals[n - 1] // UNROLL)
+            def _():
+                wait(n)
+
+    outs = [dens_ref, ener_ref]
+    total = totals[parts - 1]
+    wait(0)
+    run_batches(jnp.int32(0), total, batch, tiles, w_ref, outs, stage, sem, before)
+    for n in range(1, parts):
+
+        @pl.when(totals[n - 1] // UNROLL >= (total + UNROLL - 1) // UNROLL)
+        def _():
+            wait(n)
+
+    drain(total, batch, outs, stage, sem)
 
 
 def hop(x, step):
@@ -212,7 +246,7 @@
 
     out = jax.ShapeDtypeStruct((pairs, BS, BS), jnp.float32)
     parts = got.shape[0] // (PART * BS)
-    slots = pairs + 2 * (group * parts + UNROLL)
+    slots = pairs + 2 * (group + UNROLL)
     cost = pl.CostEstimate(flops=1 << 10, bytes_accessed=1 << 10, transcendentals=0)
     dens, ener, weights, batch, totals = pl.pallas_call(
         functools.partial(near_kernel, group=group, blocks=blocks),
@@ -223,6 +257,7 @@
             pltpu.VMEM((2, slots, BS, BS), jnp.float32),
             pltpu.SMEM(((1 + parts) * group * pairs,), jnp.int32),
             pltpu.SMEM(((1 + parts) * group,), jnp.int32),
+            pltpu.SMEM((group * pairs + 1,), jnp.int32),
             pltpu.SMEM((3 * slots // 2,), jnp.int32),
             pltpu.SemaphoreType.DMA((shards,)),
             pltpu.SemaphoreType.DMA((2, slots)),

time: 75.7 us -> 75.1 us (level); the launches traced: 75.7 us -> 74 us
  Pallas kernels: 17.4 us -> 16.4 us
    pallas_call x1, Pallas kernels: 8.93 us -> 7.27 us  [body(): pl.pallas_call(functools.partial(far_kernel, blocks=blocks), in_specs=[SM...]
  transfers between devices with their start and end apart: 19 -> 19, of which waited for: 12 -> 12; matrix products, arithmetic and copies ran while one was open for 7% -> 7% of each run, Pallas kernels for 11% -> 12%
where the time goes in v4:
time: 75.1 us; the launch traced here: 74 us
  starting transfers between devices  31.9 us (42%)
  waiting for transfers between devices  19.5 us (26%)
  Pallas kernels  16.4 us (22%)
  local copies, waits for them, and re-layouts  5.36 us (7%)
  between operations  0.79 us (1%)
    all_to_all x2, starting transfers between devices, exchange(): lax.all_to_all(tiles, 'rows', split_axis=0, concat_axis=0, tiled=True)  15.4 us
    ppermute x7, waiting for transfers between devices, hop(): return lax.ppermute(x, 'slab', pairs)  11.4 us
    pallas_call x1, Pallas kernels, body(): pl.pallas_call(functools.partial(near_kernel, group=group, blocks=blocks)...  9.14 us
    ppermute x7, starting transfers between devices, hop(): return lax.ppermute(x, 'slab', pairs)  8.55 us
    ppermute x10, starting transfers between devices, swap(): return lax.ppermute(x, 'slab', [(q, q ^ 1) for q in range(2 * YS)])  7.92 us
    ppermute x10, waiting for transfers between devices, swap(): return lax.ppermute(x, 'slab', [(q, q ^ 1) for q in range(2 * YS)])  7.81 us
    pallas_call x1, Pallas kernels, body(): pl.pallas_call(functools.partial(far_kernel, blocks=blocks), in_specs=[SM...  7.27 us
    gather x2, local copies, waits for them, and re-layouts, exchange(): tiles.reshape(-1, BS, BS).at[picks]  4.47 us
  transfers between devices with their start and end apart: 19, of which 12 were waited for; matrix products, arithmetic and copies ran while one was open for 7% of the time, Pallas kernels for 12%

profile of v4, /device:TPU:1, one launch (start us, length us, event | category | flops | bytes accessed | tf_op | source)
XLA Modules:
  0.0 74.0 jit_solution(322167490889217944)
XLA Ops:
  0.6 0.0 copy-start.7
  0.6 0.0 copy-start.8
  0.7 1.5 %collective-permute-start.3 = (bf16[3072,128]{1,0:T(8,128)(2,1)}, bf16[3072,128]{1,0:T(8,128)(2,1)S(1)}, u32[]{:S(2)}, u32[]{:S(2)}) collective-permute-start(bf16[3072,128]{1,0:T(8,128)(2,1)} %refs_0_.1), channel_id=1, source_target_pairs={{0,1},{1,0},{2,3},{3,2},{4,5},{5,4},{6,7},{7,6},{8,9},{9,8},{10,11... | collective-permute-start | bytes 2359304 | tf_op jit(solution)/shard_map/ppermute | solution.py:209
  2.2 1.4 %collective-permute-start.1 = (bf16[3072,128]{1,0:T(8,128)(2,1)}, bf16[3072,128]{1,0:T(8,128)(2,1)S(1)}, u32[]{:S(2)}, u32[]{:S(2)}) collective-permute-start(bf16[3072,128]{1,0:T(8,128)(2,1)} %refs_0_.1), channel_id=1, source_target_pairs={{0,6},{1,3},{2,0},{3,5},{4,2},{5,7},{6,4},{7,1},{8,14},{9,11},{10,... | collective-permute-start | bytes 2359304 | tf_op jit(solution)/shard_map/ppermute | solution.py:205
  3.5 1.5 %collective-permute-start = (bf16[3072,128]{1,0:T(8,128)(2,1)}, bf16[3072,128]{1,0:T(8,128)(2,1)S(1)}, u32[]{:S(2)}, u32[]{:S(2)}) collective-permute-start(bf16[3072,128]{1,0:T(8,128)(2,1)} %refs_0_.1), channel_id=1, source_target_pairs={{0,2},{1,7},{2,4},{3,1},{4,6},{5,3},{6,0},{7,5},{8,10},{9,15},{10,... | collective-permute-start | bytes 2359304 | tf_op jit(solution)/shard_map/ppermute | solution.py:205
  5.0 0.8 %copy.26 = s32[1,16,2]{2,1,0:T(8,128)S(1)} copy(s32[1,16,2]{1,2,0:T(2,128)} %param.9) | data formatting | bytes 256 | tf_op args[3]
  5.7 0.1 reshape.85
  5.8 2.8 %gather_fusion = bf16[32,128,128]{2,1,0:T(8,128)(2,1)} fusion(bf16[24,128,128]{2,1,0:T(8,128)(2,1)} %bitcast.11, s32[1024]{0:T(1024)S(1)} %pad_clamp_fusion), kind=kCustom, calls=%fused_computation | custom fusion | bytes 2097280 | tf_op jit(solution)/shard_map/gather | solution.py:213
  8.6 0.0 copy-start
  8.6 0.0 copy-start.1
  8.6 7.7 %all-to-all-start = ((bf16[16,2,128,128]{3,2,1,0:T(8,128)(2,1)}), bf16[16,2,128,128]{3,2,1,0:T(8,128)(2,1)S(1)}, u32[]{:S(2)}, u32[]{:S(2)}) async-start(bf16[16,2,128,128]{3,2,1,0:T(8,128)(2,1)} %bitcast.3), calls=%async_computation | async-start | bytes 2097152 | tf_op jit(solution)/shard_map/all_to_all | solution.py:214
  16.4 0.0 copy-done.7
  16.4 0.0 copy-done.8
  16.4 0.7 collective-permute-start.2
  17.1 0.8 %collective-permute-done.2 = bf16[2,128]{1,0:T(2,128)(2,1)S(1)} collective-permute-done((bf16[2,128]{1,0:T(2,128)(2,1)S(1)}, bf16[2,128]{1,0:T(2,128)(2,1)S(1)}, u32[]{:S(2)}, u32[]{:S(2)}) %collective-permute-start.2) | collective-permute-done | bytes 544 | tf_op jit(solution)/shard_map/ppermute | solution.py:209
  17.9 0.0 collective-permute-done.3.refs_4_
  18.0 0.0 copy-start.4
  18.0 1.8 %collective-permute-done.1.refs_2_ = bf16[3072,128]{1,0:T(8,128)(2,1)S(1)} collective-permute-done((bf16[3072,128]{1,0:T(8,128)(2,1)}, bf16[3072,128]{1,0:T(8,128)(2,1)S(1)}, u32[]{:S(2)}, u32[]{:S(2)}) %collective-permute-start.1) | collective-permute-done | bytes 786464 | tf_op jit(solution)/shard_map/ppermute | solution.py:205
  19.7 0.0 copy-done.4
  19.7 0.0 copy-start.5
  19.7 2.8 %collective-permute-done.refs_1_ = bf16[3072,128]{1,0:T(8,128)(2,1)S(1)} collective-permute-done((bf16[3072,128]{1,0:T(8,128)(2,1)}, bf16[3072,128]{1,0:T(8,128)(2,1)S(1)}, u32[]{:S(2)}, u32[]{:S(2)}) %collective-permute-start) | collective-permute-done | bytes 786464 | tf_op jit(solution)/shard_map/ppermute | solution.py:205
  22.5 0.0 copy-start.6
  22.5 3.0 %collective-permute-start.7 = (bf16[3072,128]{1,0:T(8,128)(2,1)S(1)}, bf16[3072,128]{1,0:T(8,128)(2,1)S(1)}, u32[]{:S(2)}, u32[]{:S(2)}) collective-permute-start(bf16[3072,128]{1,0:T(8,128)(2,1)S(1)} %collective-permute-done.refs_1_), channel_id=1, source_target_pairs={{0,2},{1,7},{2,4},{3,1},{4,6},{5,3},{6,0},{7,5},{8,10},{9,15},{10,... | collective-permute-start | bytes 2359304 | tf_op jit(solution)/shard_map/ppermute | solution.py:205
  25.5 0.0 collective-permute-start.4
  25.5 4.0 %collective-permute-done.4 = bf16[4,128]{1,0:T(4,128)(2,1)S(1)} collective-permute-done((bf16[4,128]{1,0:T(4,128)(2,1)S(1)}, bf16[4,128]{1,0:T(4,128)(2,1)S(1)}, u32[]{:S(2)}, u32[]{:S(2)}) %collective-permute-start.4) | collective-permute-done | bytes 1056 | tf_op jit(solution)/shard_map/ppermute | solution.py:205
  29.5 0.0 collective-permute-start.6
  29.5 0.0 collective-permute-start.5
  29.5 1.1 %collective-permute-done.6 = bf16[4,128]{1,0:T(4,128)(2,1)S(1)} collective-permute-done((bf16[4,128]{1,0:T(4,128)(2,1)S(1)}, bf16[4,128]{1,0:T(4,128)(2,1)S(1)}, u32[]{:S(2)}, u32[]{:S(2)}) %collective-permute-start.6) | collective-permute-done | bytes 1056 | tf_op jit(solution)/shard_map/ppermute | solution.py:209
  30.6 2.9 %collective-permute-done.5 = bf16[4,128]{1,0:T(4,128)(2,1)S(1)} collective-permute-done((bf16[4,128]{1,0:T(4,128)(2,1)S(1)}, bf16[4,128]{1,0:T(4,128)(2,1)S(1)}, u32[]{:S(2)}, u32[]{:S(2)}) %collective-permute-start.5) | collective-permute-done | bytes 1056 | tf_op jit(solution)/shard_map/ppermute | solution.py:205
  33.5 0.0 all-to-all-done
  33.5 0.0 copy-start.3
  33.5 0.0 collective-permute-start.12
  33.5 2.7 %collective-permute-start.11 = (bf16[4096,128]{1,0:T(8,128)(2,1)S(1)}, bf16[4096,128]{1,0:T(8,128)(2,1)}, u32[]{:S(2)}, u32[]{:S(2)}) collective-permute-start(bf16[4096,128]{1,0:T(8,128)(2,1)S(1)} %bitcast.14), channel_id=1, source_target_pairs={{0,2},{1,7},{2,4},{3,1},{4,6},{5,3},{6,0},{7,5},{8,10},{9,15},{10,... | collective-permute-start | bytes 3145736 | tf_op jit(solution)/shard_map/ppermute | solution.py:205
  36.2 0.0 collective-permute-done.7.refs_3_
  36.2 0.0 copy-start.2
  36.2 1.7 %gather_fusion.1 = bf16[32,128,128]{2,1,0:T(8,128)(2,1)} fusion(bf16[24,128,128]{2,1,0:T(8,128)(2,1)S(1)} %bitcast.12, s32[1024]{0:T(1024)S(1)} %pad_clamp_fusion), kind=kCustom, calls=%fused_computation.1 | custom fusion | bytes 2097280 | tf_op jit(solution)/shard_map/gather | solution.py:213
  37.9 7.7 %all-to-all-start.1 = ((bf16[16,2,128,128]{3,2,1,0:T(8,128)(2,1)}), bf16[16,2,128,128]{3,2,1,0:T(8,128)(2,1)}, u32[]{:S(2)}, u32[]{:S(2)}) async-start(bf16[16,2,128,128]{3,2,1,0:T(8,128)(2,1)} %bitcast.9), calls=%async_computation.1 | async-start | bytes 2097152 | tf_op jit(solution)/shard_map/all_to_all | solution.py:214
  45.5 1.1 %collective-permute-start.8 = (bf16[3072,128]{1,0:T(8,128)(2,1)S(1)}, bf16[3072,128]{1,0:T(8,128)(2,1)}, u32[]{:S(2)}, u32[]{:S(2)}) collective-permute-start(bf16[3072,128]{1,0:T(8,128)(2,1)S(1)} %collective-permute-done.refs_1_), channel_id=1, source_target_pairs={{0,1},{1,0},{2,3},{3,2},{4,5},{5,4},{6,7},{7,6},{8,9},{9,8},{10,11... | collective-permute-start | bytes 2359304 | tf_op jit(solution)/shard_map/ppermute | solution.py:209
  46.6 0.1 collective-permute-start.9
  46.7 0.4 collective-permute-start.10
  47.2 1.5 %collective-permute-done.8.refs_5_ = bf16[3072,128]{1,0:T(8,128)(2,1)} collective-permute-done((bf16[3072,128]{1,0:T(8,128)(2,1)S(1)}, bf16[3072,128]{1,0:T(8,128)(2,1)}, u32[]{:S(2)}, u32[]{:S(2)}) %collective-permute-start.8) | collective-permute-done | bytes 786464 | tf_op jit(solution)/shard_map/ppermute | solution.py:209
  48.6 0.4 collective-permute-start.13
  49.0 0.8 %collective-permute-done.9.refs_6_ = bf16[3072,128]{1,0:T(8,128)(2,1)} collective-permute-done((bf16[3072,128]{1,0:T(8,128)(2,1)S(1)}, bf16[3072,128]{1,0:T(8,128)(2,1)}, u32[]{:S(2)}, u32[]{:S(2)}) %collective-permute-start.9) | collective-permute-done | bytes 786464 | tf_op jit(solution)/shard_map/ppermute | solution.py:209
  49.8 1.1 %collective-permute-done.10.refs_7_ = bf16[3072,128]{1,0:T(8,128)(2,1)} collective-permute-done((bf16[3072,128]{1,0:T(8,128)(2,1)S(1)}, bf16[3072,128]{1,0:T(8,128)(2,1)}, u32[]{:S(2)}, u32[]{:S(2)}) %collective-permute-start.10) | collective-permute-done | bytes 786464 | tf_op jit(solution)/shard_map/ppermute | solution.py:209
  50.9 0.0 copy-done.5
  50.9 0.0 copy-done.6
  50.9 0.0 copy-done.2
  50.9 0.0 copy-done
  50.9 0.0 copy-done.1
  50.9 9.1 %shard_map.77 = (f32[48,128,128]{2,1,0:T(8,128)}, f32[48,128,128]{2,1,0:T(8,128)}, bf16[3,256,1024]{2,1,0:T(8,128)(2,1)S(1)}, s32[90]{0:T(128)S(1)}, s32[4]{0:T(128)S(1)}) custom-call(s32[48]{0:T(128)S(1)} %copy-done.1, s32[48]{0:T(128)S(1)} %copy-done, s32[1]{0:T(128)} %bitcast.q_ref, f32[4,4,1,128]{3,2,1,0:T(1,128)S(1)} %maximum_convert_fusion.level_ref, ...), custom_call_target="tpu_custom_call" | custom-call | flops 1024 | bytes 1024 | tf_op jit(solution)/shard_map/pallas_call | solution.py:251
  60.1 0.0 copy-done.3
  60.1 0.0 collective-permute-done.12.refs_2_
  60.1 0.0 collective-permute-done.11.refs_1_
  60.1 0.3 collective-permute-start.14
  60.4 0.2 collective-permute-start.15
  60.7 0.4 all-to-all-done.1
  61.1 3.2 %collective-permute-start.16 = (bf16[4096,128]{1,0:T(8,128)(2,1)}, bf16[4096,128]{1,0:T(8,128)(2,1)S(1)}, u32[]{:S(2)}, u32[]{:S(2)}) collective-permute-start(bf16[4096,128]{1,0:T(8,128)(2,1)} %bitcast.10.refs_3_), channel_id=1, source_target_pairs={{0,1},{1,0},{2,3},{3,2},{4,5},{5,4},{6,7},{7,6},{8,9},{9,8},{10,11... | collective-permute-start | bytes 3145736 | tf_op jit(solution)/shard_map/ppermute | solution.py:209
  64.2 0.0 collective-permute-done.13.refs_4_
  64.2 0.0 collective-permute-done.14.refs_5_
  64.2 0.5 collective-permute-done.15.refs_6_
  64.7 2.0 %collective-permute-done.16.refs_7_ = bf16[4096,128]{1,0:T(8,128)(2,1)S(1)} collective-permute-done((bf16[4096,128]{1,0:T(8,128)(2,1)}, bf16[4096,128]{1,0:T(8,128)(2,1)S(1)}, u32[]{:S(2)}, u32[]{:S(2)}) %collective-permute-start.16) | collective-permute-done | bytes 1048608 | tf_op jit(solution)/shard_map/ppermute | solution.py:209
  66.7 7.3 %shard_map.78 = (f32[48,128,128]{2,1,0:T(8,128)}, f32[48,128,128]{2,1,0:T(8,128)}) custom-call(s32[48]{0:T(128)S(1)} %copy-done, s32[90]{0:T(128)S(1)} %get-tuple-element.33.batch, s32[4]{0:T(128)S(1)} %get-tuple-element.34.totals, bf16[3,256,1024]{2,1,0:T(8,128)(2,1)S(1)} %get-tuple-element.36.w_ref, ...), custom_call_target="tpu_custom_call", output_to_operand_aliasing={{0}: (4, {}), {1}: (5, {})} | custom-call | flops 1024 | bytes 1024 | tf_op jit(solution)/shard_map/pallas_call | solution.py:278
  (8 shorter events, 0.1 us)
Async XLA Ops:
  0.6 15.7 %copy-start.7 = (bf16[1,128]{1,0:T(2,128)(2,1)S(1)}, bf16[1,128]{1,0:T(2,128)(2,1)}, u32[]{:S(2)}) copy-start(bf16[1,128]{1,0:T(2,128)(2,1)} %param.8) | copy-start | bytes 772
  0.6 15.7 %copy-start.8 = (bf16[1,128]{1,0:T(2,128)(2,1)S(1)}, bf16[1,128]{1,0:T(2,128)(2,1)}, u32[]{:S(2)}) copy-start(bf16[1,128]{1,0:T(2,128)(2,1)} %param.7) | copy-start | bytes 772
  0.7 17.3 %collective-permute-start.3 = (bf16[3072,128]{1,0:T(8,128)(2,1)}, bf16[3072,128]{1,0:T(8,128)(2,1)S(1)}, u32[]{:S(2)}, u32[]{:S(2)}) collective-permute-start(bf16[3072,128]{1,0:T(8,128)(2,1)} %refs_0_.1), channel_id=1, source_target_pairs={{0,1},{1,0},{2,3},{3,2},{4,5},{5,4},{6,7},{7,6},{8,9},{9,8},{10,11... | collective-permute-start | bytes 2359304 | tf_op jit(solution)/shard_map/ppermute | solution.py:209
  2.2 17.6 %collective-permute-start.1 = (bf16[3072,128]{1,0:T(8,128)(2,1)}, bf16[3072,128]{1,0:T(8,128)(2,1)S(1)}, u32[]{:S(2)}, u32[]{:S(2)}) collective-permute-start(bf16[3072,128]{1,0:T(8,128)(2,1)} %refs_0_.1), channel_id=1, source_target_pairs={{0,6},{1,3},{2,0},{3,5},{4,2},{5,7},{6,4},{7,1},{8,14},{9,11},{10,... | collective-permute-start | bytes 2359304 | tf_op jit(solution)/shard_map/ppermute | solution.py:205
  3.5 18.9 %collective-permute-start = (bf16[3072,128]{1,0:T(8,128)(2,1)}, bf16[3072,128]{1,0:T(8,128)(2,1)S(1)}, u32[]{:S(2)}, u32[]{:S(2)}) collective-permute-start(bf16[3072,128]{1,0:T(8,128)(2,1)} %refs_0_.1), channel_id=1, source_target_pairs={{0,2},{1,7},{2,4},{3,1},{4,6},{5,3},{6,0},{7,5},{8,10},{9,15},{10,... | collective-permute-start | bytes 2359304 | tf_op jit(solution)/shard_map/ppermute | solution.py:205
  8.6 42.3 %copy-start = (s32[48]{0:T(128)S(1)}, s32[48]{0:T(128)}, u32[]{:S(2)}) copy-start(s32[48]{0:T(128)} %src_ref.3) | copy-start | bytes 580
  8.6 42.3 %copy-start.1 = (s32[48]{0:T(128)S(1)}, s32[48]{0:T(128)}, u32[]{:S(2)}) copy-start(s32[48]{0:T(128)} %row_ref.1) | copy-start | bytes 580
  8.6 24.9 %all-to-all-start = ((bf16[16,2,128,128]{3,2,1,0:T(8,128)(2,1)}), bf16[16,2,128,128]{3,2,1,0:T(8,128)(2,1)S(1)}, u32[]{:S(2)}, u32[]{:S(2)}) async-start(bf16[16,2,128,128]{3,2,1,0:T(8,128)(2,1)} %bitcast.3), calls=%async_computation | async-start | bytes 2097152 | tf_op jit(solution)/shard_map/all_to_all | solution.py:214
  16.4 1.5 %collective-permute-start.2 = (bf16[2,128]{1,0:T(2,128)(2,1)S(1)}, bf16[2,128]{1,0:T(2,128)(2,1)S(1)}, u32[]{:S(2)}, u32[]{:S(2)}) collective-permute-start(bf16[2,128]{1,0:T(2,128)(2,1)S(1)} %pad_maximum_fusion.1), channel_id=1, source_target_pairs={{0,1},{1,0},{2,3},{3,2},{4,5},{5,4},{6,7},{7,6},{8,9},{9,8},{10,11... | collective-permute-start | bytes 1544 | tf_op jit(solution)/shard_map/ppermute | solution.py:209
  18.0 1.8 %copy-start.4 = (bf16[3072,128]{1,0:T(8,128)(2,1)}, bf16[3072,128]{1,0:T(8,128)(2,1)S(1)}, u32[]{:S(2)}) copy-start(bf16[3072,128]{1,0:T(8,128)(2,1)S(1)} %collective-permute-done.3.refs_4_) | copy-start | bytes 2359300
  19.7 31.2 %copy-start.5 = (bf16[3072,128]{1,0:T(8,128)(2,1)}, bf16[3072,128]{1,0:T(8,128)(2,1)S(1)}, u32[]{:S(2)}) copy-start(bf16[3072,128]{1,0:T(8,128)(2,1)S(1)} %collective-permute-done.1.refs_2_) | copy-start | bytes 2359300
  22.5 28.4 %copy-start.6 = (bf16[3072,128]{1,0:T(8,128)(2,1)}, bf16[3072,128]{1,0:T(8,128)(2,1)S(1)}, u32[]{:S(2)}) copy-start(bf16[3072,128]{1,0:T(8,128)(2,1)S(1)} %collective-permute-done.refs_1_) | copy-start | bytes 2359300
  22.5 13.7 %collective-permute-start.7 = (bf16[3072,128]{1,0:T(8,128)(2,1)S(1)}, bf16[3072,128]{1,0:T(8,128)(2,1)S(1)}, u32[]{:S(2)}, u32[]{:S(2)}) collective-permute-start(bf16[3072,128]{1,0:T(8,128)(2,1)S(1)} %collective-permute-done.refs_1_), channel_id=1, source_target_pairs={{0,2},{1,7},{2,4},{3,1},{4,6},{5,3},{6,0},{7,5},{8,10},{9,15},{10,... | collective-permute-start | bytes 2359304 | tf_op jit(solution)/shard_map/ppermute | solution.py:205
  25.5 4.0 %collective-permute-start.4 = (bf16[4,128]{1,0:T(4,128)(2,1)S(1)}, bf16[4,128]{1,0:T(4,128)(2,1)S(1)}, u32[]{:S(2)}, u32[]{:S(2)}) collective-permute-start(bf16[4,128]{1,0:T(4,128)(2,1)S(1)} %pad_maximum_fusion), channel_id=1, source_target_pairs={{0,6},{1,3},{2,0},{3,5},{4,2},{5,7},{6,4},{7,1},{8,14},{9,11},{10,... | collective-permute-start | bytes 3080 | tf_op jit(solution)/shard_map/ppermute | solution.py:205
  29.5 1.1 %collective-permute-start.6 = (bf16[4,128]{1,0:T(4,128)(2,1)S(1)}, bf16[4,128]{1,0:T(4,128)(2,1)S(1)}, u32[]{:S(2)}, u32[]{:S(2)}) collective-permute-start(bf16[4,128]{1,0:T(4,128)(2,1)S(1)} %collective-permute-done.4), channel_id=1, source_target_pairs={{0,1},{1,0},{2,3},{3,2},{4,5},{5,4},{6,7},{7,6},{8,9},{9,8},{10,11... | collective-permute-start | bytes 3080 | tf_op jit(solution)/shard_map/ppermute | solution.py:209
  29.5 4.0 %collective-permute-start.5 = (bf16[4,128]{1,0:T(4,128)(2,1)S(1)}, bf16[4,128]{1,0:T(4,128)(2,1)S(1)}, u32[]{:S(2)}, u32[]{:S(2)}) collective-permute-start(bf16[4,128]{1,0:T(4,128)(2,1)S(1)} %collective-permute-done.4), channel_id=1, source_target_pairs={{0,6},{1,3},{2,0},{3,5},{4,2},{5,7},{6,4},{7,1},{8,14},{9,11},{10,... | collective-permute-start | bytes 3080 | tf_op jit(solution)/shard_map/ppermute | solution.py:205
  33.5 26.6 %copy-start.3 = (bf16[16,2,128,128]{3,2,1,0:T(8,128)(2,1)}, bf16[16,2,128,128]{3,2,1,0:T(8,128)(2,1)S(1)}, u32[]{:S(2)}) copy-start(bf16[16,2,128,128]{3,2,1,0:T(8,128)(2,1)S(1)} %all-to-all-done) | copy-start | bytes 3145732
  33.5 26.6 %collective-permute-start.12 = (bf16[4096,128]{1,0:T(8,128)(2,1)S(1)}, bf16[4096,128]{1,0:T(8,128)(2,1)}, u32[]{:S(2)}, u32[]{:S(2)}) collective-permute-start(bf16[4096,128]{1,0:T(8,128)(2,1)S(1)} %bitcast.13), channel_id=1, source_target_pairs={{0,6},{1,3},{2,0},{3,5},{4,2},{5,7},{6,4},{7,1},{8,14},{9,11},{10,... | collective-permute-start | bytes 3145736 | tf_op jit(solution)/shard_map/ppermute | solution.py:205
  33.5 26.6 %collective-permute-start.11 = (bf16[4096,128]{1,0:T(8,128)(2,1)S(1)}, bf16[4096,128]{1,0:T(8,128)(2,1)}, u32[]{:S(2)}, u32[]{:S(2)}) collective-permute-start(bf16[4096,128]{1,0:T(8,128)(2,1)S(1)} %bitcast.14), channel_id=1, source_target_pairs={{0,2},{1,7},{2,4},{3,1},{4,6},{5,3},{6,0},{7,5},{8,10},{9,15},{10,... | collective-permute-start | bytes 3145736 | tf_op jit(solution)/shard_map/ppermute | solution.py:205
  36.2 14.7 %copy-start.2 = (bf16[3072,128]{1,0:T(8,128)(2,1)}, bf16[3072,128]{1,0:T(8,128)(2,1)S(1)}, u32[]{:S(2)}) copy-start(bf16[3072,128]{1,0:T(8,128)(2,1)S(1)} %collective-permute-done.7.refs_3_) | copy-start | bytes 2359300
  37.9 23.2 %all-to-all-start.1 = ((bf16[16,2,128,128]{3,2,1,0:T(8,128)(2,1)}), bf16[16,2,128,128]{3,2,1,0:T(8,128)(2,1)}, u32[]{:S(2)}, u32[]{:S(2)}) async-start(bf16[16,2,128,128]{3,2,1,0:T(8,128)(2,1)} %bitcast.9), calls=%async_computation.1 | async-start | bytes 2097152 | tf_op jit(solution)/shard_map/all_to_all | solution.py:214
  45.5 3.1 %collective-permute-start.8 = (bf16[3072,128]{1,0:T(8,128)(2,1)S(1)}, bf16[3072,128]{1,0:T(8,128)(2,1)}, u32[]{:S(2)}, u32[]{:S(2)}) collective-permute-start(bf16[3072,128]{1,0:T(8,128)(2,1)S(1)} %collective-permute-done.refs_1_), channel_id=1, source_target_pairs={{0,1},{1,0},{2,3},{3,2},{4,5},{5,4},{6,7},{7,6},{8,9},{9,8},{10,11... | collective-permute-start | bytes 2359304 | tf_op jit(solution)/shard_map/ppermute | solution.py:209
  46.6 3.2 %collective-permute-start.9 = (bf16[3072,128]{1,0:T(8,128)(2,1)S(1)}, bf16[3072,128]{1,0:T(8,128)(2,1)}, u32[]{:S(2)}, u32[]{:S(2)}) collective-permute-start(bf16[3072,128]{1,0:T(8,128)(2,1)S(1)} %collective-permute-done.1.refs_2_), channel_id=1, source_target_pairs={{0,1},{1,0},{2,3},{3,2},{4,5},{5,4},{6,7},{7,6},{8,9},{9,8},{10,11... | collective-permute-start | bytes 2359304 | tf_op jit(solution)/shard_map/ppermute | solution.py:209
  46.7 4.2 %collective-permute-start.10 = (bf16[3072,128]{1,0:T(8,128)(2,1)S(1)}, bf16[3072,128]{1,0:T(8,128)(2,1)}, u32[]{:S(2)}, u32[]{:S(2)}) collective-permute-start(bf16[3072,128]{1,0:T(8,128)(2,1)S(1)} %collective-permute-done.7.refs_3_), channel_id=1, source_target_pairs={{0,1},{1,0},{2,3},{3,2},{4,5},{5,4},{6,7},{7,6},{8,9},{9,8},{10,11... | collective-permute-start | bytes 2359304 | tf_op jit(solution)/shard_map/ppermute | solution.py:209
  48.6 15.6 %collective-permute-start.13 = (bf16[4096,128]{1,0:T(8,128)(2,1)S(1)}, bf16[4096,128]{1,0:T(8,128)(2,1)}, u32[]{:S(2)}, u32[]{:S(2)}) collective-permute-start(bf16[4096,128]{1,0:T(8,128)(2,1)S(1)} %bitcast.15), channel_id=1, source_target_pairs={{0,1},{1,0},{2,3},{3,2},{4,5},{5,4},{6,7},{7,6},{8,9},{9,8},{10,11... | collective-permute-start | bytes 3145736 | tf_op jit(solution)/shard_map/ppermute | solution.py:209
  60.1 4.1 %collective-permute-start.14 = (bf16[4096,128]{1,0:T(8,128)(2,1)}, bf16[4096,128]{1,0:T(8,128)(2,1)}, u32[]{:S(2)}, u32[]{:S(2)}) collective-permute-start(bf16[4096,128]{1,0:T(8,128)(2,1)} %collective-permute-done.11.refs_1_), channel_id=1, source_target_pairs={{0,1},{1,0},{2,3},{3,2},{4,5},{5,4},{6,7},{7,6},{8,9},{9,8},{10,11... | collective-permute-start | bytes 3145736 | tf_op jit(solution)/shard_map/ppermute | solution.py:209
  60.4 4.2 %collective-permute-start.15 = (bf16[4096,128]{1,0:T(8,128)(2,1)}, bf16[4096,128]{1,0:T(8,128)(2,1)}, u32[]{:S(2)}, u32[]{:S(2)}) collective-permute-start(bf16[4096,128]{1,0:T(8,128)(2,1)} %collective-permute-done.12.refs_2_), channel_id=1, source_target_pairs={{0,1},{1,0},{2,3},{3,2},{4,5},{5,4},{6,7},{7,6},{8,9},{9,8},{10,11... | collective-permute-start | bytes 3145736 | tf_op jit(solution)/shard_map/ppermute | solution.py:209
  61.1 5.7 %collective-permute-start.16 = (bf16[4096,128]{1,0:T(8,128)(2,1)}, bf16[4096,128]{1,0:T(8,128)(2,1)S(1)}, u32[]{:S(2)}, u32[]{:S(2)}) collective-permute-start(bf16[4096,128]{1,0:T(8,128)(2,1)} %bitcast.10.refs_3_), channel_id=1, source_target_pairs={{0,1},{1,0},{2,3},{3,2},{4,5},{5,4},{6,7},{7,6},{8,9},{9,8},{10,11... | collective-permute-start | bytes 3145736 | tf_op jit(solution)/shard_map/ppermute | solution.py:209

commit v5 on v4

--- a/solution.py
+++ b/solution.py
@@ -209,9 +209,12 @@
     return lax.ppermute(x, "slab", [(q, q ^ 1) for q in range(2 * YS)])
 
 
-def exchange(tiles, picks):
-    tiles = tiles.reshape(-1, BS, BS).at[picks].get(mode="promise_in_bounds", wrap_negative_indices=False)
-    return lax.all_to_all(tiles, "rows", split_axis=0, concat_axis=0, tiled=True).reshape(-1, BS)
+def choose(tiles, picks):
+    return tiles.reshape(-1, BS, BS).at[picks].get(mode="promise_in_bounds", wrap_negative_indices=False)
+
+
+def exchange(chosen):
+    return lax.all_to_all(chosen, "rows", split_axis=0, concat_axis=0, tiled=True).reshape(-1, BS)
 
 
 def limit(mib):
@@ -228,19 +231,21 @@
     group = blocks // shards
     pairs = pair_rows.shape[0]
     own = coefficients
-    front, back = hop(own, 1), hop(own, -1)
-    got = exchange(own, send_lists[0])
+    chosen = choose(own, send_lists[0])
+    chosen, again = lax.optimization_barrier((chosen, own))
+    front, back = hop(own, 1), hop(again, -1)
+    got = exchange(chosen)
     level = jnp.concatenate([occupations, energies], axis=0)
     level = jnp.concatenate([level, swap(level)], axis=0)
-    front, back, level, own_x = lax.optimization_barrier((front, back, level, swap(own)))
+    front, back, level = lax.optimization_barrier((front, back, level))
     last = hop(front, 1)
     behind = hop(level, -1)
     turned = [behind, hop(behind, -1), swap(behind)]
-    got, front, back, *turned = lax.optimization_barrier((got, front, back, *turned))
+    got, front, back, own_x, *turned = lax.optimization_barrier((got, front, back, swap(own), *turned))
     levels = jnp.stack([level, *turned]).astype(jnp.float32)[:, :, None, :]
     got_front, got_back = hop(got, 1), hop(got, -1)
     got_late, last = lax.optimization_barrier((got, last))
-    got_last = exchange(last, send_lists[0])
+    got_last = exchange(choose(last, send_lists[0]))
     held = [own, front, back, last, own_x, swap(front), swap(back), swap(last)]
     q = lax.axis_index("slab").reshape(1).astype(jnp.int32)
 

time: 75.1 us -> 75 us (level); the launches traced: 74 us -> 74.7 us
  starting transfers between devices: 31.9 us -> 29.3 us
  waiting for transfers between devices: 19.5 us -> 21.8 us
  local copies, waits for them, and re-layouts: 5.36 us -> 6.3 us
    ppermute x10, starting transfers between devices: 7.92 us -> 6.09 us  [swap(): return lax.ppermute(x, 'slab', [(q, q ^ 1) for q in range(2 * YS)])]
    all_to_all x2, waiting for transfers between devices: 0.37 us -> 2.02 us  [exchange(): lax.all_to_all(chosen, 'rows', split_axis=0, concat_axis=0, tiled=True)]
    ppermute x7, waiting for transfers between devices: 11.4 us -> 12.7 us  [hop(): return lax.ppermute(x, 'slab', pairs)]
    unnamed x19 -> x23, local copies, waits for them, and re-layouts: 0.79 us -> 1.72 us
  transfers between devices with their start and end apart: 19 -> 19, of which waited for: 12 -> 12; matrix products, arithmetic and copies ran while one was open for 7% -> 7% of each run, Pallas kernels for 12% -> 11%
where the time goes in v5:
time: 75 us; the launch traced here: 74.7 us
  starting transfers between devices  29.3 us (39%)
  waiting for transfers between devices  21.8 us (29%)
  Pallas kernels  16.4 us (22%)
  local copies, waits for them, and re-layouts  6.3 us (8%)
  between operations  0.81 us (1%)
    all_to_all x2, starting transfers between devices, exchange(): lax.all_to_all(chosen, 'rows', split_axis=0, concat_axis=0, tiled=True)  15.3 us
    ppermute x7, waiting for transfers between devices, hop(): return lax.ppermute(x, 'slab', pairs)  12.7 us
    pallas_call x1, Pallas kernels, body(): pl.pallas_call(functools.partial(near_kernel, group=group, blocks=blocks)...  8.42 us
    pallas_call x1, Pallas kernels, body(): pl.pallas_call(functools.partial(far_kernel, blocks=blocks), in_specs=[SM...  8.01 us
    ppermute x7, starting transfers between devices, hop(): return lax.ppermute(x, 'slab', pairs)  7.92 us
    ppermute x10, waiting for transfers between devices, swap(): return lax.ppermute(x, 'slab', [(q, q ^ 1) for q in range(2 * YS)])  7.06 us
    ppermute x10, starting transfers between devices, swap(): return lax.ppermute(x, 'slab', [(q, q ^ 1) for q in range(2 * YS)])  6.09 us
    gather x2, local copies, waits for them, and re-layouts, choose(): tiles.reshape(-1, BS, BS).at[picks]  4.48 us
  transfers between devices with their start and end apart: 19, of which 12 were waited for; matrix products, arithmetic and copies ran while one was open for 7% of the time, Pallas kernels for 11%

profile of v5, /device:TPU:1, one launch (start us, length us, event | category | flops | bytes accessed | tf_op | source)
XLA Modules:
  0.0 74.7 jit_solution(6170343641116348197)
XLA Ops:
  0.6 0.0 copy-start.2
  0.6 0.0 copy-start.9
  0.7 0.0 copy-start.10
  0.7 3.6 %collective-permute-start = (bf16[3072,128]{1,0:T(8,128)(2,1)}, bf16[3072,128]{1,0:T(8,128)(2,1)S(1)}, u32[]{:S(2)}, u32[]{:S(2)}) collective-permute-start(bf16[3072,128]{1,0:T(8,128)(2,1)} %refs_0_.1), channel_id=1, source_target_pairs={{0,2},{1,7},{2,4},{3,1},{4,6},{5,3},{6,0},{7,5},{8,10},{9,15},{10,... | collective-permute-start | bytes 2359304 | tf_op jit(solution)/shard_map/ppermute | solution.py:205
  4.3 0.8 %copy.26 = s32[1,16,2]{2,1,0:T(8,128)S(1)} copy(s32[1,16,2]{1,2,0:T(2,128)} %param.9) | data formatting | bytes 256 | tf_op args[3]
  5.1 0.1 reshape.85
  5.2 2.8 %gather_fusion = bf16[32,128,128]{2,1,0:T(8,128)(2,1)} fusion(bf16[24,128,128]{2,1,0:T(8,128)(2,1)} %bitcast.11, s32[1024]{0:T(1024)S(1)} %pad_clamp_fusion), kind=kCustom, calls=%fused_computation | custom fusion | bytes 2097280 | tf_op jit(solution)/shard_map/gather | solution.py:213
  7.9 0.0 copy-start
  7.9 0.0 copy-start.1
  7.9 0.0 collective-permute-start.1
  7.9 7.8 %all-to-all-start = ((bf16[16,2,128,128]{3,2,1,0:T(8,128)(2,1)}), bf16[16,2,128,128]{3,2,1,0:T(8,128)(2,1)}, u32[]{:S(2)}, u32[]{:S(2)}) async-start(bf16[16,2,128,128]{3,2,1,0:T(8,128)(2,1)} %bitcast.2), calls=%async_computation | async-start | bytes 2097152 | tf_op jit(solution)/shard_map/all_to_all | solution.py:217
  15.7 0.0 copy-done.9
  15.8 0.0 copy-done.10
  15.8 1.4 %collective-permute-start.2 = (bf16[2,128]{1,0:T(2,128)(2,1)S(1)}, bf16[2,128]{1,0:T(2,128)(2,1)S(1)}, u32[]{:S(2)}, u32[]{:S(2)}) collective-permute-start(bf16[2,128]{1,0:T(2,128)(2,1)S(1)} %pad_maximum_fusion.1), channel_id=1, source_target_pairs={{0,1},{1,0},{2,3},{3,2},{4,5},{5,4},{6,7},{7,6},{8,9},{9,8},{10,11... | collective-permute-start | bytes 1544 | tf_op jit(solution)/shard_map/ppermute | solution.py:209
  17.2 0.0 copy-done.2
  17.2 0.1 collective-permute-start.3
  17.3 0.7 collective-permute-done.2
  18.0 0.0 collective-permute-done.refs_1_
  18.0 0.0 copy-start.5
  18.0 5.7 %collective-permute-done.1.refs_2_ = bf16[3072,128]{1,0:T(8,128)(2,1)S(1)} collective-permute-done((bf16[3072,128]{1,0:T(8,128)(2,1)}, bf16[3072,128]{1,0:T(8,128)(2,1)S(1)}, u32[]{:S(2)}, u32[]{:S(2)}) %collective-permute-start.1) | collective-permute-done | bytes 786464 | tf_op jit(solution)/shard_map/ppermute | solution.py:205
  23.7 0.0 copy-start.6
  23.7 1.6 %collective-permute-start.7 = (bf16[3072,128]{1,0:T(8,128)(2,1)S(1)}, bf16[3072,128]{1,0:T(8,128)(2,1)S(1)}, u32[]{:S(2)}, u32[]{:S(2)}) collective-permute-start(bf16[3072,128]{1,0:T(8,128)(2,1)S(1)} %collective-permute-done.refs_1_), channel_id=1, source_target_pairs={{0,2},{1,7},{2,4},{3,1},{4,6},{5,3},{6,0},{7,5},{8,10},{9,15},{10,... | collective-permute-start | bytes 2359304 | tf_op jit(solution)/shard_map/ppermute | solution.py:205
  25.3 0.0 collective-permute-start.4
  25.3 4.1 %collective-permute-done.4 = bf16[4,128]{1,0:T(4,128)(2,1)S(1)} collective-permute-done((bf16[4,128]{1,0:T(4,128)(2,1)S(1)}, bf16[4,128]{1,0:T(4,128)(2,1)S(1)}, u32[]{:S(2)}, u32[]{:S(2)}) %collective-permute-start.4) | collective-permute-done | bytes 1056 | tf_op jit(solution)/shard_map/ppermute | solution.py:205
  29.4 0.0 collective-permute-start.6
  29.4 0.0 collective-permute-start.5
  29.4 0.0 collective-permute-done.3.refs_4_
  29.4 0.0 copy-start.7
  29.4 0.9 %copy-done.7 = bf16[3072,128]{1,0:T(8,128)(2,1)} copy-done((bf16[3072,128]{1,0:T(8,128)(2,1)}, bf16[3072,128]{1,0:T(8,128)(2,1)S(1)}, u32[]{:S(2)}) %copy-start.7) | copy-done | bytes 786456
  30.4 0.2 collective-permute-done.6
  30.6 2.9 %collective-permute-done.5 = bf16[4,128]{1,0:T(4,128)(2,1)S(1)} collective-permute-done((bf16[4,128]{1,0:T(4,128)(2,1)S(1)}, bf16[4,128]{1,0:T(4,128)(2,1)S(1)}, u32[]{:S(2)}, u32[]{:S(2)}) %collective-permute-start.5) | collective-permute-done | bytes 1056 | tf_op jit(solution)/shard_map/ppermute | solution.py:205
  33.5 0.0 all-to-all-done
  33.5 0.0 collective-permute-start.12
  33.5 2.7 %collective-permute-start.11 = (bf16[4096,128]{1,0:T(8,128)(2,1)}, bf16[4096,128]{1,0:T(8,128)(2,1)}, u32[]{:S(2)}, u32[]{:S(2)}) collective-permute-start(bf16[4096,128]{1,0:T(8,128)(2,1)} %bitcast.4.refs_0_), channel_id=1, source_target_pairs={{0,2},{1,7},{2,4},{3,1},{4,6},{5,3},{6,0},{7,5},{8,10},{9,15},{10,... | collective-permute-start | bytes 3145736 | tf_op jit(solution)/shard_map/ppermute | solution.py:205
  36.1 0.0 collective-permute-done.7.refs_3_
  36.1 0.0 copy-start.3
  36.1 1.7 %gather_fusion.1 = bf16[32,128,128]{2,1,0:T(8,128)(2,1)} fusion(bf16[24,128,128]{2,1,0:T(8,128)(2,1)S(1)} %bitcast.12, s32[1024]{0:T(1024)S(1)} %pad_clamp_fusion), kind=kCustom, calls=%fused_computation.1 | custom fusion | bytes 2097280 | tf_op jit(solution)/shard_map/gather | solution.py:213
  37.8 7.5 %all-to-all-start.1 = ((bf16[16,2,128,128]{3,2,1,0:T(8,128)(2,1)}), bf16[16,2,128,128]{3,2,1,0:T(8,128)(2,1)}, u32[]{:S(2)}, u32[]{:S(2)}) async-start(bf16[16,2,128,128]{3,2,1,0:T(8,128)(2,1)} %bitcast.9), calls=%async_computation.1 | async-start | bytes 2097152 | tf_op jit(solution)/shard_map/all_to_all | solution.py:217
  45.4 0.3 collective-permute-start.8
  45.7 0.3 collective-permute-start.9
  45.9 0.2 collective-permute-start.10
  46.2 1.5 %collective-permute-done.8.refs_5_ = bf16[3072,128]{1,0:T(8,128)(2,1)S(1)} collective-permute-done((bf16[3072,128]{1,0:T(8,128)(2,1)S(1)}, bf16[3072,128]{1,0:T(8,128)(2,1)S(1)}, u32[]{:S(2)}, u32[]{:S(2)}) %collective-permute-start.8) | collective-permute-done | bytes 786464 | tf_op jit(solution)/shard_map/ppermute | solution.py:209
  47.7 0.2 collective-permute-start.13
  47.9 1.0 %collective-permute-done.9.refs_6_ = bf16[3072,128]{1,0:T(8,128)(2,1)} collective-permute-done((bf16[3072,128]{1,0:T(8,128)(2,1)S(1)}, bf16[3072,128]{1,0:T(8,128)(2,1)}, u32[]{:S(2)}, u32[]{:S(2)}) %collective-permute-start.9) | collective-permute-done | bytes 786464 | tf_op jit(solution)/shard_map/ppermute | solution.py:209
  49.0 1.1 %collective-permute-done.10.refs_7_ = bf16[3072,128]{1,0:T(8,128)(2,1)} collective-permute-done((bf16[3072,128]{1,0:T(8,128)(2,1)S(1)}, bf16[3072,128]{1,0:T(8,128)(2,1)}, u32[]{:S(2)}, u32[]{:S(2)}) %collective-permute-start.10) | collective-permute-done | bytes 786464 | tf_op jit(solution)/shard_map/ppermute | solution.py:209
  50.1 0.0 copy-done.5
  50.1 0.0 copy-done.6
  50.1 0.0 copy-done.3
  50.1 0.0 copy-done.8
  50.1 0.0 copy-done
  50.1 0.0 copy-done.1
  50.1 8.4 %shard_map.77 = (f32[48,128,128]{2,1,0:T(8,128)}, f32[48,128,128]{2,1,0:T(8,128)}, bf16[3,256,1024]{2,1,0:T(8,128)(2,1)S(1)}, s32[90]{0:T(128)S(1)}, s32[4]{0:T(128)S(1)}) custom-call(s32[48]{0:T(128)S(1)} %copy-done.1, s32[48]{0:T(128)S(1)} %copy-done, s32[1]{0:T(128)} %bitcast.q_ref, f32[4,4,1,128]{3,2,1,0:T(1,128)S(1)} %maximum_convert_fusion.level_ref, ...), custom_call_target="tpu_custom_call" | custom-call | flops 1024 | bytes 1024 | tf_op jit(solution)/shard_map/pallas_call | solution.py:256
  58.6 0.0 collective-permute-done.12.refs_2_
  58.6 0.0 collective-permute-done.11.refs_1_
  58.6 2.0 %collective-permute-start.14 = (bf16[4096,128]{1,0:T(8,128)(2,1)}, bf16[4096,128]{1,0:T(8,128)(2,1)S(1)}, u32[]{:S(2)}, u32[]{:S(2)}) collective-permute-start(bf16[4096,128]{1,0:T(8,128)(2,1)} %collective-permute-done.11.refs_1_), channel_id=1, source_target_pairs={{0,1},{1,0},{2,3},{3,2},{4,5},{5,4},{6,7},{7,6},{8,9},{9,8},{10,11... | collective-permute-start | bytes 3145736 | tf_op jit(solution)/shard_map/ppermute | solution.py:209
  60.6 0.0 collective-permute-start.15
  60.6 2.0 %all-to-all-done.1 = bf16[16,2,128,128]{3,2,1,0:T(8,128)(2,1)} async-done(((bf16[16,2,128,128]{3,2,1,0:T(8,128)(2,1)}), bf16[16,2,128,128]{3,2,1,0:T(8,128)(2,1)}, u32[]{:S(2)}, u32[]{:S(2)}) %all-to-all-start.1) | async-done | bytes 1048608 | tf_op jit(solution)/shard_map/all_to_all | solution.py:217
  62.6 1.6 %collective-permute-start.16 = (bf16[4096,128]{1,0:T(8,128)(2,1)}, bf16[4096,128]{1,0:T(8,128)(2,1)S(1)}, u32[]{:S(2)}, u32[]{:S(2)}) collective-permute-start(bf16[4096,128]{1,0:T(8,128)(2,1)} %bitcast.10.refs_3_), channel_id=1, source_target_pairs={{0,1},{1,0},{2,3},{3,2},{4,5},{5,4},{6,7},{7,6},{8,9},{9,8},{10,11... | collective-permute-start | bytes 3145736 | tf_op jit(solution)/shard_map/ppermute | solution.py:209
  64.2 0.0 collective-permute-done.13.refs_4_
  64.2 0.4 collective-permute-done.14.refs_5_
  64.5 0.2 collective-permute-done.15.refs_6_
  64.7 2.0 %collective-permute-done.16.refs_7_ = bf16[4096,128]{1,0:T(8,128)(2,1)S(1)} collective-permute-done((bf16[4096,128]{1,0:T(8,128)(2,1)}, bf16[4096,128]{1,0:T(8,128)(2,1)S(1)}, u32[]{:S(2)}, u32[]{:S(2)}) %collective-permute-start.16) | collective-permute-done | bytes 1048608 | tf_op jit(solution)/shard_map/ppermute | solution.py:209
  66.7 0.0 copy-done.4
  66.7 8.0 %shard_map.78 = (f32[48,128,128]{2,1,0:T(8,128)}, f32[48,128,128]{2,1,0:T(8,128)}) custom-call(s32[48]{0:T(128)S(1)} %copy-done, s32[90]{0:T(128)S(1)} %get-tuple-element.37.batch, s32[4]{0:T(128)S(1)} %get-tuple-element.38.totals, bf16[3,256,1024]{2,1,0:T(8,128)(2,1)S(1)} %get-tuple-element.40.w_ref, ...), custom_call_target="tpu_custom_call", output_to_operand_aliasing={{0}: (4, {}), {1}: (5, {})} | custom-call | flops 1024 | bytes 1024 | tf_op jit(solution)/shard_map/pallas_call | solution.py:283
  (10 shorter events, 0.1 us)
Async XLA Ops:
  0.6 16.5 %copy-start.2 = (bf16[3072,128]{1,0:T(8,128)(2,1)S(1)}, bf16[3072,128]{1,0:T(8,128)(2,1)}, u32[]{:S(2)}) copy-start(bf16[3072,128]{1,0:T(8,128)(2,1)} %refs_0_.1) | copy-start | bytes 2359300
  0.6 15.1 %copy-start.9 = (bf16[1,128]{1,0:T(2,128)(2,1)S(1)}, bf16[1,128]{1,0:T(2,128)(2,1)}, u32[]{:S(2)}) copy-start(bf16[1,128]{1,0:T(2,128)(2,1)} %param.8) | copy-start | bytes 772
  0.7 15.1 %copy-start.10 = (bf16[1,128]{1,0:T(2,128)(2,1)S(1)}, bf16[1,128]{1,0:T(2,128)(2,1)}, u32[]{:S(2)}) copy-start(bf16[1,128]{1,0:T(2,128)(2,1)} %param.7) | copy-start | bytes 772
  0.7 17.3 %collective-permute-start = (bf16[3072,128]{1,0:T(8,128)(2,1)}, bf16[3072,128]{1,0:T(8,128)(2,1)S(1)}, u32[]{:S(2)}, u32[]{:S(2)}) collective-permute-start(bf16[3072,128]{1,0:T(8,128)(2,1)} %refs_0_.1), channel_id=1, source_target_pairs={{0,2},{1,7},{2,4},{3,1},{4,6},{5,3},{6,0},{7,5},{8,10},{9,15},{10,... | collective-permute-start | bytes 2359304 | tf_op jit(solution)/shard_map/ppermute | solution.py:205
  7.9 42.2 %copy-start = (s32[48]{0:T(128)S(1)}, s32[48]{0:T(128)}, u32[]{:S(2)}) copy-start(s32[48]{0:T(128)} %src_ref.3) | copy-start | bytes 580
  7.9 42.2 %copy-start.1 = (s32[48]{0:T(128)S(1)}, s32[48]{0:T(128)}, u32[]{:S(2)}) copy-start(s32[48]{0:T(128)} %row_ref.1) | copy-start | bytes 580
  7.9 15.8 %collective-permute-start.1 = (bf16[3072,128]{1,0:T(8,128)(2,1)}, bf16[3072,128]{1,0:T(8,128)(2,1)S(1)}, u32[]{:S(2)}, u32[]{:S(2)}) collective-permute-start(bf16[3072,128]{1,0:T(8,128)(2,1)} %refs_0_.1), channel_id=1, source_target_pairs={{0,6},{1,3},{2,0},{3,5},{4,2},{5,7},{6,4},{7,1},{8,14},{9,11},{10,... | collective-permute-start | bytes 2359304 | tf_op jit(solution)/shard_map/ppermute | solution.py:205
  7.9 25.5 %all-to-all-start = ((bf16[16,2,128,128]{3,2,1,0:T(8,128)(2,1)}), bf16[16,2,128,128]{3,2,1,0:T(8,128)(2,1)}, u32[]{:S(2)}, u32[]{:S(2)}) async-start(bf16[16,2,128,128]{3,2,1,0:T(8,128)(2,1)} %bitcast.2), calls=%async_computation | async-start | bytes 2097152 | tf_op jit(solution)/shard_map/all_to_all | solution.py:217
  15.8 2.2 %collective-permute-start.2 = (bf16[2,128]{1,0:T(2,128)(2,1)S(1)}, bf16[2,128]{1,0:T(2,128)(2,1)S(1)}, u32[]{:S(2)}, u32[]{:S(2)}) collective-permute-start(bf16[2,128]{1,0:T(2,128)(2,1)S(1)} %pad_maximum_fusion.1), channel_id=1, source_target_pairs={{0,1},{1,0},{2,3},{3,2},{4,5},{5,4},{6,7},{7,6},{8,9},{9,8},{10,11... | collective-permute-start | bytes 1544 | tf_op jit(solution)/shard_map/ppermute | solution.py:209
  17.2 12.3 %collective-permute-start.3 = (bf16[3072,128]{1,0:T(8,128)(2,1)S(1)}, bf16[3072,128]{1,0:T(8,128)(2,1)S(1)}, u32[]{:S(2)}, u32[]{:S(2)}) collective-permute-start(bf16[3072,128]{1,0:T(8,128)(2,1)S(1)} %copy-done.2), channel_id=1, source_target_pairs={{0,1},{1,0},{2,3},{3,2},{4,5},{5,4},{6,7},{7,6},{8,9},{9,8},{10,11... | collective-permute-start | bytes 2359304 | tf_op jit(solution)/shard_map/ppermute | solution.py:209
  18.0 32.1 %copy-start.5 = (bf16[3072,128]{1,0:T(8,128)(2,1)}, bf16[3072,128]{1,0:T(8,128)(2,1)S(1)}, u32[]{:S(2)}) copy-start(bf16[3072,128]{1,0:T(8,128)(2,1)S(1)} %collective-permute-done.refs_1_) | copy-start | bytes 2359300
  23.7 26.4 %copy-start.6 = (bf16[3072,128]{1,0:T(8,128)(2,1)}, bf16[3072,128]{1,0:T(8,128)(2,1)S(1)}, u32[]{:S(2)}) copy-start(bf16[3072,128]{1,0:T(8,128)(2,1)S(1)} %collective-permute-done.1.refs_2_) | copy-start | bytes 2359300
  23.7 12.4 %collective-permute-start.7 = (bf16[3072,128]{1,0:T(8,128)(2,1)S(1)}, bf16[3072,128]{1,0:T(8,128)(2,1)S(1)}, u32[]{:S(2)}, u32[]{:S(2)}) collective-permute-start(bf16[3072,128]{1,0:T(8,128)(2,1)S(1)} %collective-permute-done.refs_1_), channel_id=1, source_target_pairs={{0,2},{1,7},{2,4},{3,1},{4,6},{5,3},{6,0},{7,5},{8,10},{9,15},{10,... | collective-permute-start | bytes 2359304 | tf_op jit(solution)/shard_map/ppermute | solution.py:205
  25.3 4.1 %collective-permute-start.4 = (bf16[4,128]{1,0:T(4,128)(2,1)S(1)}, bf16[4,128]{1,0:T(4,128)(2,1)S(1)}, u32[]{:S(2)}, u32[]{:S(2)}) collective-permute-start(bf16[4,128]{1,0:T(4,128)(2,1)S(1)} %pad_maximum_fusion), channel_id=1, source_target_pairs={{0,6},{1,3},{2,0},{3,5},{4,2},{5,7},{6,4},{7,1},{8,14},{9,11},{10,... | collective-permute-start | bytes 3080 | tf_op jit(solution)/shard_map/ppermute | solution.py:205
  29.4 1.1 %collective-permute-start.6 = (bf16[4,128]{1,0:T(4,128)(2,1)S(1)}, bf16[4,128]{1,0:T(4,128)(2,1)S(1)}, u32[]{:S(2)}, u32[]{:S(2)}) collective-permute-start(bf16[4,128]{1,0:T(4,128)(2,1)S(1)} %collective-permute-done.4), channel_id=1, source_target_pairs={{0,1},{1,0},{2,3},{3,2},{4,5},{5,4},{6,7},{7,6},{8,9},{9,8},{10,11... | collective-permute-start | bytes 3080 | tf_op jit(solution)/shard_map/ppermute | solution.py:209
  29.4 4.0 %collective-permute-start.5 = (bf16[4,128]{1,0:T(4,128)(2,1)S(1)}, bf16[4,128]{1,0:T(4,128)(2,1)S(1)}, u32[]{:S(2)}, u32[]{:S(2)}) collective-permute-start(bf16[4,128]{1,0:T(4,128)(2,1)S(1)} %collective-permute-done.4), channel_id=1, source_target_pairs={{0,6},{1,3},{2,0},{3,5},{4,2},{5,7},{6,4},{7,1},{8,14},{9,11},{10,... | collective-permute-start | bytes 3080 | tf_op jit(solution)/shard_map/ppermute | solution.py:205
  29.4 0.9 %copy-start.7 = (bf16[3072,128]{1,0:T(8,128)(2,1)}, bf16[3072,128]{1,0:T(8,128)(2,1)S(1)}, u32[]{:S(2)}) copy-start(bf16[3072,128]{1,0:T(8,128)(2,1)S(1)} %collective-permute-done.3.refs_4_) | copy-start | bytes 2359300
  33.5 25.1 %collective-permute-start.12 = (bf16[4096,128]{1,0:T(8,128)(2,1)}, bf16[4096,128]{1,0:T(8,128)(2,1)}, u32[]{:S(2)}, u32[]{:S(2)}) collective-permute-start(bf16[4096,128]{1,0:T(8,128)(2,1)} %bitcast.4.refs_0_), channel_id=1, source_target_pairs={{0,6},{1,3},{2,0},{3,5},{4,2},{5,7},{6,4},{7,1},{8,14},{9,11},{10,... | collective-permute-start | bytes 3145736 | tf_op jit(solution)/shard_map/ppermute | solution.py:205
  33.5 25.1 %collective-permute-start.11 = (bf16[4096,128]{1,0:T(8,128)(2,1)}, bf16[4096,128]{1,0:T(8,128)(2,1)}, u32[]{:S(2)}, u32[]{:S(2)}) collective-permute-start(bf16[4096,128]{1,0:T(8,128)(2,1)} %bitcast.4.refs_0_), channel_id=1, source_target_pairs={{0,2},{1,7},{2,4},{3,1},{4,6},{5,3},{6,0},{7,5},{8,10},{9,15},{10,... | collective-permute-start | bytes 3145736 | tf_op jit(solution)/shard_map/ppermute | solution.py:205
  36.1 14.0 %copy-start.3 = (bf16[3072,128]{1,0:T(8,128)(2,1)}, bf16[3072,128]{1,0:T(8,128)(2,1)S(1)}, u32[]{:S(2)}) copy-start(bf16[3072,128]{1,0:T(8,128)(2,1)S(1)} %collective-permute-done.7.refs_3_) | copy-start | bytes 2359300
  37.8 24.7 %all-to-all-start.1 = ((bf16[16,2,128,128]{3,2,1,0:T(8,128)(2,1)}), bf16[16,2,128,128]{3,2,1,0:T(8,128)(2,1)}, u32[]{:S(2)}, u32[]{:S(2)}) async-start(bf16[16,2,128,128]{3,2,1,0:T(8,128)(2,1)} %bitcast.9), calls=%async_computation.1 | async-start | bytes 2097152 | tf_op jit(solution)/shard_map/all_to_all | solution.py:217
  45.4 2.4 %collective-permute-start.8 = (bf16[3072,128]{1,0:T(8,128)(2,1)S(1)}, bf16[3072,128]{1,0:T(8,128)(2,1)S(1)}, u32[]{:S(2)}, u32[]{:S(2)}) collective-permute-start(bf16[3072,128]{1,0:T(8,128)(2,1)S(1)} %collective-permute-done.refs_1_), channel_id=1, source_target_pairs={{0,1},{1,0},{2,3},{3,2},{4,5},{5,4},{6,7},{7,6},{8,9},{9,8},{10,11... | collective-permute-start | bytes 2359304 | tf_op jit(solution)/shard_map/ppermute | solution.py:209
  45.7 3.3 %collective-permute-start.9 = (bf16[3072,128]{1,0:T(8,128)(2,1)S(1)}, bf16[3072,128]{1,0:T(8,128)(2,1)}, u32[]{:S(2)}, u32[]{:S(2)}) collective-permute-start(bf16[3072,128]{1,0:T(8,128)(2,1)S(1)} %collective-permute-done.1.refs_2_), channel_id=1, source_target_pairs={{0,1},{1,0},{2,3},{3,2},{4,5},{5,4},{6,7},{7,6},{8,9},{9,8},{10,11... | collective-permute-start | bytes 2359304 | tf_op jit(solution)/shard_map/ppermute | solution.py:209
  45.9 4.2 %collective-permute-start.10 = (bf16[3072,128]{1,0:T(8,128)(2,1)S(1)}, bf16[3072,128]{1,0:T(8,128)(2,1)}, u32[]{:S(2)}, u32[]{:S(2)}) collective-permute-start(bf16[3072,128]{1,0:T(8,128)(2,1)S(1)} %collective-permute-done.7.refs_3_), channel_id=1, source_target_pairs={{0,1},{1,0},{2,3},{3,2},{4,5},{5,4},{6,7},{7,6},{8,9},{9,8},{10,11... | collective-permute-start | bytes 2359304 | tf_op jit(solution)/shard_map/ppermute | solution.py:209
  47.7 2.4 %copy-start.8 = (bf16[3072,128]{1,0:T(8,128)(2,1)}, bf16[3072,128]{1,0:T(8,128)(2,1)S(1)}, u32[]{:S(2)}) copy-start(bf16[3072,128]{1,0:T(8,128)(2,1)S(1)} %collective-permute-done.8.refs_5_) | copy-start | bytes 2359300
  47.7 16.4 %collective-permute-start.13 = (bf16[4096,128]{1,0:T(8,128)(2,1)}, bf16[4096,128]{1,0:T(8,128)(2,1)}, u32[]{:S(2)}, u32[]{:S(2)}) collective-permute-start(bf16[4096,128]{1,0:T(8,128)(2,1)} %bitcast.4.refs_0_), channel_id=1, source_target_pairs={{0,1},{1,0},{2,3},{3,2},{4,5},{5,4},{6,7},{7,6},{8,9},{9,8},{10,11... | collective-permute-start | bytes 3145736 | tf_op jit(solution)/shard_map/ppermute | solution.py:209
  58.6 5.9 %collective-permute-start.14 = (bf16[4096,128]{1,0:T(8,128)(2,1)}, bf16[4096,128]{1,0:T(8,128)(2,1)S(1)}, u32[]{:S(2)}, u32[]{:S(2)}) collective-permute-start(bf16[4096,128]{1,0:T(8,128)(2,1)} %collective-permute-done.11.refs_1_), channel_id=1, source_target_pairs={{0,1},{1,0},{2,3},{3,2},{4,5},{5,4},{6,7},{7,6},{8,9},{9,8},{10,11... | collective-permute-start | bytes 3145736 | tf_op jit(solution)/shard_map/ppermute | solution.py:209
  60.6 4.1 %collective-permute-start.15 = (bf16[4096,128]{1,0:T(8,128)(2,1)}, bf16[4096,128]{1,0:T(8,128)(2,1)}, u32[]{:S(2)}, u32[]{:S(2)}) collective-permute-start(bf16[4096,128]{1,0:T(8,128)(2,1)} %collective-permute-done.12.refs_2_), channel_id=1, source_target_pairs={{0,1},{1,0},{2,3},{3,2},{4,5},{5,4},{6,7},{7,6},{8,9},{9,8},{10,11... | collective-permute-start | bytes 3145736 | tf_op jit(solution)/shard_map/ppermute | solution.py:209
  62.6 4.1 %collective-permute-start.16 = (bf16[4096,128]{1,0:T(8,128)(2,1)}, bf16[4096,128]{1,0:T(8,128)(2,1)S(1)}, u32[]{:S(2)}, u32[]{:S(2)}) collective-permute-start(bf16[4096,128]{1,0:T(8,128)(2,1)} %bitcast.10.refs_3_), channel_id=1, source_target_pairs={{0,1},{1,0},{2,3},{3,2},{4,5},{5,4},{6,7},{7,6},{8,9},{9,8},{10,11... | collective-permute-start | bytes 3145736 | tf_op jit(solution)/shard_map/ppermute | solution.py:209
  64.5 2.1 %copy-start.4 = (bf16[4096,128]{1,0:T(8,128)(2,1)}, bf16[4096,128]{1,0:T(8,128)(2,1)S(1)}, u32[]{:S(2)}) copy-start(bf16[4096,128]{1,0:T(8,128)(2,1)S(1)} %collective-permute-done.14.refs_5_) | copy-start | bytes 3145732
